TPU v7x, 32 devices: a whole 2x2x4 slice. The times are simulated.
32 devices in a mesh: seq: 16 (over z, y, x), fsdp: 2 (over core).
Axes of the slice: x: 2, y: 2, z: 4, core: 2. Of those that a mesh axis runs over, the one named last changes fastest.
Arguments:
- tokens: bfloat16 [2, 12288, 1024], P('fsdp', 'seq'), may hold values from -6 to 6
- span_flags: int32 [2, 16], P('fsdp', 'seq'), may hold values from 0 to 1, as said below
- norm_gain: bfloat16 [1024], P(('seq', 'fsdp')), may hold values from 0.5 to 1.5
- conv_weight: bfloat16 [3, 1024], P(None, ('seq', 'fsdp')), may hold values from -3.5 to 3.5
- in_weight: bfloat16 [1024, 3072], P(('seq', 'fsdp')), may hold values from -0.1875 to 0.1875
- out_weight: bfloat16 [1024, 1024], P(('seq', 'fsdp')), may hold values from -0.1875 to 0.1875
- ffn_gain: bfloat16 [1024], P(('seq', 'fsdp')), may hold values from 0.5 to 1.5
- gate_weight: bfloat16 [1024, 4608], P(('seq', 'fsdp')), may hold values from -0.1875 to 0.1875
- up_weight: bfloat16 [1024, 4608], P(('seq', 'fsdp')), may hold values from -0.1875 to 0.1875
- down_weight: bfloat16 [4608, 1024], P(('seq', 'fsdp')), may hold values from -0.09375 to 0.09375
- cotangent: bfloat16 [2, 12288, 1024], P('fsdp', 'seq'), may hold values from -6 to 6
Outputs:
- output: bfloat16 [2, 12288, 1024], P('fsdp', 'seq')
- input_grad: float32 [2, 12288, 1024], P('fsdp', 'seq')
- norm_gain_grad: float32 [1024], P(('seq', 'fsdp'))
- conv_weight_grad: float32 [3, 1024], P(None, ('seq', 'fsdp'))
- in_weight_grad: float32 [1024, 3072], P(('seq', 'fsdp'))
- out_weight_grad: float32 [1024, 1024], P(('seq', 'fsdp'))
- ffn_gain_grad: float32 [1024], P(('seq', 'fsdp'))
- gate_weight_grad: float32 [1024, 4608], P(('seq', 'fsdp'))
- up_weight_grad: float32 [1024, 4608], P(('seq', 'fsdp'))
- down_weight_grad: float32 [4608, 1024], P(('seq', 'fsdp'))
Inputs may be any that keep to these rules, and one draw needn't show every extreme that they name: span_flags[s, c] is 1 where block c of stream s begins a new sequence; block 0 of every stream begins one and block 1 never does.
All inputs are finite; a program needn't handle non-finite values.
Results may differ from a plain program's by a relative error of at most 0.015.
Values may be sent and summed in bfloat16 or wider, within the bound.
No kernel may reach another device: no remote copies, remote signals or barrier semaphores. Data moves between devices by JAX's collectives and lax.ppermute only.
A program may use at most 256 MiB of HBM per device.

v0:
```python
import jax
import jax.numpy as jnp
from jax import lax
from jax.sharding import PartitionSpec as P

EPSILON = 1e-05


def from_behind(x, axis, by):
    peers = lax.axis_size(axis)
    pairs = [(i, i + by) for i in range(peers) if 0 <= i + by < peers]
    return lax.ppermute(x, axis, pairs)


def rms_scale(values):
    return lax.rsqrt(jnp.mean(values * values, axis=-1, keepdims=True) + EPSILON)


def inner_rows(left, right):
    return lax.dot_general(
        left, right, (((0,), (0,)), ((), ())), preferred_element_type=jnp.float32
    )


def times_transposed(left, right):
    return lax.dot_general(
        left, right, (((1,), (1,)), ((), ())), preferred_element_type=jnp.float32
    )


def local(
    tokens,
    span_flags,
    norm_gain,
    conv_weight,
    in_weight,
    out_weight,
    ffn_gain,
    gate_weight,
    up_weight,
    down_weight,
    cotangent,
):
    gathered = (
        lax.all_gather(norm_gain, ("seq", "fsdp"), axis=0, tiled=True),
        lax.all_gather(conv_weight, ("seq", "fsdp"), axis=1, tiled=True),
        lax.all_gather(in_weight, ("seq", "fsdp"), axis=0, tiled=True),
        lax.all_gather(out_weight, ("seq", "fsdp"), axis=0, tiled=True),
        lax.all_gather(ffn_gain, ("seq", "fsdp"), axis=0, tiled=True),
        lax.all_gather(gate_weight, ("seq", "fsdp"), axis=0, tiled=True),
        lax.all_gather(up_weight, ("seq", "fsdp"), axis=0, tiled=True),
        lax.all_gather(down_weight, ("seq", "fsdp"), axis=0, tiled=True),
    )
    gain_one, conv_taps, weight_in, weight_out, gain_two, weight_gate, weight_up, weight_down = (
        gathered
    )
    inputs = tokens[0].astype(jnp.float32)
    row_count, model_width = inputs.shape
    keep_state = (1 - span_flags[0, 0]).astype(jnp.float32)
    gain_first = gain_one.astype(jnp.float32)
    gain_second = gain_two.astype(jnp.float32)
    taps_float = conv_taps.astype(jnp.float32)
    scale_one = rms_scale(inputs)
    normed_one = inputs * scale_one
    hidden = (normed_one * gain_first).astype(jnp.bfloat16)
    projected = jnp.dot(hidden, weight_in, preferred_element_type=jnp.float32)
    b_part = projected[:, :model_width]
    c_part = projected[:, model_width : 2 * model_width]
    v_part = projected[:, 2 * model_width :]
    gated = (b_part * v_part).astype(jnp.bfloat16)
    incoming = from_behind(gated[-2:], "seq", 1)
    extended = jnp.concatenate(
        [incoming.astype(jnp.float32) * keep_state, gated.astype(jnp.float32)], axis=0
    )
    conv_out = (
        taps_float[0] * extended[:-2]
        + taps_float[1] * extended[1:-1]
        + taps_float[2] * extended[2:]
    )
    mixed = (c_part * conv_out).astype(jnp.bfloat16)
    resid = inputs + jnp.dot(mixed, weight_out, preferred_element_type=jnp.float32)
    scale_two = rms_scale(resid)
    normed_two = resid * scale_two
    hidden2 = (normed_two * gain_second).astype(jnp.bfloat16)
    gate_proj = jnp.dot(hidden2, weight_gate, preferred_element_type=jnp.float32)
    up_proj = jnp.dot(hidden2, weight_up, preferred_element_type=jnp.float32)
    sigmoid_gate = jax.nn.sigmoid(gate_proj)
    silu_gate = gate_proj * sigmoid_gate
    active = (silu_gate * up_proj).astype(jnp.bfloat16)
    result = resid + jnp.dot(active, weight_down, preferred_element_type=jnp.float32)
    output = result.astype(jnp.bfloat16)[None]
    grad_out = cotangent[0].astype(jnp.float32)
    d_down = grad_out.astype(jnp.bfloat16)
    grad_down = inner_rows(active, d_down)
    d_active = times_transposed(d_down, weight_down)
    d_gate = (d_active * up_proj * sigmoid_gate * (1.0 + gate_proj * (1.0 - sigmoid_gate))).astype(
        jnp.bfloat16
    )
    d_upper = (d_active * silu_gate).astype(jnp.bfloat16)
    grad_gate = inner_rows(hidden2, d_gate)
    grad_up = inner_rows(hidden2, d_upper)
    d_hidden2 = times_transposed(d_gate, weight_gate) + times_transposed(d_upper, weight_up)
    grad_gain_two = jnp.sum(d_hidden2 * normed_two, axis=0)
    d_normed_two = d_hidden2 * gain_second
    d_resid = grad_out + scale_two * (
        d_normed_two - normed_two * jnp.mean(d_normed_two * normed_two, axis=1, keepdims=True)
    )
    d_branch = d_resid.astype(jnp.bfloat16)
    grad_out_weight = inner_rows(mixed, d_branch)
    d_mixed = times_transposed(d_branch, weight_out)
    d_c_part = d_mixed * conv_out
    d_conv = d_mixed * c_part
    grad_taps = jnp.stack(
        [
            jnp.sum(d_conv * extended[:-2], axis=0),
            jnp.sum(d_conv * extended[1:-1], axis=0),
            jnp.sum(d_conv * extended[2:], axis=0),
        ]
    )
    pad_one = jnp.zeros((1, model_width), jnp.float32)
    pad_two = jnp.zeros((2, model_width), jnp.float32)
    d_extended = (
        jnp.concatenate([taps_float[0] * d_conv, pad_two], axis=0)
        + jnp.concatenate([pad_one, taps_float[1] * d_conv, pad_one], axis=0)
        + jnp.concatenate([pad_two, taps_float[2] * d_conv], axis=0)
    )
    d_state = d_extended[:2] * keep_state
    from_next = from_behind(d_state, "seq", -1)
    d_gated = d_extended[2:] + jnp.concatenate(
        [jnp.zeros((row_count - 2, model_width), jnp.float32), from_next], axis=0
    )
    d_projected = jnp.concatenate([d_gated * v_part, d_c_part, d_gated * b_part], axis=1).astype(
        jnp.bfloat16
    )
    grad_in_weight = inner_rows(hidden, d_projected)
    d_hidden = times_transposed(d_projected, weight_in)
    grad_gain_one = jnp.sum(d_hidden * normed_one, axis=0)
    d_normed_one = d_hidden * gain_first
    input_grad = d_resid + scale_one * (
        d_normed_one - normed_one * jnp.mean(d_normed_one * normed_one, axis=1, keepdims=True)
    )
    summed = (
        lax.psum_scatter(grad_gain_one, ("seq", "fsdp"), scatter_dimension=0, tiled=True),
        lax.psum_scatter(grad_taps, ("seq", "fsdp"), scatter_dimension=1, tiled=True),
        lax.psum_scatter(grad_in_weight, ("seq", "fsdp"), scatter_dimension=0, tiled=True),
        lax.psum_scatter(grad_out_weight, ("seq", "fsdp"), scatter_dimension=0, tiled=True),
        lax.psum_scatter(grad_gain_two, ("seq", "fsdp"), scatter_dimension=0, tiled=True),
        lax.psum_scatter(grad_gate, ("seq", "fsdp"), scatter_dimension=0, tiled=True),
        lax.psum_scatter(grad_up, ("seq", "fsdp"), scatter_dimension=0, tiled=True),
        lax.psum_scatter(grad_down, ("seq", "fsdp"), scatter_dimension=0, tiled=True),
    )
    (
        shard_gain_one,
        shard_taps,
        shard_in,
        shard_out,
        shard_gain_two,
        shard_gate,
        shard_up,
        shard_down,
    ) = summed
    return (
        output,
        input_grad[None],
        shard_gain_one,
        shard_taps,
        shard_in,
        shard_out,
        shard_gain_two,
        shard_gate,
        shard_up,
        shard_down,
    )


def solution(mesh):
    return jax.shard_map(
        local,
        mesh=mesh,
        in_specs=(
            P("fsdp", "seq", None),
            P("fsdp", "seq"),
            P(("seq", "fsdp")),
            P(None, ("seq", "fsdp")),
            P(("seq", "fsdp"), None),
            P(("seq", "fsdp"), None),
            P(("seq", "fsdp")),
            P(("seq", "fsdp"), None),
            P(("seq", "fsdp"), None),
            P(("seq", "fsdp"), None),
            P("fsdp", "seq", None),
        ),
        out_specs=(
            P("fsdp", "seq", None),
            P("fsdp", "seq", None),
            P(("seq", "fsdp")),
            P(None, ("seq", "fsdp")),
            P(("seq", "fsdp"), None),
            P(("seq", "fsdp"), None),
            P(("seq", "fsdp")),
            P(("seq", "fsdp"), None),
            P(("seq", "fsdp"), None),
            P(("seq", "fsdp"), None),
        ),
        check_vma=False,
    )
```

profile of v0, /device:TPU:1, one launch (start us, length us, event | category | flops | bytes accessed | tf_op | source)
XLA Modules:
  0.0 1530.2 jit_solution(6557725329033438580)
XLA Ops:
  7.2 0.7 all-gather.7.cloned.1.call-update
  8.0 0.7 all-gather.9.cloned.1.call-update
  8.7 0.7 all-gather.11.cloned.1.call-update
  9.4 0.5 all-gather.13.cloned.1.call-update
  10.0 0.5 all-gather.15.cloned.1.call-update
  10.6 0.8 dynamic-update-slice
  11.5 0.8 dynamic-update-slice.1
  12.3 41.5 %all-reduce.8 = (bf16[1024]{0:T(1024)(128)(2,1)S(1)}, bf16[1024]{0:T(1024)(128)(2,1)S(1)}) all-reduce(bf16[1024]{0:T(1024)(128)(2,1)S(1)} %dynamic-update-slice, bf16[1024]{0:T(1024)(128)(2,1)S(1)} %dynamic-update-slice.1), channel_id=1, replica_groups=mesh['seq'=16,'fsdp'=2] {'seq','fsdp'}, use_global_device_ids=true, to_apply=%add.3 | all-reduce | flops 2048 | bytes 8192
  53.8 41.4 %all-gather = bf16[32,32,3]{1,2,0:T(4,128)(2,1)S(1)} all-gather(bf16[1,32,3]{1,2,0:T(4,128)(2,1)} %bitcast.73), channel_id=1, replica_groups=mesh['seq'=16,'fsdp'=2] {'seq','fsdp'}, dimensions={0}, use_global_device_ids=true | all-gather | bytes 6336 | tf_op jit(solution)/shard_map/all_gather | solution.py:46
  95.3 1.8 fusion.14
  97.2 0.5 copy-done.24
  97.7 7.8 fusion.27
  105.6 0.9 fusion.31
  106.5 1.7 copy-done.10
  108.2 1.8 collective-permute-start
  110.7 2.8 multiply_convert_fusion.7
  113.5 27.5 %all-gather.9.cloned.1.call-done = bf16[1024,1024]{1,0:T(8,128)(2,1)} async-done(((bf16[32,1024]{1,0:T(8,128)(2,1)}), bf16[1024,1024]{1,0:T(8,128)(2,1)}) %all-gather.9.cloned.1.call-update) | async-done | bytes 2097168 | tf_op jit(solution)/shard_map/all_gather | solution.py:48
  141.0 4.4 multiply_reduce_fusion.5
  145.5 1.6 copy-done.2
  147.1 1.5 multiply_convert_fusion.6
  148.6 76.2 %all-gather.11.cloned.1.call-done = bf16[1024,4608]{1,0:T(8,128)(2,1)} async-done(((bf16[32,4608]{1,0:T(8,128)(2,1)}), bf16[1024,4608]{1,0:T(8,128)(2,1)}) %all-gather.11.cloned.1.call-update) | async-done | bytes 9437200 | tf_op jit(solution)/shard_map/all_gather | solution.py:50
  224.9 13.4 fusion.33
  238.3 70.0 %all-gather.13.cloned.1.call-done = bf16[1024,4608]{1,0:T(8,128)(2,1)} async-done(((bf16[32,4608]{1,0:T(8,128)(2,1)}), bf16[1024,4608]{1,0:T(8,128)(2,1)}) %all-gather.13.cloned.1.call-update) | async-done | bytes 9437200 | tf_op jit(solution)/shard_map/all_gather | solution.py:51
  308.3 13.4 fusion.34
  321.7 70.0 %all-gather.15.cloned.1.call-done = bf16[4608,1024]{1,0:T(8,128)(2,1)} async-done(((bf16[144,1024]{1,0:T(8,128)(2,1)}), bf16[4608,1024]{1,0:T(8,128)(2,1)}) %all-gather.15.cloned.1.call-update) | async-done | bytes 9437200 | tf_op jit(solution)/shard_map/all_gather | solution.py:52
  391.7 27.8 %multiply_convert_fusion = (bf16[768,4608]{1,0:T(8,128)(2,1)}, bf16[768,4608]{1,0:T(8,128)(2,1)}, bf16[768,4608]{1,0:T(8,128)(2,1)}) fusion(f32[768,4608]{1,0:T(8,128)} %fusion.33, f32[768,4608]{1,0:T(8,128)} %fusion.34, bf16[4608,1024]{1,0:T(8,128)(2,1)} %all-gather.15.cloned.1.call-done, bf16[1,768,1024]{2,1,0:T(8,128)(2,1)} %param.21), kind=kOutput, calls=%fused_computation | convolution fusion | flops 7300841472 | bytes 60555264 | tf_op jit(solution)/shard_map/dot_general | solution.py:26
  419.6 13.5 fusion.35
  433.0 11.3 multiply_reduce_fusion
  444.3 0.8 multiply_add_fusion
  445.1 0.8 copy-done.26
  445.9 1.8 fusion.24
  447.8 1.2 copy-done.7
  449.0 0.5 copy-done.11
  449.4 4.7 multiply_reduce_fusion.3
  454.1 1.0 copy.24
  455.2 0.4 reduce-scatter.11.cloned.1.call-start
  455.6 6.2 fusion.22
  461.9 1.8 copy-done.8
  463.7 1.2 broadcast_multiply_fusion.1
  465.0 1.6 collective-permute-start.1
  466.5 1.5 fusion.5
  468.1 1.7 collective-permute-done.1
  469.8 1.4 multiply_convert_fusion.5
  471.2 1.1 copy-done.18
  472.3 0.5 copy-done.20
  472.8 8.6 fusion.15
  481.5 1.3 copy-done.1
  482.9 14.5 fusion.36
  497.6 14.5 fusion.37
  512.1 1.3 copy-done.17
  513.5 14.5 fusion.17
  528.0 1.9 copy-done.4
  529.8 13.1 fusion.21
  543.0 9.9 fusion.13
  552.9 40.9 %all-reduce.7 = (f32[1024]{0:T(1024)S(1)}, f32[1024]{0:T(1024)S(1)}) all-reduce(f32[1024]{0:T(1024)S(1)} %get-tuple-element.14, f32[1024]{0:T(1024)S(1)} %get-tuple-element.12), channel_id=2, replica_groups=mesh['seq'=16,'fsdp'=2] {'seq','fsdp'}, use_global_device_ids=true, to_apply=%region_5.0.clone | all-reduce | flops 2048 | bytes 16384
  593.8 0.6 dynamic-slice
  594.4 0.6 dynamic-slice.1
  595.0 4.8 fusion.12
  599.8 1.4 copy.25
  601.2 120.9 %reduce-scatter.11.cloned.1.call-done = f32[32,1024]{1,0:T(8,128)} async-done(((f32[1024,1024]{1,0:T(8,128)}), f32[32,1024]{1,0:T(8,128)}) %reduce-scatter.11.cloned.1.call-update) | async-done | bytes 131088 | tf_op jit(solution)/shard_map/reduce_scatter | solution.py:146
  722.1 163.4 %reduce-scatter.9.cloned.1.call-done = f32[32,3072]{1,0:T(8,128)} async-done(((f32[1024,3072]{1,0:T(8,128)}), f32[32,3072]{1,0:T(8,128)}) %reduce-scatter.9.cloned.1.call-update) | async-done | bytes 393232 | tf_op jit(solution)/shard_map/reduce_scatter | solution.py:145
  885.4 212.9 %reduce-scatter.13.cloned.1.call-done = f32[32,4608]{1,0:T(8,128)} async-done(((f32[1024,4608]{1,0:T(8,128)}), f32[32,4608]{1,0:T(8,128)}) %reduce-scatter.13.cloned.1.call-update) | async-done | bytes 589840 | tf_op jit(solution)/shard_map/reduce_scatter | solution.py:148
  1098.3 212.5 %reduce-scatter.15.cloned.1.call-done = f32[32,4608]{1,0:T(8,128)} async-done(((f32[1024,4608]{1,0:T(8,128)}), f32[32,4608]{1,0:T(8,128)}) %reduce-scatter.15.cloned.1.call-update) | async-done | bytes 589840 | tf_op jit(solution)/shard_map/reduce_scatter | solution.py:149
  1310.8 212.6 %reduce-scatter.17.cloned.1.call-done = f32[144,1024]{1,0:T(8,128)} async-done(((f32[4608,1024]{1,0:T(8,128)}), f32[144,1024]{1,0:T(8,128)}) %reduce-scatter.17.cloned.1.call-update) | async-done | bytes 589840 | tf_op jit(solution)/shard_map/reduce_scatter | solution.py:150
  (84 shorter events, 1.0 us)
Async XLA Ops:
  7.2 90.0 %all-gather.7.cloned.1.call-start = ((), (), s32[]{:S(2)}) async-start(), calls=%async_computation.6 | async-start | bytes 6488064 | tf_op jit(solution)/shard_map/all_gather | solution.py:47
  7.9 133.1 %all-gather.9.cloned.1.call-start = ((), (), s32[]{:S(2)}) async-start(), calls=%async_computation.7 | async-start | bytes 2162688 | tf_op jit(solution)/shard_map/all_gather | solution.py:48
  8.7 216.2 %all-gather.11.cloned.1.call-start = ((), (), s32[]{:S(2)}) async-start(), calls=%async_computation.8 | async-start | bytes 9732096 | tf_op jit(solution)/shard_map/all_gather | solution.py:50
  9.4 298.9 %all-gather.13.cloned.1.call-start = ((), (), s32[]{:S(2)}) async-start(), calls=%async_computation.9 | async-start | bytes 9732096 | tf_op jit(solution)/shard_map/all_gather | solution.py:51
  10.0 381.7 %all-gather.15.cloned.1.call-start = ((), (), s32[]{:S(2)}) async-start(), calls=%async_computation.10 | async-start | bytes 9732096 | tf_op jit(solution)/shard_map/all_gather | solution.py:52
  10.6 589.3 %reduce-scatter.19.cloned.1.call-start = ((), (), s32[]{:S(2)}) async-start(), calls=%async_computation.16 | async-start | bytes 540672
  53.8 43.4 %copy-start.22 = (f32[1024]{0:T(1024)}, f32[1024]{0:T(1024)S(1)}, u32[]{:S(2)}) copy-start(f32[1024]{0:T(1024)S(1)} %convert_element_type.61) | copy-start | bytes 12292
  97.1 0.6 copy-start.24
  105.6 5.1 copy-start
  106.5 1.7 copy-start.10
  108.2 2.4 collective-permute-start
  145.4 1.7 copy-start.2
  419.6 13.5 copy-start.3
  419.6 13.5 copy-start.9
  433.0 11.3 copy-start.16
  444.3 1.6 copy-start.26
  445.9 1.8 copy-start.5
  445.9 3.0 copy-start.7
  445.9 3.5 copy-start.11
  455.2 266.9 %reduce-scatter.11.cloned.1.call-start = ((), (), s32[]{:S(2)}) async-start(), calls=%async_computation.12 | async-start | bytes 4325376 | tf_op jit(solution)/shard_map/reduce_scatter | solution.py:146
  461.8 1.9 copy-start.8
  461.8 423.6 %reduce-scatter.9.cloned.1.call-start = ((), (), s32[]{:S(2)}) async-start(), calls=%async_computation.11 | async-start | bytes 12976128 | tf_op jit(solution)/shard_map/reduce_scatter | solution.py:145
  464.9 4.9 slice-start
  464.9 4.9 slice-start.1
  465.0 4.8 slice-start.2
  465.0 4.8 collective-permute-start.1
  468.1 4.8 copy-start.12
  468.1 4.8 copy-start.14
  468.1 4.8 copy-start.23
  468.1 4.7 copy-start.25
  471.2 1.2 copy-start.18
  471.2 1.7 copy-start.20
  481.5 1.4 copy-start.1
  481.5 616.9 %reduce-scatter.13.cloned.1.call-start = ((), (), s32[]{:S(2)}) async-start(), calls=%async_computation.13 | async-start | bytes 19464192 | tf_op jit(solution)/shard_map/reduce_scatter | solution.py:148
  497.3 813.5 %reduce-scatter.15.cloned.1.call-start = ((), (), s32[]{:S(2)}) async-start(), calls=%async_computation.14 | async-start | bytes 19464192 | tf_op jit(solution)/shard_map/reduce_scatter | solution.py:149
  512.1 1.4 copy-start.17
  512.1 1011.3 %reduce-scatter.17.cloned.1.call-start = ((), (), s32[]{:S(2)}) async-start(), calls=%async_computation.15 | async-start | bytes 19464192 | tf_op jit(solution)/shard_map/reduce_scatter | solution.py:150
  527.9 1.9 copy-start.4
  529.8 13.1 copy-start.13
  529.8 13.1 copy-start.15
  529.8 13.1 copy-start.19
  529.8 13.2 copy-start.21
  543.0 52.0 %copy-start.6 = (f32[768,1024]{1,0:T(8,128)S(1)}, f32[768,1024]{1,0:T(8,128)}, u32[]{:S(2)}) copy-start(f32[768,1024]{1,0:T(8,128)} %copy-done.5) | copy-start | bytes 9437188
Sparse Core Ops, SparseCore 0:
  10.9 72.3 all-gather.6
  86.1 54.8 all-gather.8
  143.9 80.8 all-gather.10
  227.6 80.6 all-gather.12
  311.0 80.6 all-gather.14
  455.3 126.9 reduce-scatter.18
  585.3 136.7 reduce-scatter.10
  729.7 155.6 reduce-scatter.8
  892.4 205.8 reduce-scatter.12
  1105.2 205.6 reduce-scatter.14
  1317.8 205.5 reduce-scatter.16
where the time goes:
time: 1540 us; the launch traced here: 1530 us
  waiting for transfers between devices  1170 us (76%)
  matrix products  175 us (11%)
  blocking collectives  124 us (8%)
  other arithmetic  21.5 us (1%)
  local copies, waits for them, and re-layouts  19.8 us (1%)
    reduce_scatter x1, waiting for transfers between devices, local(): lax.psum_scatter(grad_gate, ('seq', 'fsdp'), scatter_dimension=0, tiled=T...  213 us
    reduce_scatter x1, waiting for transfers between devices, local(): lax.psum_scatter(grad_down, ('seq', 'fsdp'), scatter_dimension=0, tiled=T...  213 us
    reduce_scatter x1, waiting for transfers between devices, local(): lax.psum_scatter(grad_up, ('seq', 'fsdp'), scatter_dimension=0, tiled=True)  213 us
    reduce_scatter x1, waiting for transfers between devices, local(): lax.psum_scatter(grad_in_weight, ('seq', 'fsdp'), scatter_dimension=0, ti...  163 us
    reduce_scatter x1, waiting for transfers between devices, local(): lax.psum_scatter(grad_out_weight, ('seq', 'fsdp'), scatter_dimension=0, t...  121 us
    unnamed x2, blocking collectives  82.4 us
    all_gather x1, waiting for transfers between devices, local(): lax.all_gather(gate_weight, ('seq', 'fsdp'), axis=0, tiled=True)  76.2 us
    all_gather x1, waiting for transfers between devices, local(): lax.all_gather(down_weight, ('seq', 'fsdp'), axis=0, tiled=True)  70 us
  transfers between devices with their start and end apart: 13, of which 10 were waited for; matrix products, arithmetic and copies ran while one was open for 9% of the time, Pallas kernels for 0%

commit v1 on v0

v1 whole, which is shorter than its diff:
```python
import jax
import jax.numpy as jnp
from jax import lax
from jax.sharding import PartitionSpec as P

EPSILON = 1e-05
LANES = 128
BF16 = jnp.bfloat16
F32 = jnp.float32


def swap_cores(x):
    return lax.ppermute(x, "fsdp", [(0, 1), (1, 0)])


def across(x, bit):
    peers = lax.axis_size("seq")
    return lax.ppermute(x, "seq", [(i, i ^ bit) for i in range(peers)])


def shift(x, by):
    peers = lax.axis_size("seq")
    pairs = [(i, i + by) for i in range(peers) if 0 <= i + by < peers]
    return lax.ppermute(x, "seq", pairs)


def columns_of_line(peers):
    return [[4 * z + p for z in range(peers // 4)] for p in range(4)]


def gather_chips(shard):
    peers = lax.axis_size("seq")
    rows, cols = shard.shape
    if peers != 16:
        whole = lax.all_gather(shard, "seq", axis=0, tiled=True)
        return whole.reshape(peers, rows, cols)
    depth = peers // 4
    half = depth // 2
    plane = lax.axis_index("seq") % 4
    line = lax.all_gather(
        shard, "seq", axis_index_groups=columns_of_line(peers), axis=0, tiled=True
    ).reshape(depth, 1, rows, cols)
    from_x = across(line, 1)
    from_y = across(line, 2)
    corner_low = across(from_x[:half], 2)
    corner_high = across(from_y[half:], 1)
    whole = jnp.zeros((depth, 4, rows, cols), shard.dtype)
    whole = lax.dynamic_update_slice(whole, line, (0, plane, 0, 0))
    whole = lax.dynamic_update_slice(whole, from_x, (0, plane ^ 1, 0, 0))
    whole = lax.dynamic_update_slice(whole, from_y, (0, plane ^ 2, 0, 0))
    whole = lax.dynamic_update_slice(whole, corner_low, (0, plane ^ 3, 0, 0))
    whole = lax.dynamic_update_slice(whole, corner_high, (half, plane ^ 3, 0, 0))
    return whole.reshape(peers, rows, cols)


def scatter_chips(terms):
    peers, rows, cols = terms.shape
    if peers != 16:
        flat = terms.reshape(peers * rows, cols)
        return lax.psum_scatter(flat, "seq", scatter_dimension=0, tiled=True)
    depth = peers // 4
    half = depth // 2
    plane = lax.axis_index("seq") % 4
    terms = terms.reshape(depth, 4, rows, cols)

    def piece(bits, start, count):
        return lax.dynamic_slice(
            terms, (start, plane ^ bits, 0, 0), (count, 1, rows, cols)
        )

    add_y = across(piece(3, 0, half), 1)
    add_x = across(piece(3, half, half), 2)
    for_x = jnp.concatenate([piece(1, 0, half), piece(1, half, half) + add_x], axis=0)
    for_y = jnp.concatenate([piece(2, 0, half) + add_y, piece(2, half, half)], axis=0)
    mine = (
        piece(0, 0, depth).astype(F32)
        + across(for_x, 1).astype(F32)
        + across(for_y, 2).astype(F32)
    ).astype(BF16)
    return lax.psum_scatter(
        mine.reshape(depth * rows, cols),
        "seq",
        axis_index_groups=columns_of_line(peers),
        scatter_dimension=0,
        tiled=True,
    )


def rms_scale(values):
    return lax.rsqrt(jnp.mean(values * values, axis=-1, keepdims=True) + EPSILON)


def inner_rows(left, right):
    return lax.dot_general(
        left, right, (((0,), (0,)), ((), ())), preferred_element_type=F32
    )


def times(left, right):
    return jnp.dot(left, right, preferred_element_type=F32)


def times_transposed(left, right):
    return lax.dot_general(
        left, right, (((1,), (1,)), ((), ())), preferred_element_type=F32
    )


def local(
    tokens,
    span_flags,
    norm_gain,
    conv_weight,
    in_weight,
    out_weight,
    ffn_gain,
    gate_weight,
    up_weight,
    down_weight,
    cotangent,
):
    chips = lax.axis_size("seq")
    core = lax.axis_index("fsdp")
    first = core == 0
    rows, width = tokens.shape[1:]
    half = width // 2
    part = in_weight.shape[0]
    pair = 2 * part
    ff_block = down_weight.shape[0]
    ff_half = chips * ff_block

    def ordered(mine, other):
        return jnp.where(first, mine, other), jnp.where(first, other, mine)

    def trade(low, high):
        keep, give = jnp.where(first, low, high), jnp.where(first, high, low)
        return ordered(keep, swap_cores(give))

    tokens_other = swap_cores(tokens[0])
    flag_other = swap_cores(jnp.broadcast_to(span_flags.astype(F32), (8, LANES)))

    in_split = in_weight.reshape(part, 3, 2, half)
    tiny = jnp.concatenate(
        [norm_gain[:, None], ffn_gain[:, None], conv_weight.T], axis=1
    )
    tiny = jnp.pad(tiny, ((0, 0), (0, LANES - tiny.shape[1])))
    in_low = jnp.concatenate([in_split[:, :, 0].reshape(part, 3 * half), tiny], axis=1)
    in_high = jnp.concatenate([in_split[:, :, 1].reshape(part, 3 * half), tiny], axis=1)
    in_pair = jnp.concatenate(trade(in_low, in_high), axis=0)
    out_fold = jnp.concatenate([out_weight[:, :half], out_weight[:, half:]], axis=0)
    front = gather_chips(jnp.concatenate([in_pair, out_fold], axis=1))

    wide = jnp.concatenate([gate_weight, up_weight], axis=1)
    wide = wide.reshape(part, 2 * chips, 2, ff_block)
    wide_low = wide[:, :, 0].reshape(part, 2 * ff_half)
    wide_high = wide[:, :, 1].reshape(part, 2 * ff_half)
    wide_pair = jnp.concatenate(trade(wide_low, wide_high), axis=0)
    weight_gate = gather_chips(wide_pair[:, :ff_half]).reshape(width, ff_half)
    weight_up = gather_chips(wide_pair[:, ff_half:]).reshape(width, ff_half)
    weight_down = gather_chips(down_weight).reshape(ff_half, width)
    cotangent_other = swap_cores(cotangent[0])

    weight_in = front[:, :, : 3 * half].reshape(width, 3 * half)
    small = front[:, :, 3 * half : 3 * half + LANES].reshape(width, LANES)
    small = small[:, :8].astype(F32).T
    gain_first, gain_second = small[0], small[1]
    taps = lax.dynamic_slice(small[2:5], (0, core * half), (3, half))
    out_mine = front[:, :, 3 * half + LANES :]
    out_even, out_odd = ordered(out_mine, swap_cores(out_mine))
    weight_out = jnp.stack(
        [
            jnp.concatenate([out_even[:, :part], out_even[:, part:]], axis=2),
            jnp.concatenate([out_odd[:, :part], out_odd[:, part:]], axis=2),
        ],
        axis=1,
    ).reshape(width, width)

    own_inputs = tokens[0].astype(F32)
    inputs = jnp.concatenate([tokens[0], tokens_other], axis=0).astype(F32)
    keep_state = 1.0 - jnp.stack([span_flags[0, 0].astype(F32), flag_other[0, 0]])
    keep_state = keep_state[:, None, None]
    hidden = (inputs * rms_scale(inputs) * gain_first).astype(BF16)
    projected = times(hidden, weight_in)
    b_part = projected[:, :half]
    c_part = projected[:, half : 2 * half]
    v_part = projected[:, 2 * half :]
    gated = (b_part * v_part).astype(BF16).reshape(2, rows, half)
    incoming = shift(gated[:, -2:], 1)
    extended = jnp.concatenate(
        [incoming.astype(F32) * keep_state, gated.astype(F32)], axis=1
    )
    conv_out = (
        taps[0] * extended[:, :-2] + taps[1] * extended[:, 1:-1] + taps[2] * extended[:, 2:]
    ).reshape(2 * rows, half)
    mixed_half = (c_part * conv_out).astype(BF16)
    mixed = jnp.concatenate(
        ordered(mixed_half[:rows], swap_cores(mixed_half[rows:])), axis=1
    )

    resid = own_inputs + times(mixed, weight_out)
    scale_two = rms_scale(resid)
    normed_two = resid * scale_two
    hidden2_own = (normed_two * gain_second).astype(BF16)
    hidden2 = jnp.concatenate([hidden2_own, swap_cores(hidden2_own)], axis=0)

    gate_proj = times(hidden2, weight_gate)
    up_proj = times(hidden2, weight_up)
    sigmoid_gate = jax.nn.sigmoid(gate_proj)
    silu_gate = gate_proj * sigmoid_gate
    active = (silu_gate * up_proj).astype(BF16)
    result = times(active, weight_down)
    result = resid + result[:rows] + swap_cores(result[rows:].astype(BF16)).astype(F32)
    output = result.astype(BF16)[None]

    d_down = jnp.concatenate([cotangent[0], cotangent_other], axis=0)
    grad_down = inner_rows(active, d_down).astype(BF16)
    shard_down = scatter_chips(grad_down.reshape(chips, ff_block, width))
    d_active = times_transposed(d_down, weight_down)
    d_gate = (
        d_active * up_proj * sigmoid_gate * (1.0 + gate_proj * (1.0 - sigmoid_gate))
    ).astype(BF16)
    d_upper = (d_active * silu_gate).astype(BF16)
    d_hidden2 = times_transposed(d_gate, weight_gate) + times_transposed(d_upper, weight_up)
    d_hidden2 = d_hidden2[:rows] + swap_cores(d_hidden2[rows:])
    grad_gate = inner_rows(hidden2, d_gate).astype(BF16)
    shard_gate = scatter_chips(grad_gate.reshape(chips, pair, ff_half))
    grad_up = inner_rows(hidden2, d_upper).astype(BF16)
    shard_up = scatter_chips(grad_up.reshape(chips, pair, ff_half))

    grad_gain_two = jnp.sum(d_hidden2 * normed_two, axis=0)
    d_normed_two = d_hidden2 * gain_second
    d_resid = cotangent[0].astype(F32) + scale_two * (
        d_normed_two - normed_two * jnp.mean(d_normed_two * normed_two, axis=1, keepdims=True)
    )
    d_branch = d_resid.astype(BF16)
    d_mixed_own = times_transposed(d_branch, weight_out)
    d_mixed_keep = jnp.where(first, d_mixed_own[:, :half], d_mixed_own[:, half:])
    d_mixed_give = jnp.where(first, d_mixed_own[:, half:], d_mixed_own[:, :half])
    d_mixed = jnp.concatenate([d_mixed_keep, swap_cores(d_mixed_give)], axis=0)
    grad_out = inner_rows(mixed, d_branch).reshape(chips, 2, part, width)
    out_keep = jnp.where(first, grad_out[:, 0], grad_out[:, 1])
    out_give = jnp.where(first, grad_out[:, 1], grad_out[:, 0]).astype(BF16)
    grad_out = (out_keep + swap_cores(out_give).astype(F32)).astype(BF16)
    grad_out = jnp.concatenate([grad_out[:, :, :half], grad_out[:, :, half:]], axis=1)

    d_c_part = d_mixed * conv_out
    d_conv = (d_mixed * c_part).reshape(2, rows, half)
    grad_taps = jnp.stack(
        [
            jnp.sum(d_conv * extended[:, :-2], axis=(0, 1)),
            jnp.sum(d_conv * extended[:, 1:-1], axis=(0, 1)),
            jnp.sum(d_conv * extended[:, 2:], axis=(0, 1)),
        ]
    )
    d_state = (
        jnp.concatenate(
            [
                taps[0] * d_conv[:, :1],
                taps[0] * d_conv[:, 1:2] + taps[1] * d_conv[:, :1],
            ],
            axis=1,
        )
        * keep_state
    )
    from_next = shift(d_state, -1)
    following = jnp.pad(d_conv, ((0, 0), (0, 2), (0, 0)))
    d_gated = (
        taps[2] * following[:, :-2] + taps[1] * following[:, 1:-1] + taps[0] * following[:, 2:]
    ) + jnp.pad(from_next, ((0, 0), (rows - 2, 0), (0, 0)))
    d_gated = d_gated.reshape(2 * rows, half)
    d_projected = jnp.concatenate(
        [d_gated * v_part, d_c_part, d_gated * b_part], axis=1
    ).astype(BF16)
    d_hidden = times_transposed(d_projected, weight_in)
    d_hidden = d_hidden[:rows] + swap_cores(d_hidden[rows:])
    grad_in = inner_rows(hidden, d_projected).astype(BF16)

    scale_one = rms_scale(own_inputs)
    normed_one = own_inputs * scale_one
    grad_gain_one = jnp.sum(d_hidden * normed_one, axis=0)
    d_normed_one = d_hidden * gain_first
    input_grad = d_resid + scale_one * (
        d_normed_one - normed_one * jnp.mean(d_normed_one * normed_one, axis=1, keepdims=True)
    )

    zero_half = jnp.zeros_like(grad_taps)
    taps_wide = jnp.concatenate(
        [jnp.where(first, grad_taps, zero_half), jnp.where(first, zero_half, grad_taps)], axis=1
    )
    small_grads = jnp.concatenate([grad_gain_one[None], grad_gain_two[None], taps_wide], axis=0)
    small_grads = jnp.pad(small_grads.T, ((0, 0), (0, LANES - small_grads.shape[0])))
    shard_front = scatter_chips(
        jnp.concatenate(
            [
                grad_in.reshape(chips, pair, 3 * half),
                small_grads.astype(BF16).reshape(chips, pair, LANES),
                grad_out,
            ],
            axis=2,
        )
    )

    def rejoin(shard):
        keep = jnp.where(first, shard[:part], shard[part:])
        give = jnp.where(first, shard[part:], shard[:part])
        return keep, swap_cores(give)

    keep, got = rejoin(shard_front[:, : 3 * half + LANES])
    low, high = ordered(keep[:, : 3 * half], got[:, : 3 * half])
    shard_in = (
        jnp.stack([low.reshape(part, 3, half), high.reshape(part, 3, half)], axis=2)
        .reshape(part, 3 * width)
        .astype(F32)
    )
    tail = keep[:, 3 * half :].astype(F32) + got[:, 3 * half :].astype(F32)
    tail = tail[:, :8].T
    out_pieces = shard_front[:, 3 * half + LANES :]
    shard_out = jnp.concatenate([out_pieces[:part], out_pieces[part:]], axis=1).astype(F32)

    def interleave(shard):
        low, high = ordered(*rejoin(shard))
        return (
            jnp.stack(
                [low.reshape(part, chips, ff_block), high.reshape(part, chips, ff_block)], axis=2
            )
            .reshape(part, 2 * ff_half)
            .astype(F32)
        )

    return (
        output,
        input_grad[None],
        tail[0],
        tail[2:5],
        shard_in,
        shard_out,
        tail[1],
        interleave(shard_gate),
        interleave(shard_up),
        shard_down.astype(F32),
    )


def solution(mesh):
    return jax.shard_map(
        local,
        mesh=mesh,
        in_specs=(
            P("fsdp", "seq", None),
            P("fsdp", "seq"),
            P(("seq", "fsdp")),
            P(None, ("seq", "fsdp")),
            P(("seq", "fsdp"), None),
            P(("seq", "fsdp"), None),
            P(("seq", "fsdp")),
            P(("seq", "fsdp"), None),
            P(("seq", "fsdp"), None),
            P(("seq", "fsdp"), None),
            P("fsdp", "seq", None),
        ),
        out_specs=(
            P("fsdp", "seq", None),
            P("fsdp", "seq", None),
            P(("seq", "fsdp")),
            P(None, ("seq", "fsdp")),
            P(("seq", "fsdp"), None),
            P(("seq", "fsdp"), None),
            P(("seq", "fsdp")),
            P(("seq", "fsdp"), None),
            P(("seq", "fsdp"), None),
            P(("seq", "fsdp"), None),
        ),
        check_vma=False,
    )
```

time: 1540 us -> 590 us (0.38)
  waiting for transfers between devices: 1170 us -> 198 us
  blocking collectives: 124 us -> 0 us
  local copies, waits for them, and re-layouts: 19.8 us -> 88.3 us
  other arithmetic: 21.5 us -> 79 us
  starting transfers between devices: 4.32 us -> 54.8 us
  matrix products: 175 us -> 147 us
    reduce_scatter x5 -> x4, waiting for transfers between devices: 922 us -> 26.5 us  [scatter_chips(): lax.psum_scatter(mine.reshape(depth * rows, cols), 'seq', axis_index_grou...]
    all_gather x5 -> x4, waiting for transfers between devices: 244 us -> 92.6 us  [gather_chips(): lax.all_gather(shard, 'seq', axis_index_groups=columns_of_line(peers), ax...]
    unnamed x2 -> x0, blocking collectives: 82.4 us -> none
    ppermute x2 -> x50, waiting for transfers between devices: 1.68 us -> 78.5 us  [the longest x32 74.4 us: across(): return lax.ppermute(x, 'seq', [(i, i ^ bit) for i in range(peers)])]
    ppermute x2 -> x50, starting transfers between devices: 3.31 us -> 53.7 us  [the longest x32 29.8 us: across(): return lax.ppermute(x, 'seq', [(i, i ^ bit) for i in range(peers)])]
    all_gather x1 -> x0, blocking collectives: 41.4 us -> none  [local(): lax.all_gather(conv_weight, ('seq', 'fsdp'), axis=1, tiled=True)]
    dynamic_update_slice x0 -> x20, local copies, waits for them, and re-layouts: none -> 26.9 us  [the longest x4 7.68 us: gather_chips(): whole = lax.dynamic_update_slice(whole, from_x, (0, plane ^ 1, 0, 0))]
    slice x2 -> x30, local copies, waits for them, and re-layouts: 0.02 us -> 26.3 us  [the longest x4 4.15 us: gather_chips(): corner_low = across(from_x[:half], 2)]
  transfers between devices with their start and end apart: 13 -> 58, of which waited for: 10 -> 18; matrix products, arithmetic and copies ran while one was open for 9% -> 41% of each run, Pallas kernels for 0% -> 0%
where the time goes in v1:
time: 590 us; the launch traced here: 584 us
  waiting for transfers between devices  198 us (34%)
  matrix products  147 us (25%)
  local copies, waits for them, and re-layouts  88.3 us (15%)
  other arithmetic  79 us (13%)
  starting transfers between devices  54.8 us (9%)
  between operations  17 us (3%)
    all_gather x4, waiting for transfers between devices, gather_chips(): lax.all_gather(shard, 'seq', axis_index_groups=columns_of_line(peers), ax...  92.6 us
    ppermute x32, waiting for transfers between devices, across(): return lax.ppermute(x, 'seq', [(i, i ^ bit) for i in range(peers)])  74.4 us
    dot_general x5, matrix products, times(): return jnp.dot(left, right, preferred_element_type=F32)  60 us
    dot_general x5, matrix products, times_transposed(): lax.dot_general(left, right, (((1,), (1,)), ((), ())), preferred_element_...  45.6 us
    dot_general x5, matrix products, inner_rows(): lax.dot_general(left, right, (((0,), (0,)), ((), ())), preferred_element_...  41.1 us
    ppermute x32, starting transfers between devices, across(): return lax.ppermute(x, 'seq', [(i, i ^ bit) for i in range(peers)])  29.8 us
    reduce_scatter x4, waiting for transfers between devices, scatter_chips(): lax.psum_scatter(mine.reshape(depth * rows, cols), 'seq', axis_index_grou...  26.5 us
    ppermute x16, starting transfers between devices, swap_cores(): return lax.ppermute(x, 'fsdp', [(0, 1), (1, 0)])  19.6 us
  transfers between devices with their start and end apart: 58, of which 18 were waited for; matrix products, arithmetic and copies ran while one was open for 41% of the time, Pallas kernels for 0%

profile of v1, /device:TPU:1, one launch (start us, length us, event | category | flops | bytes accessed | tf_op | source)
XLA Modules:
  0.0 584.2 jit_solution(654545241368167642)
XLA Ops:
  10.9 2.3 fusion.51
  25.7 15.9 %all-gather.11.cloned.1.call-done = bf16[576,1024]{1,0:T(8,128)(2,1)} async-done(((bf16[144,1024]{1,0:T(8,128)(2,1)}), bf16[576,1024]{1,0:T(8,128)(2,1)}) %all-gather.11.cloned.1.call-update) | async-done | bytes 1179664 | tf_op jit(solution)/shard_map/all_gather | solution.py:40
  44.0 2.8 broadcast_in_dim.47
  47.8 24.4 %all-gather.5.cloned.1.call-done = bf16[256,2176]{1,0:T(8,128)(2,1)} async-done(((bf16[64,2176]{1,0:T(8,128)(2,1)}), bf16[256,2176]{1,0:T(8,128)(2,1)}) %all-gather.5.cloned.1.call-update) | async-done | bytes 1114128 | tf_op jit(solution)/shard_map/all_gather | solution.py:40
  74.6 2.6 broadcast_in_dim.42
  78.4 25.6 %all-gather.7.cloned.1.call-done = bf16[256,2304]{1,0:T(8,128)(2,1)} async-done(((bf16[64,2304]{1,0:T(8,128)(2,1)}), bf16[256,2304]{1,0:T(8,128)(2,1)}) %all-gather.7.cloned.1.call-update) | async-done | bytes 1179664 | tf_op jit(solution)/shard_map/all_gather | solution.py:40
  105.2 2.6 broadcast.86.clone.1
  108.8 26.7 %all-gather.9.cloned.1.call-done = bf16[256,2304]{1,0:T(8,128)(2,1)} async-done(((bf16[64,2304]{1,0:T(8,128)(2,1)}), bf16[256,2304]{1,0:T(8,128)(2,1)}) %all-gather.9.cloned.1.call-update) | async-done | bytes 1179664 | tf_op jit(solution)/shard_map/all_gather | solution.py:40
  138.7 2.7 constant_dynamic-update-slice_fusion.18
  144.8 2.3 constant_dynamic-update-slice_fusion.17
  152.4 2.4 constant_dynamic-update-slice_fusion.3
  154.8 2.4 constant_dynamic-update-slice_fusion.2
  158.7 5.2 collective-permute-done.13
  166.1 34.8 %collective-permute-done.4 = bf16[2,1,64,2176]{3,2,1,0:T(8,128)(2,1)S(1)} collective-permute-done((bf16[2,1,64,2176]{3,2,1,0:T(8,128)(2,1)S(1)}, bf16[2,1,64,2176]{3,2,1,0:T(8,128)(2,1)S(1)}, u32[]{:S(2)}, u32[]{:S(2)}) %collective-permute-start.4) | collective-permute-done | bytes 557088 | tf_op jit(solution)/shard_map/ppermute | solution.py:18
  203.9 3.8 slice.318
  208.8 7.5 %fusion.46 = f32[1536,1536]{1,0:T(8,128)S(1)} fusion(bf16[1024,1536]{1,0:T(8,128)(2,1)} %bitcast.173, f32[1024]{0:T(1024)S(1)} %bitcast.201, f32[1536]{0:T(1024)S(1)} %add_rsqrt_fusion, bf16[768,1024]{1,0:T(8,128)(2,1)} %copy-done.33, bf16[768,1024]{1,0:T(8,128)(2,1)S(1)} %bitcast.143), kind=kOutput, calls=%fused_computation.209 | convolution fusion | flops 4842848256 | bytes 15738880 | tf_op jit(solution)/shard_map/dot_general | solution.py:100
  217.0 2.7 collective-permute-start.6
  220.2 2.0 slice.328
  222.3 4.6 collective-permute-start.9
  236.4 1.9 collective-permute-start.14
  238.4 1.9 constant_dynamic-update-slice_fusion.1
  246.8 1.9 multiply_reduce_fusion.5
  252.3 13.8 %fusion.24 = f32[1536,2304]{1,0:T(8,128)} fusion(bf16[2304,1024]{1,0:T(8,128)(2,1)} %bitcast.36, bf16[768,1024]{1,0:T(8,128)(2,1)S(1)} %collective-permute-done.25, bf16[768,1024]{1,0:T(8,128)(2,1)S(1)} %bitcast.179), kind=kOutput, calls=%fused_computation.74 | convolution fusion | flops 7254048768 | bytes 22020096 | tf_op jit(solution)/shard_map/dot_general | solution.py:104
  267.9 11.5 %fusion.43 = f32[1536,2304]{1,0:T(8,128)} fusion(bf16[1024,2304]{1,0:T(8,128)(2,1)S(1)} %bitcast.158, bf16[768,1024]{1,0:T(8,128)(2,1)S(1)} %collective-permute-done.10, bf16[768,1024]{1,0:T(8,128)(2,1)S(1)} %multiply_convert_fusion.3), kind=kOutput, calls=%fused_computation.207 | convolution fusion | flops 7254048768 | bytes 22020096 | tf_op jit(solution)/shard_map/dot_general | solution.py:100
  279.4 26.1 %multiply_convert_fusion.1 = (bf16[1536,2304]{1,0:T(8,128)(2,1)}, bf16[1536,2304]{1,0:T(8,128)(2,1)}, bf16[1536,2304]{1,0:T(8,128)(2,1)}) fusion(f32[1536,2304]{1,0:T(8,128)} %fusion.24, f32[1536,2304]{1,0:T(8,128)} %fusion.43, bf16[1024,2304]{1,0:T(8,128)(2,1)} %bitcast.29, bf16[768,1024]{1,0:T(8,128)(2,1)} %copy-done.74, ...), kind=kOutput, calls=%fused_computation.1 | convolution fusion | flops 7307132928 | bytes 57409536 | tf_op jit(solution)/shard_map/dot_general | solution.py:100
  305.5 12.9 %fusion.55 = f32[1536,1024]{1,0:T(8,128)} fusion(bf16[1536,2304]{1,0:T(8,128)(2,1)} %get-tuple-element.74, bf16[2304,1024]{1,0:T(8,128)(2,1)} %bitcast.36), kind=kOutput, calls=%fused_computation.217 | convolution fusion | flops 7247757312 | bytes 18087936 | tf_op jit(solution)/shard_map/dot_general | solution.py:100
  318.4 10.1 %convolution_convert_fusion.2 = bf16[2304,1024]{1,0:T(8,128)(2,1)S(1)} fusion(bf16[1536,2304]{1,0:T(8,128)(2,1)} %get-tuple-element.74, bf16[768,1024]{1,0:T(8,128)(2,1)S(1)} %collective-permute-done.25, bf16[768,1024]{1,0:T(8,128)(2,1)S(1)} %bitcast.180), kind=kOutput, calls=%fused_computation.12 | convolution fusion | flops 7256408064 | bytes 14942208 | tf_op jit(solution)/shard_map/dot_general | solution.py:94
  332.0 9.8 %fusion.56 = f32[1536,1024]{1,0:T(8,128)} fusion(bf16[1536,2304]{1,0:T(8,128)(2,1)S(1)} %bitcast.220, bf16[1024,2304]{1,0:T(8,128)(2,1)S(1)} %bitcast.159), kind=kOutput, calls=%fused_computation.218 | convolution fusion | flops 7247757312 | bytes 18087936 | tf_op jit(solution)/shard_map/dot_general | solution.py:104
  341.8 8.2 %convolution_convert_fusion = bf16[1024,2304]{1,0:T(8,128)(2,1)S(1)} fusion(bf16[1536,2304]{1,0:T(8,128)(2,1)S(1)} %bitcast.220, bf16[768,1024]{1,0:T(8,128)(2,1)S(1)} %copy-done.75, bf16[768,1024]{1,0:T(8,128)(2,1)S(1)} %multiply_convert_fusion.3), kind=kOutput, calls=%fused_computation.10 | convolution fusion | flops 7256408064 | bytes 14942208 | tf_op jit(solution)/shard_map/dot_general | solution.py:94
  352.5 12.4 %convolution_add_fusion = f32[1536,1024]{1,0:T(8,128)S(1)} fusion(f32[1536,1024]{1,0:T(8,128)} %fusion.56, bf16[1536,2304]{1,0:T(8,128)(2,1)} %get-tuple-element.72, bf16[1024,2304]{1,0:T(8,128)(2,1)} %bitcast.29), kind=kOutput, calls=%fused_computation.21 | convolution fusion | flops 7249330176 | bytes 24379392 | tf_op jit(solution)/shard_map/dot_general | solution.py:104
  365.0 1.9 slice.347
  366.9 2.0 collective-permute-start.26
  368.9 11.1 %convolution_convert_fusion.1 = bf16[1024,2304]{1,0:T(8,128)(2,1)S(1)} fusion(bf16[1536,2304]{1,0:T(8,128)(2,1)} %get-tuple-element.72, bf16[768,1024]{1,0:T(8,128)(2,1)} %copy-done.74, bf16[768,1024]{1,0:T(8,128)(2,1)S(1)} %copy-done.36), kind=kOutput, calls=%fused_computation.11 | convolution fusion | flops 7256408064 | bytes 14942208 | tf_op jit(solution)/shard_map/dot_general | solution.py:94
  386.0 9.9 %collective-permute-done.36 = bf16[2,1,64,2304]{3,2,1,0:T(8,128)(2,1)S(1)} collective-permute-done((bf16[2,1,64,2304]{3,2,1,0:T(8,128)(2,1)S(1)}, bf16[2,1,64,2304]{3,2,1,0:T(8,128)(2,1)S(1)}, u32[]{:S(2)}, u32[]{:S(2)}) %collective-permute-start.36) | collective-permute-done | bytes 589856 | tf_op jit(solution)/shard_map/ppermute | solution.py:18
  403.7 3.9 multiply_add_fusion
  407.6 4.6 fusion.30
  412.2 2.1 slice_select_fusion.1
  418.0 2.4 dynamic-slice_add_fusion.1
  420.3 4.5 collective-permute-done.42
  424.8 3.7 collective-permute-done.44
  428.5 3.1 add_convert_fusion.1
  431.7 4.4 fusion.28
  436.1 6.6 %multiply_reduce_fusion = (f32[512]{0:T(512)S(1)}, f32[1536,512]{1,0:T(8,128)S(1)}, bf16[1536,512]{1,0:T(8,128)(2,1)S(1)}) fusion(f32[1536,1536]{1,0:T(8,128)} %copy-done, f32[768,512]{1,0:T(8,128)} %collective-permute-done.27, f32[768,512]{1,0:T(8,128)S(1)} %copy-done.13, f32[2,768,512]{2,1,0:T(8,128)S(1)} %copy-done.4), kind=kLoop, calls=%fused_computation.52 | loop fusion | flops 7077376 | bytes 20449280 | tf_op jit(solution)/shard_map/reduce_sum | solution.py:252
  444.7 3.3 collective-permute-start.30
  448.0 2.3 collective-permute-done.28
  450.3 2.1 multiply_reduce_fusion.2
  454.4 5.1 fusion.25
  461.4 2.0 copy-done.10
  468.8 2.7 collective-permute-start.49
  471.6 3.5 add_convert_fusion.2
  475.4 3.0 fusion.23
  480.5 7.3 %convolution_convert_fusion.3 = bf16[1024,1536]{1,0:T(8,128)(2,1)} fusion(bf16[1536,512]{1,0:T(8,128)(2,1)S(1)} %copy-done.32, bf16[1536,512]{1,0:T(8,128)(2,1)S(1)} %copy-done.41, bf16[1536,512]{1,0:T(8,128)(2,1)S(1)} %copy-done.30, f32[1024]{0:T(1024)S(1)} %bitcast.202, f32[1536]{0:T(1024)S(1)} %copy-done.68, bf16[768,1024]{1,0:T(8,128)(2,1)S(1)} %copy-done.34, ...), kind=kOutput, calls=%fused_computation.22 | convolution fusion | flops 4858576896 | bytes 11020288 | tf_op jit(solution)/shard_map/dot_general | solution.py:94
  487.9 3.0 fusion.13
  491.2 2.2 pad_maximum_fusion.1
  495.0 3.0 collective-permute-done.49
  498.0 3.8 add_convert_fusion
  502.1 7.6 %collective-permute-done.31 = bf16[2,1,64,2176]{3,2,1,0:T(8,128)(2,1)S(1)} collective-permute-done((bf16[2,1,64,2176]{3,2,1,0:T(8,128)(2,1)}, bf16[2,1,64,2176]{3,2,1,0:T(8,128)(2,1)S(1)}, u32[]{:S(2)}, u32[]{:S(2)}) %collective-permute-start.31) | collective-permute-done | bytes 557088 | tf_op jit(solution)/shard_map/ppermute | solution.py:18
  519.2 12.6 %reduce-scatter.11.cloned.1.call-done = bf16[144,1024]{1,0:T(8,128)(2,1)} async-done(((bf16[576,1024]{1,0:T(8,128)(2,1)}), bf16[144,1024]{1,0:T(8,128)(2,1)}) %reduce-scatter.11.cloned.1.call-update) | async-done | bytes 294928 | tf_op jit(solution)/shard_map/reduce_scatter | solution.py:80
  533.6 4.3 collective-permute-done.32
  539.2 3.0 add_convert_fusion.3
  544.1 2.1 reshape.182
  548.1 2.1 reshape.181
  550.2 6.3 %fusion.12 = f32[1,768,1024]{2,1,0:T(8,128)} fusion(f32[768,1024]{1,0:T(8,128)} %copy-done.11, f32[768]{0:T(1024)S(1)} %broadcast_multiply_fusion, f32[1024]{0:T(1024)S(1)} %bitcast.204, f32[768]{0:T(1024)S(1)} %copy-done.58, bf16[1,768,1024]{2,1,0:T(8,128)(2,1)S(1)} %copy-done.8, f32[768,1024]{1,0:T(8,128)} %collective-permute-done.29, ...), kind=kLoop, calls=%fused_computation.30 | loop fusion | flops 6291456 | bytes 14166016 | tf_op jit(solution)/shard_map/broadcast_in_dim | solution.py:332
  556.5 13.9 %reduce-scatter.5.cloned.1.call-done = bf16[64,2176]{1,0:T(8,128)(2,1)} async-done(((bf16[256,2176]{1,0:T(8,128)(2,1)}), bf16[64,2176]{1,0:T(8,128)(2,1)}) %reduce-scatter.5.cloned.1.call-update) | async-done | bytes 278544 | tf_op jit(solution)/shard_map/reduce_scatter | solution.py:80
  (413 shorter events, 128.1 us)
Async XLA Ops:
  7.2 34.4 %all-gather.11.cloned.1.call-start = ((), (), s32[]{:S(2)}) async-start(), calls=%async_computation.7 | async-start | bytes 1474560 | tf_op jit(solution)/shard_map/all_gather | solution.py:40
  7.9 64.3 %all-gather.5.cloned.1.call-start = ((), (), s32[]{:S(2)}) async-start(), calls=%async_computation.4 | async-start | bytes 1392640 | tf_op jit(solution)/shard_map/all_gather | solution.py:40
  14.8 4.5 collective-permute-start.11
  16.3 1.5 collective-permute-start.1
  18.6 85.4 %all-gather.7.cloned.1.call-start = ((), (), s32[]{:S(2)}) async-start(), calls=%async_computation.5 | async-start | bytes 1474560 | tf_op jit(solution)/shard_map/all_gather | solution.py:40
  20.2 115.3 %all-gather.9.cloned.1.call-start = ((), (), s32[]{:S(2)}) async-start(), calls=%async_computation.6 | async-start | bytes 1474560 | tf_op jit(solution)/shard_map/all_gather | solution.py:40
  20.3 4.7 collective-permute-start
  21.4 2.4 collective-permute-start.7
  21.6 493.6 %reduce-scatter.9.cloned.1.call-start = ((), (), s32[]{:S(2)}) async-start(), calls=%async_computation.10 | async-start | bytes 1474560 | tf_op jit(solution)/shard_map/reduce_scatter | solution.py:80
  25.0 201.9 %copy-start.69 = (f32[2]{0:T(128)}, f32[2]{0:T(128)S(1)}, u32[]{:S(2)}) copy-start(f32[2]{0:T(128)S(1)} %maximum_subtract_fusion) | copy-start | bytes 28
  25.7 183.1 %copy-start.67 = (f32[1536]{0:T(1024)}, f32[1536]{0:T(1024)S(1)}, u32[]{:S(2)}) copy-start(f32[1536]{0:T(1024)S(1)} %add_rsqrt_fusion) | copy-start | bytes 18436
  41.6 105.5 %collective-permute-start.20 = (bf16[4,1,144,1024]{3,2,1,0:T(8,128)(2,1)}, bf16[4,1,144,1024]{3,2,1,0:T(8,128)(2,1)}, u32[]{:S(2)}, u32[]{:S(2)}) collective-permute-start(bf16[4,1,144,1024]{3,2,1,0:T(8,128)(2,1)} %bitcast.181), channel_id=1, source_target_pairs={{0,2},{2,0},{4,6},{6,4},{8,10},{10,8},{12,14},{14,12},{16,18},{18,... | collective-permute-start | bytes 3538952 | tf_op jit(solution)/shard_map/ppermute | solution.py:18
  42.8 107.1 %collective-permute-start.21 = (bf16[4,1,144,1024]{3,2,1,0:T(8,128)(2,1)}, bf16[4,1,144,1024]{3,2,1,0:T(8,128)(2,1)}, u32[]{:S(2)}, u32[]{:S(2)}) collective-permute-start(bf16[4,1,144,1024]{3,2,1,0:T(8,128)(2,1)} %bitcast.182), channel_id=1, source_target_pairs={{0,4},{2,6},{4,0},{6,2},{8,12},{10,14},{12,8},{14,10},{16,20},{18,... | collective-permute-start | bytes 3538952 | tf_op jit(solution)/shard_map/ppermute | solution.py:18
  72.3 65.2 %collective-permute-start.2 = (bf16[4,1,64,2176]{3,2,1,0:T(8,128)(2,1)}, bf16[4,1,64,2176]{3,2,1,0:T(8,128)(2,1)}, u32[]{:S(2)}, u32[]{:S(2)}) collective-permute-start(bf16[4,1,64,2176]{3,2,1,0:T(8,128)(2,1)} %bitcast.187), channel_id=1, source_target_pairs={{0,2},{2,0},{4,6},{6,4},{8,10},{10,8},{12,14},{14,12},{16,18},{18,... | collective-permute-start | bytes 3342344 | tf_op jit(solution)/shard_map/ppermute | solution.py:18
  73.4 69.0 %collective-permute-start.3 = (bf16[4,1,64,2176]{3,2,1,0:T(8,128)(2,1)}, bf16[4,1,64,2176]{3,2,1,0:T(8,128)(2,1)}, u32[]{:S(2)}, u32[]{:S(2)}) collective-permute-start(bf16[4,1,64,2176]{3,2,1,0:T(8,128)(2,1)} %bitcast.188), channel_id=1, source_target_pairs={{0,4},{2,6},{4,0},{6,2},{8,12},{10,14},{12,8},{14,10},{16,20},{18,... | collective-permute-start | bytes 3342344 | tf_op jit(solution)/shard_map/ppermute | solution.py:18
  104.0 53.2 %collective-permute-start.12 = (bf16[4,1,64,2304]{3,2,1,0:T(8,128)(2,1)}, bf16[4,1,64,2304]{3,2,1,0:T(8,128)(2,1)S(1)}, u32[]{:S(2)}, u32[]{:S(2)}) collective-permute-start(bf16[4,1,64,2304]{3,2,1,0:T(8,128)(2,1)} %bitcast.184), channel_id=1, source_target_pairs={{0,2},{2,0},{4,6},{6,4},{8,10},{10,8},{12,14},{14,12},{16,18},{18,... | collective-permute-start | bytes 3538952 | tf_op jit(solution)/shard_map/ppermute | solution.py:18
  137.4 26.4 %collective-permute-start.13 = (bf16[4,1,64,2304]{3,2,1,0:T(8,128)(2,1)S(1)}, bf16[4,1,64,2304]{3,2,1,0:T(8,128)(2,1)S(1)}, u32[]{:S(2)}, u32[]{:S(2)}) collective-permute-start(bf16[4,1,64,2304]{3,2,1,0:T(8,128)(2,1)S(1)} %bitcast.186), channel_id=1, source_target_pairs={{0,4},{2,6},{4,0},{6,2},{8,12},{10,14},{12,8},{14,10},{16,20},{18,... | collective-permute-start | bytes 3538952 | tf_op jit(solution)/shard_map/ppermute | solution.py:18
  142.5 88.0 %collective-permute-start.16 = (bf16[4,1,64,2304]{3,2,1,0:T(8,128)(2,1)}, bf16[4,1,64,2304]{3,2,1,0:T(8,128)(2,1)}, u32[]{:S(2)}, u32[]{:S(2)}) collective-permute-start(bf16[4,1,64,2304]{3,2,1,0:T(8,128)(2,1)} %bitcast.31), channel_id=1, source_target_pairs={{0,2},{2,0},{4,6},{6,4},{8,10},{10,8},{12,14},{14,12},{16,18},{18,... | collective-permute-start | bytes 3538952 | tf_op jit(solution)/shard_map/ppermute | solution.py:18
  147.1 86.7 %collective-permute-start.17 = (bf16[4,1,64,2304]{3,2,1,0:T(8,128)(2,1)}, bf16[4,1,64,2304]{3,2,1,0:T(8,128)(2,1)}, u32[]{:S(2)}, u32[]{:S(2)}) collective-permute-start(bf16[4,1,64,2304]{3,2,1,0:T(8,128)(2,1)} %bitcast.31), channel_id=1, source_target_pairs={{0,4},{2,6},{4,0},{6,2},{8,12},{10,14},{12,8},{14,10},{16,20},{18,... | collective-permute-start | bytes 3538952 | tf_op jit(solution)/shard_map/ppermute | solution.py:18
  149.9 51.1 %collective-permute-start.4 = (bf16[2,1,64,2176]{3,2,1,0:T(8,128)(2,1)S(1)}, bf16[2,1,64,2176]{3,2,1,0:T(8,128)(2,1)S(1)}, u32[]{:S(2)}, u32[]{:S(2)}) collective-permute-start(bf16[2,1,64,2176]{3,2,1,0:T(8,128)(2,1)S(1)} %slice.313), channel_id=1, source_target_pairs={{0,4},{2,6},{4,0},{6,2},{8,12},{10,14},{12,8},{14,10},{16,20},{18,... | collective-permute-start | bytes 1671176 | tf_op jit(solution)/shard_map/ppermute | solution.py:18
  157.2 45.8 %collective-permute-start.5 = (bf16[2,1,64,2176]{3,2,1,0:T(8,128)(2,1)S(1)}, bf16[2,1,64,2176]{3,2,1,0:T(8,128)(2,1)S(1)}, u32[]{:S(2)}, u32[]{:S(2)}) collective-permute-start(bf16[2,1,64,2176]{3,2,1,0:T(8,128)(2,1)S(1)} %slice.314), channel_id=1, source_target_pairs={{0,2},{2,0},{4,6},{6,4},{8,10},{10,8},{12,14},{14,12},{16,18},{18,... | collective-permute-start | bytes 1671176 | tf_op jit(solution)/shard_map/ppermute | solution.py:18
  163.8 72.6 %collective-permute-start.22 = (bf16[2,1,144,1024]{3,2,1,0:T(8,128)(2,1)}, bf16[2,1,144,1024]{3,2,1,0:T(8,128)(2,1)}, u32[]{:S(2)}, u32[]{:S(2)}) collective-permute-start(bf16[2,1,144,1024]{3,2,1,0:T(8,128)(2,1)} %slice.342), channel_id=1, source_target_pairs={{0,4},{2,6},{4,0},{6,2},{8,12},{10,14},{12,8},{14,10},{16,20},{18,... | collective-permute-start | bytes 1769480 | tf_op jit(solution)/shard_map/ppermute | solution.py:18
  200.9 39.4 %collective-permute-start.23 = (bf16[2,1,144,1024]{3,2,1,0:T(8,128)(2,1)}, bf16[2,1,144,1024]{3,2,1,0:T(8,128)(2,1)}, u32[]{:S(2)}, u32[]{:S(2)}) collective-permute-start(bf16[2,1,144,1024]{3,2,1,0:T(8,128)(2,1)} %slice.343), channel_id=1, source_target_pairs={{0,2},{2,0},{4,6},{6,4},{8,10},{10,8},{12,14},{14,12},{16,18},{18,... | collective-permute-start | bytes 1769480 | tf_op jit(solution)/shard_map/ppermute | solution.py:18
  208.8 40.0 %copy-start.56 = (f32[1,1024]{1,0:T(1,128)}, f32[1,1024]{1,0:T(1,128)S(1)}, u32[]{:S(2)}) copy-start(f32[1,1024]{1,0:T(1,128)S(1)} %get-tuple-element.141) | copy-start | bytes 12292
  217.0 5.3 collective-permute-start.6
  222.3 21.8 %collective-permute-start.9 = (bf16[16,64,512]{2,1,0:T(8,128)(2,1)S(1)}, bf16[16,64,512]{2,1,0:T(8,128)(2,1)S(1)}, u32[]{:S(2)}, u32[]{:S(2)}) collective-permute-start(bf16[16,64,512]{2,1,0:T(8,128)(2,1)S(1)} %slice.328), channel_id=1, source_target_pairs={{0,1},{1,0},{2,3},{3,2},{4,5},{5,4},{6,7},{7,6},{8,9},{9,8},{10,11... | collective-permute-start | bytes 3145736 | tf_op jit(solution)/shard_map/ppermute | solution.py:13
  230.5 12.6 %collective-permute-start.8 = (bf16[768,512]{1,0:T(8,128)(2,1)S(1)}, bf16[768,512]{1,0:T(8,128)(2,1)S(1)}, u32[]{:S(2)}, u32[]{:S(2)}) collective-permute-start(bf16[768,512]{1,0:T(8,128)(2,1)S(1)} %slice.327), channel_id=1, source_target_pairs={{0,1},{1,0},{2,3},{3,2},{4,5},{5,4},{6,7},{7,6},{8,9},{9,8},{10,11... | collective-permute-start | bytes 2359304 | tf_op jit(solution)/shard_map/ppermute | solution.py:13
  233.8 17.0 %collective-permute-start.25 = (bf16[768,1024]{1,0:T(8,128)(2,1)S(1)}, bf16[768,1024]{1,0:T(8,128)(2,1)S(1)}, u32[]{:S(2)}, u32[]{:S(2)}) collective-permute-start(bf16[768,1024]{1,0:T(8,128)(2,1)S(1)} %bitcast.178), channel_id=1, source_target_pairs={{0,1},{1,0},{2,3},{3,2},{4,5},{5,4},{6,7},{7,6},{8,9},{9,8},{10,11... | collective-permute-start | bytes 4718600 | tf_op jit(solution)/shard_map/ppermute | solution.py:13
  236.4 29.6 %collective-permute-start.14 = (bf16[2,1,64,2304]{3,2,1,0:T(8,128)(2,1)S(1)}, bf16[2,1,64,2304]{3,2,1,0:T(8,128)(2,1)S(1)}, u32[]{:S(2)}, u32[]{:S(2)}) collective-permute-start(bf16[2,1,64,2304]{3,2,1,0:T(8,128)(2,1)S(1)} %slice.338), channel_id=1, source_target_pairs={{0,4},{2,6},{4,0},{6,2},{8,12},{10,14},{12,8},{14,10},{16,20},{18,... | collective-permute-start | bytes 1769480 | tf_op jit(solution)/shard_map/ppermute | solution.py:18
  240.3 26.6 %collective-permute-start.15 = (bf16[2,1,64,2304]{3,2,1,0:T(8,128)(2,1)S(1)}, bf16[2,1,64,2304]{3,2,1,0:T(8,128)(2,1)S(1)}, u32[]{:S(2)}, u32[]{:S(2)}) collective-permute-start(bf16[2,1,64,2304]{3,2,1,0:T(8,128)(2,1)S(1)} %slice.339), channel_id=1, source_target_pairs={{0,2},{2,0},{4,6},{6,4},{8,10},{10,8},{12,14},{14,12},{16,18},{18,... | collective-permute-start | bytes 1769480 | tf_op jit(solution)/shard_map/ppermute | solution.py:18
  243.1 24.6 %collective-permute-start.18 = (bf16[2,1,64,2304]{3,2,1,0:T(8,128)(2,1)S(1)}, bf16[2,1,64,2304]{3,2,1,0:T(8,128)(2,1)S(1)}, u32[]{:S(2)}, u32[]{:S(2)}) collective-permute-start(bf16[2,1,64,2304]{3,2,1,0:T(8,128)(2,1)S(1)} %slice.340), channel_id=1, source_target_pairs={{0,4},{2,6},{4,0},{6,2},{8,12},{10,14},{12,8},{14,10},{16,20},{18,... | collective-permute-start | bytes 1769480 | tf_op jit(solution)/shard_map/ppermute | solution.py:18
  244.1 23.8 %collective-permute-start.19 = (bf16[2,1,64,2304]{3,2,1,0:T(8,128)(2,1)S(1)}, bf16[2,1,64,2304]{3,2,1,0:T(8,128)(2,1)S(1)}, u32[]{:S(2)}, u32[]{:S(2)}) collective-permute-start(bf16[2,1,64,2304]{3,2,1,0:T(8,128)(2,1)S(1)} %slice.341), channel_id=1, source_target_pairs={{0,2},{2,0},{4,6},{6,4},{8,10},{10,8},{12,14},{14,12},{16,18},{18,... | collective-permute-start | bytes 1769480 | tf_op jit(solution)/shard_map/ppermute | solution.py:18
  250.8 90.9 %copy-start.35 = (bf16[768,1024]{1,0:T(8,128)(2,1)}, bf16[768,1024]{1,0:T(8,128)(2,1)S(1)}, u32[]{:S(2)}) copy-start(bf16[768,1024]{1,0:T(8,128)(2,1)S(1)} %multiply_convert_fusion.3) | copy-start | bytes 4718596
  250.9 17.0 %collective-permute-start.10 = (bf16[768,1024]{1,0:T(8,128)(2,1)S(1)}, bf16[768,1024]{1,0:T(8,128)(2,1)S(1)}, u32[]{:S(2)}, u32[]{:S(2)}) collective-permute-start(bf16[768,1024]{1,0:T(8,128)(2,1)S(1)} %multiply_convert_fusion.3), channel_id=1, source_target_pairs={{0,1},{1,0},{2,3},{3,2},{4,5},{5,4},{6,7},{7,6},{8,9},{9,8},{10,11... | collective-permute-start | bytes 4718600 | tf_op jit(solution)/shard_map/ppermute | solution.py:13
  305.5 26.5 %slice-start.9 = ((s8[7077888]{0:T(1024)(128)(4,1)}), s8[4194304]{0:T(1024)(128)(4,1)S(1)}, s32[]{:S(2)}) async-start(s8[7077888]{0:T(1024)(128)(4,1)} %bitcast.219), calls=%async_computation.21 | async-start | bytes 8388608
  328.6 89.4 %copy-start.15 = (bf16[2304,1024]{1,0:T(8,128)(2,1)}, bf16[2304,1024]{1,0:T(8,128)(2,1)S(1)}, u32[]{:S(2)}) copy-start(bf16[2304,1024]{1,0:T(8,128)(2,1)S(1)} %convolution_convert_fusion.2) | copy-start | bytes 14155780
  330.1 86.7 %collective-permute-start.46 = (bf16[2,1,144,1024]{3,2,1,0:T(8,128)(2,1)}, bf16[2,1,144,1024]{3,2,1,0:T(8,128)(2,1)}, u32[]{:S(2)}, u32[]{:S(2)}) collective-permute-start(bf16[2,1,144,1024]{3,2,1,0:T(8,128)(2,1)} %get-tuple-element.82), channel_id=1, source_target_pairs={{0,4},{2,6},{4,0},{6,2},{8,12},{10,14},{12,8},{14,10},{16,20},{18,... | collective-permute-start | bytes 1769480 | tf_op jit(solution)/shard_map/ppermute | solution.py:18
  331.2 86.1 %collective-permute-start.48 = (bf16[2,1,144,1024]{3,2,1,0:T(8,128)(2,1)}, bf16[2,1,144,1024]{3,2,1,0:T(8,128)(2,1)}, u32[]{:S(2)}, u32[]{:S(2)}) collective-permute-start(bf16[2,1,144,1024]{3,2,1,0:T(8,128)(2,1)} %get-tuple-element.81), channel_id=1, source_target_pairs={{0,2},{2,0},{4,6},{6,4},{8,10},{10,8},{12,14},{14,12},{16,18},{18,... | collective-permute-start | bytes 1769480 | tf_op jit(solution)/shard_map/ppermute | solution.py:18
  351.5 30.3 %collective-permute-start.41 = (bf16[2,1,64,2304]{3,2,1,0:T(8,128)(2,1)}, bf16[2,1,64,2304]{3,2,1,0:T(8,128)(2,1)}, u32[]{:S(2)}, u32[]{:S(2)}) collective-permute-start(bf16[2,1,64,2304]{3,2,1,0:T(8,128)(2,1)} %get-tuple-element.88), channel_id=1, source_target_pairs={{0,4},{2,6},{4,0},{6,2},{8,12},{10,14},{12,8},{14,10},{16,20},{18,... | collective-permute-start | bytes 1769480 | tf_op jit(solution)/shard_map/ppermute | solution.py:18
  352.4 30.1 %collective-permute-start.43 = (bf16[2,1,64,2304]{3,2,1,0:T(8,128)(2,1)}, bf16[2,1,64,2304]{3,2,1,0:T(8,128)(2,1)}, u32[]{:S(2)}, u32[]{:S(2)}) collective-permute-start(bf16[2,1,64,2304]{3,2,1,0:T(8,128)(2,1)} %get-tuple-element.87), channel_id=1, source_target_pairs={{0,2},{2,0},{4,6},{6,4},{8,10},{10,8},{12,14},{14,12},{16,18},{18,... | collective-permute-start | bytes 1769480 | tf_op jit(solution)/shard_map/ppermute | solution.py:18
  366.9 34.8 %collective-permute-start.26 = (f32[768,1024]{1,0:T(8,128)}, f32[768,1024]{1,0:T(8,128)S(1)}, u32[]{:S(2)}, u32[]{:S(2)}) collective-permute-start(f32[768,1024]{1,0:T(8,128)} %slice.347), channel_id=1, source_target_pairs={{0,1},{1,0},{2,3},{3,2},{4,5},{5,4},{6,7},{7,6},{8,9},{9,8},{10,11... | collective-permute-start | bytes 9437192 | tf_op jit(solution)/shard_map/ppermute | solution.py:13
  381.8 14.1 %collective-permute-start.36 = (bf16[2,1,64,2304]{3,2,1,0:T(8,128)(2,1)S(1)}, bf16[2,1,64,2304]{3,2,1,0:T(8,128)(2,1)S(1)}, u32[]{:S(2)}, u32[]{:S(2)}) collective-permute-start(bf16[2,1,64,2304]{3,2,1,0:T(8,128)(2,1)S(1)} %get-tuple-element.94), channel_id=1, source_target_pairs={{0,4},{2,6},{4,0},{6,2},{8,12},{10,14},{12,8},{14,10},{16,20},{18,... | collective-permute-start | bytes 1769480 | tf_op jit(solution)/shard_map/ppermute | solution.py:18
  382.5 15.1 %collective-permute-start.38 = (bf16[2,1,64,2304]{3,2,1,0:T(8,128)(2,1)S(1)}, bf16[2,1,64,2304]{3,2,1,0:T(8,128)(2,1)S(1)}, u32[]{:S(2)}, u32[]{:S(2)}) collective-permute-start(bf16[2,1,64,2304]{3,2,1,0:T(8,128)(2,1)S(1)} %get-tuple-element.93), channel_id=1, source_target_pairs={{0,2},{2,0},{4,6},{6,4},{8,10},{10,8},{12,14},{14,12},{16,18},{18,... | collective-permute-start | bytes 1769480 | tf_op jit(solution)/shard_map/ppermute | solution.py:18
  395.9 7.7 %collective-permute-start.24 = (bf16[768,1024]{1,0:T(8,128)(2,1)}, bf16[768,1024]{1,0:T(8,128)(2,1)}, u32[]{:S(2)}, u32[]{:S(2)}) collective-permute-start(bf16[768,1024]{1,0:T(8,128)(2,1)} %slice.484), channel_id=1, source_target_pairs={{0,1},{1,0},{2,3},{3,2},{4,5},{5,4},{6,7},{7,6},{8,9},{9,8},{10,11... | collective-permute-start | bytes 4718600 | tf_op jit(solution)/shard_map/ppermute | solution.py:13
  397.6 27.2 %collective-permute-start.42 = (bf16[4,1,64,2304]{3,2,1,0:T(8,128)(2,1)}, bf16[4,1,64,2304]{3,2,1,0:T(8,128)(2,1)}, u32[]{:S(2)}, u32[]{:S(2)}) collective-permute-start(bf16[4,1,64,2304]{3,2,1,0:T(8,128)(2,1)} %pad_maximum_fusion.15), channel_id=1, source_target_pairs={{0,2},{2,0},{4,6},{6,4},{8,10},{10,8},{12,14},{14,12},{16,18},{18,... | collective-permute-start | bytes 3538952 | tf_op jit(solution)/shard_map/ppermute | solution.py:18
  401.8 26.8 %collective-permute-start.44 = (bf16[4,1,64,2304]{3,2,1,0:T(8,128)(2,1)}, bf16[4,1,64,2304]{3,2,1,0:T(8,128)(2,1)}, u32[]{:S(2)}, u32[]{:S(2)}) collective-permute-start(bf16[4,1,64,2304]{3,2,1,0:T(8,128)(2,1)} %pad_maximum_fusion.16), channel_id=1, source_target_pairs={{0,4},{2,6},{4,0},{6,2},{8,12},{10,14},{12,8},{14,10},{16,20},{18,... | collective-permute-start | bytes 3538952 | tf_op jit(solution)/shard_map/ppermute | solution.py:18
  414.3 21.8 %collective-permute-start.27 = (f32[768,512]{1,0:T(8,128)}, f32[768,512]{1,0:T(8,128)}, u32[]{:S(2)}, u32[]{:S(2)}) collective-permute-start(f32[768,512]{1,0:T(8,128)} %get-tuple-element.108), channel_id=1, source_target_pairs={{0,1},{1,0},{2,3},{3,2},{4,5},{5,4},{6,7},{7,6},{8,9},{9,8},{10,11... | collective-permute-start | bytes 4718600 | tf_op jit(solution)/shard_map/ppermute | solution.py:13
  416.8 52.1 %collective-permute-start.37 = (bf16[4,1,64,2304]{3,2,1,0:T(8,128)(2,1)}, bf16[4,1,64,2304]{3,2,1,0:T(8,128)(2,1)}, u32[]{:S(2)}, u32[]{:S(2)}) collective-permute-start(bf16[4,1,64,2304]{3,2,1,0:T(8,128)(2,1)} %pad_maximum_fusion.13), channel_id=1, source_target_pairs={{0,2},{2,0},{4,6},{6,4},{8,10},{10,8},{12,14},{14,12},{16,18},{18,... | collective-permute-start | bytes 3538952 | tf_op jit(solution)/shard_map/ppermute | solution.py:18
  417.3 54.2 %collective-permute-start.39 = (bf16[4,1,64,2304]{3,2,1,0:T(8,128)(2,1)}, bf16[4,1,64,2304]{3,2,1,0:T(8,128)(2,1)}, u32[]{:S(2)}, u32[]{:S(2)}) collective-permute-start(bf16[4,1,64,2304]{3,2,1,0:T(8,128)(2,1)} %pad_maximum_fusion.14), channel_id=1, source_target_pairs={{0,4},{2,6},{4,0},{6,2},{8,12},{10,14},{12,8},{14,10},{16,20},{18,... | collective-permute-start | bytes 3538952 | tf_op jit(solution)/shard_map/ppermute | solution.py:18
  431.6 85.8 %reduce-scatter.7.cloned.1.call-start = ((), (), s32[]{:S(2)}) async-start(), calls=%async_computation.9 | async-start | bytes 1474560 | tf_op jit(solution)/shard_map/reduce_scatter | solution.py:80
  442.9 7.4 %collective-permute-start.28 = (f32[2,2,512]{2,1,0:T(2,128)S(1)}, f32[2,2,512]{2,1,0:T(2,128)S(1)}, u32[]{:S(2)}, u32[]{:S(2)}) collective-permute-start(f32[2,2,512]{2,1,0:T(2,128)S(1)} %maximum_multiply_fusion), channel_id=1, source_target_pairs={{2,0},{4,2},{6,4},{8,6},{10,8},{12,10},{14,12},{16,14},{18,16},{20... | collective-permute-start | bytes 24584 | tf_op jit(solution)/shard_map/ppermute | solution.py:24
  444.7 30.7 %collective-permute-start.30 = (bf16[16,32,1024]{2,1,0:T(8,128)(2,1)S(1)}, bf16[16,32,1024]{2,1,0:T(8,128)(2,1)S(1)}, u32[]{:S(2)}, u32[]{:S(2)}) collective-permute-start(bf16[16,32,1024]{2,1,0:T(8,128)(2,1)S(1)} %fusion.27), channel_id=1, source_target_pairs={{0,1},{1,0},{2,3},{3,2},{4,5},{5,4},{6,7},{7,6},{8,9},{9,8},{10,11... | collective-permute-start | bytes 3145736 | tf_op jit(solution)/shard_map/ppermute | solution.py:13
  463.4 24.4 %collective-permute-start.29 = (f32[768,1024]{1,0:T(8,128)}, f32[768,1024]{1,0:T(8,128)}, u32[]{:S(2)}, u32[]{:S(2)}) collective-permute-start(f32[768,1024]{1,0:T(8,128)} %slice.353), channel_id=1, source_target_pairs={{0,1},{1,0},{2,3},{3,2},{4,5},{5,4},{6,7},{7,6},{8,9},{9,8},{10,11... | collective-permute-start | bytes 9437192 | tf_op jit(solution)/shard_map/ppermute | solution.py:13
  466.2 28.8 %collective-permute-start.47 = (bf16[4,1,144,1024]{3,2,1,0:T(8,128)(2,1)}, bf16[4,1,144,1024]{3,2,1,0:T(8,128)(2,1)}, u32[]{:S(2)}, u32[]{:S(2)}) collective-permute-start(bf16[4,1,144,1024]{3,2,1,0:T(8,128)(2,1)} %pad_maximum_fusion.17), channel_id=1, source_target_pairs={{0,2},{2,0},{4,6},{6,4},{8,10},{10,8},{12,14},{14,12},{16,18},{18,... | collective-permute-start | bytes 3538952 | tf_op jit(solution)/shard_map/ppermute | solution.py:18
  468.8 29.2 %collective-permute-start.49 = (bf16[4,1,144,1024]{3,2,1,0:T(8,128)(2,1)}, bf16[4,1,144,1024]{3,2,1,0:T(8,128)(2,1)}, u32[]{:S(2)}, u32[]{:S(2)}) collective-permute-start(bf16[4,1,144,1024]{3,2,1,0:T(8,128)(2,1)} %pad_maximum_fusion.18), channel_id=1, source_target_pairs={{0,4},{2,6},{4,0},{6,2},{8,12},{10,14},{12,8},{14,10},{16,20},{18,... | collective-permute-start | bytes 3538952 | tf_op jit(solution)/shard_map/ppermute | solution.py:18
  475.1 56.6 %reduce-scatter.11.cloned.1.call-start = ((), (), s32[]{:S(2)}) async-start(), calls=%async_computation.11 | async-start | bytes 1474560 | tf_op jit(solution)/shard_map/reduce_scatter | solution.py:80
  494.8 14.9 %collective-permute-start.31 = (bf16[2,1,64,2176]{3,2,1,0:T(8,128)(2,1)}, bf16[2,1,64,2176]{3,2,1,0:T(8,128)(2,1)S(1)}, u32[]{:S(2)}, u32[]{:S(2)}) collective-permute-start(bf16[2,1,64,2176]{3,2,1,0:T(8,128)(2,1)} %get-tuple-element.100), channel_id=1, source_target_pairs={{0,4},{2,6},{4,0},{6,2},{8,12},{10,14},{12,8},{14,10},{16,20},{18,... | collective-permute-start | bytes 1671176 | tf_op jit(solution)/shard_map/ppermute | solution.py:18
  495.0 14.7 %collective-permute-start.33 = (bf16[2,1,64,2176]{3,2,1,0:T(8,128)(2,1)}, bf16[2,1,64,2176]{3,2,1,0:T(8,128)(2,1)}, u32[]{:S(2)}, u32[]{:S(2)}) collective-permute-start(bf16[2,1,64,2176]{3,2,1,0:T(8,128)(2,1)} %get-tuple-element.99), channel_id=1, source_target_pairs={{0,2},{2,0},{4,6},{6,4},{8,10},{10,8},{12,14},{14,12},{16,18},{18,... | collective-permute-start | bytes 1671176 | tf_op jit(solution)/shard_map/ppermute | solution.py:18
  501.8 68.6 %reduce-scatter.5.cloned.1.call-start = ((), (), s32[]{:S(2)}) async-start(), calls=%async_computation.8 | async-start | bytes 1392640 | tf_op jit(solution)/shard_map/reduce_scatter | solution.py:80
  512.4 25.5 %collective-permute-start.32 = (bf16[4,1,64,2176]{3,2,1,0:T(8,128)(2,1)}, bf16[4,1,64,2176]{3,2,1,0:T(8,128)(2,1)S(1)}, u32[]{:S(2)}, u32[]{:S(2)}) collective-permute-start(bf16[4,1,64,2176]{3,2,1,0:T(8,128)(2,1)} %pad_maximum_fusion.19), channel_id=1, source_target_pairs={{0,2},{2,0},{4,6},{6,4},{8,10},{10,8},{12,14},{14,12},{16,18},{18,... | collective-permute-start | bytes 3342344 | tf_op jit(solution)/shard_map/ppermute | solution.py:18
  513.7 25.5 %collective-permute-start.34 = (bf16[4,1,64,2176]{3,2,1,0:T(8,128)(2,1)}, bf16[4,1,64,2176]{3,2,1,0:T(8,128)(2,1)}, u32[]{:S(2)}, u32[]{:S(2)}) collective-permute-start(bf16[4,1,64,2176]{3,2,1,0:T(8,128)(2,1)} %pad_maximum_fusion.20), channel_id=1, source_target_pairs={{0,4},{2,6},{4,0},{6,2},{8,12},{10,14},{12,8},{14,10},{16,20},{18,... | collective-permute-start | bytes 3342344 | tf_op jit(solution)/shard_map/ppermute | solution.py:18
  516.2 26.0 %collective-permute-start.45 = (bf16[32,2304]{1,0:T(8,128)(2,1)S(1)}, bf16[32,2304]{1,0:T(8,128)(2,1)S(1)}, u32[]{:S(2)}, u32[]{:S(2)}) collective-permute-start(bf16[32,2304]{1,0:T(8,128)(2,1)S(1)} %broadcast_select_fusion.10), channel_id=1, source_target_pairs={{0,1},{1,0},{2,3},{3,2},{4,5},{5,4},{6,7},{7,6},{8,9},{9,8},{10,11... | collective-permute-start | bytes 442376 | tf_op jit(solution)/shard_map/ppermute | solution.py:13
  519.1 27.1 %collective-permute-start.40 = (bf16[32,2304]{1,0:T(8,128)(2,1)}, bf16[32,2304]{1,0:T(8,128)(2,1)S(1)}, u32[]{:S(2)}, u32[]{:S(2)}) collective-permute-start(bf16[32,2304]{1,0:T(8,128)(2,1)} %broadcast_select_fusion.14), channel_id=1, source_target_pairs={{0,1},{1,0},{2,3},{3,2},{4,5},{5,4},{6,7},{7,6},{8,9},{9,8},{10,11... | collective-permute-start | bytes 442376 | tf_op jit(solution)/shard_map/ppermute | solution.py:13
  571.4 2.4 collective-permute-start.35
  (81 other events, 533.1 us)
Sparse Core Ops, SparseCore 0:
  9.6 31.9 all-gather.10
  43.7 28.4 all-gather.4
  74.4 29.5 all-gather.6
  106.0 29.5 all-gather.8
  431.7 30.1 reduce-scatter.8
  475.2 25.6 reduce-scatter.6
  503.8 27.8 reduce-scatter.10
  542.3 28.0 reduce-scatter.4

commit v2 on v1

--- a/solution.py
+++ b/solution.py
@@ -1,6 +1,8 @@
 import jax
 import jax.numpy as jnp
 from jax import lax
+from jax.experimental import pallas as pl
+from jax.experimental.pallas import tpu as pltpu
 from jax.sharding import PartitionSpec as P
 
 EPSILON = 1e-05
@@ -28,62 +30,116 @@
     return [[4 * z + p for z in range(peers // 4)] for p in range(4)]
 
 
-def gather_chips(shard):
+def after(x, *before):
+    return lax.optimization_barrier((x, *before))[0]
+
+
+def line_gather(shard):
     peers = lax.axis_size("seq")
     rows, cols = shard.shape
     if peers != 16:
         whole = lax.all_gather(shard, "seq", axis=0, tiled=True)
-        return whole.reshape(peers, rows, cols)
-    depth = peers // 4
-    half = depth // 2
-    plane = lax.axis_index("seq") % 4
-    line = lax.all_gather(
+        return whole.reshape(peers // 4, 4, rows, cols)
+    return lax.all_gather(
         shard, "seq", axis_index_groups=columns_of_line(peers), axis=0, tiled=True
-    ).reshape(depth, 1, rows, cols)
-    from_x = across(line, 1)
-    from_y = across(line, 2)
-    corner_low = across(from_x[:half], 2)
-    corner_high = across(from_y[half:], 1)
-    whole = jnp.zeros((depth, 4, rows, cols), shard.dtype)
-    whole = lax.dynamic_update_slice(whole, line, (0, plane, 0, 0))
-    whole = lax.dynamic_update_slice(whole, from_x, (0, plane ^ 1, 0, 0))
-    whole = lax.dynamic_update_slice(whole, from_y, (0, plane ^ 2, 0, 0))
-    whole = lax.dynamic_update_slice(whole, corner_low, (0, plane ^ 3, 0, 0))
-    whole = lax.dynamic_update_slice(whole, corner_high, (half, plane ^ 3, 0, 0))
-    return whole.reshape(peers, rows, cols)
-
-
-def scatter_chips(terms):
-    peers, rows, cols = terms.shape
-    if peers != 16:
-        flat = terms.reshape(peers * rows, cols)
-        return lax.psum_scatter(flat, "seq", scatter_dimension=0, tiled=True)
-    depth = peers // 4
-    half = depth // 2
-    plane = lax.axis_index("seq") % 4
-    terms = terms.reshape(depth, 4, rows, cols)
-
-    def piece(bits, start, count):
+    ).reshape(peers // 4, 1, rows, cols)
+
+
+class Plane:
+    def __init__(self, line):
+        self.line = line
+        self.direct = lax.axis_size("seq") != 16
+        if self.direct:
+            self.from_x = self.from_y = self.low = self.high = line
+            return
+        self.from_x = across(line, 1)
+        self.from_y = across(line, 2)
+
+    def corners(self):
+        if self.direct:
+            return
+        depth, _, rows, _ = self.line.shape
+        if depth > 1:
+            half = depth // 2
+            self.low = across(self.from_x[:half], 2)
+            self.high = across(self.from_y[half:], 1)
+            self.high_at = (half, 0)
+        else:
+            half = rows // 32 * 16
+            self.low = across(self.from_x[:, :, :half], 2)
+            self.high = across(self.from_y[:, :, half:], 1)
+            self.high_at = (0, half)
+
+    def place(self, pick=lambda block: block):
+        plane = lax.axis_index("seq") % 4
+        line = pick(self.line)
+        if self.direct:
+            return line
+        depth, _, rows, cols = line.shape
+        whole = jnp.zeros((depth, 4, rows, cols), line.dtype)
+        put = lax.dynamic_update_slice
+        whole = put(whole, line, (0, plane, 0, 0))
+        whole = put(whole, pick(self.from_x), (0, plane ^ 1, 0, 0))
+        whole = put(whole, pick(self.from_y), (0, plane ^ 2, 0, 0))
+        whole = put(whole, pick(self.low), (0, plane ^ 3, 0, 0))
+        deep, row = self.high_at
+        return put(whole, pick(self.high), (deep, plane ^ 3, row, 0))
+
+
+class Scatter:
+    def __init__(self, terms):
+        self.peers, self.rows, self.cols = terms.shape
+        self.depth = self.peers // 4
+        self.half = self.depth // 2
+        self.terms = terms
+        if self.peers == 16:
+            self.terms = terms.reshape(self.depth, 4, self.rows, self.cols)
+
+    def piece(self, bits, start, count):
+        plane = lax.axis_index("seq") % 4
         return lax.dynamic_slice(
-            terms, (start, plane ^ bits, 0, 0), (count, 1, rows, cols)
+            self.terms, (start, plane ^ bits, 0, 0), (count, 1, self.rows, self.cols)
         )
 
-    add_y = across(piece(3, 0, half), 1)
-    add_x = across(piece(3, half, half), 2)
-    for_x = jnp.concatenate([piece(1, 0, half), piece(1, half, half) + add_x], axis=0)
-    for_y = jnp.concatenate([piece(2, 0, half) + add_y, piece(2, half, half)], axis=0)
-    mine = (
-        piece(0, 0, depth).astype(F32)
-        + across(for_x, 1).astype(F32)
-        + across(for_y, 2).astype(F32)
-    ).astype(BF16)
-    return lax.psum_scatter(
-        mine.reshape(depth * rows, cols),
-        "seq",
-        axis_index_groups=columns_of_line(peers),
-        scatter_dimension=0,
-        tiled=True,
-    )
+    def opened(self, x):
+        if self.peers != 16:
+            return x
+        self.sent = [self.piece(3, 0, self.half), self.piece(3, self.half, self.half)]
+        *self.sent, x = lax.optimization_barrier((*self.sent, x))
+        self.add_y = across(self.sent[0], 1)
+        self.add_x = across(self.sent[1], 2)
+        return x
+
+    def turned(self, x):
+        if self.peers != 16:
+            return x
+        half, piece = self.half, self.piece
+        add_y, add_x, x = lax.optimization_barrier((self.add_y, self.add_x, x))
+        for_x = jnp.concatenate([piece(1, 0, half), piece(1, half, half) + add_x], axis=0)
+        for_y = jnp.concatenate([piece(2, 0, half) + add_y, piece(2, half, half)], axis=0)
+        for_x, for_y, x = lax.optimization_barrier((for_x, for_y, x))
+        self.from_x = across(for_x, 1)
+        self.from_y = across(for_y, 2)
+        return x
+
+    def landed(self, x):
+        if self.peers != 16:
+            flat = self.terms.reshape(self.peers * self.rows, self.cols)
+            self.shard = lax.psum_scatter(flat, "seq", scatter_dimension=0, tiled=True)
+            return x
+        from_x, from_y, x = lax.optimization_barrier((self.from_x, self.from_y, x))
+        mine = (
+            self.piece(0, 0, self.depth).astype(F32) + from_x.astype(F32) + from_y.astype(F32)
+        ).astype(BF16)
+        mine, x = lax.optimization_barrier((mine, x))
+        self.shard = lax.psum_scatter(
+            mine.reshape(self.depth * self.rows, self.cols),
+            "seq",
+            axis_index_groups=columns_of_line(self.peers),
+            scatter_dimension=0,
+            tiled=True,
+        )
+        return x
 
 
 def rms_scale(values):
@@ -104,6 +160,212 @@
     return lax.dot_general(
         left, right, (((1,), (1,)), ((), ())), preferred_element_type=F32
     )
+
+
+def chunked(rows):
+    step = 256 if rows % 256 == 0 else rows
+    return [pl.ds(start, step) for start in range(0, rows, step)]
+
+
+def call(body, grid, ins, outs, args, flops):
+    return pl.pallas_call(
+        body,
+        grid=(grid,),
+        in_specs=ins,
+        out_specs=[spec for _, spec in outs],
+        out_shape=[shape for shape, _ in outs],
+        compiler_params=pltpu.CompilerParams(vmem_limit_bytes=44 * 1024 * 1024),
+        cost_estimate=pl.CostEstimate(
+            flops=flops, bytes_accessed=flops // 500, transcendentals=0
+        ),
+    )(*args)
+
+
+def column_tile(cols):
+    for tile in (256, 128):
+        if cols % tile == 0:
+            return tile
+    return cols
+
+
+def held(x):
+    return pl.BlockSpec(x.shape, lambda i: (0, 0))
+
+
+def by_columns(rows, tile):
+    return pl.BlockSpec((rows, tile), lambda i: (0, i))
+
+
+def by_rows(tile, cols):
+    return pl.BlockSpec((tile, cols), lambda i: (i, 0))
+
+
+def gate_kernel(hidden, weight):
+    rows, depth = hidden.shape
+    cols = weight.shape[1]
+    tile = column_tile(cols)
+
+    def body(hidden_ref, weight_ref, gate_ref):
+        for part in chunked(rows):
+            gate_ref[part, :] = times(hidden_ref[part, :], weight_ref[...]).astype(BF16)
+
+    out = jax.ShapeDtypeStruct((rows, cols), BF16)
+    return call(
+        body,
+        cols // tile,
+        [held(hidden), by_columns(depth, tile)],
+        [(out, by_columns(rows, tile))],
+        (hidden, weight),
+        2 * rows * depth * cols,
+    )[0]
+
+
+def active_kernel(hidden, weight, gate):
+    rows, depth = hidden.shape
+    cols = weight.shape[1]
+    tile = column_tile(cols)
+
+    def body(hidden_ref, weight_ref, gate_ref, active_ref, upper_ref):
+        for part in chunked(rows):
+            upper = times(hidden_ref[part, :], weight_ref[...])
+            gate = gate_ref[part, :].astype(F32)
+            active_ref[part, :] = (gate * lax.logistic(gate) * upper).astype(BF16)
+            upper_ref[part, :] = upper.astype(BF16)
+
+    out = jax.ShapeDtypeStruct((rows, cols), BF16)
+    block = by_columns(rows, tile)
+    return call(
+        body,
+        cols // tile,
+        [held(hidden), by_columns(depth, tile), block],
+        [(out, block), (out, block)],
+        (hidden, weight, gate),
+        2 * rows * depth * cols,
+    )
+
+
+def split_kernel(d_down, weight, gate, upper):
+    rows, depth = d_down.shape
+    cols = weight.shape[0]
+    tile = column_tile(cols)
+
+    def body(d_down_ref, weight_ref, gate_ref, upper_ref, d_gate_ref, d_upper_ref):
+        for part in chunked(rows):
+            d_active = times_transposed(d_down_ref[part, :], weight_ref[...])
+            gate = gate_ref[part, :].astype(F32)
+            sigmoid = lax.logistic(gate)
+            silu = gate * sigmoid
+            upper = upper_ref[part, :].astype(F32)
+            d_gate_ref[part, :] = (
+                d_active * upper * (sigmoid + silu * (1.0 - sigmoid))
+            ).astype(BF16)
+            d_upper_ref[part, :] = (d_active * silu).astype(BF16)
+
+    out = jax.ShapeDtypeStruct((rows, cols), BF16)
+    block = by_columns(rows, tile)
+    return call(
+        body,
+        cols // tile,
+        [held(d_down), by_rows(tile, depth), block, block],
+        [(out, block), (out, block)],
+        (d_down, weight, gate, upper),
+        2 * rows * depth * cols,
+    )
+
+
+def by_stream(tile, cols, steps):
+    return [
+        pl.BlockSpec((tile, cols), lambda i: (jnp.minimum(i, steps - 1), 0)),
+        pl.BlockSpec((tile, cols), lambda i: (jnp.maximum(i - steps, 0), 0)),
+    ]
+
+
+def rows_kernel(product, lefts, rights, types):
+    rows, depth = lefts[0].shape
+    cols = rights[0].shape[1] if product is times else rights[0].shape[0]
+    tile = column_tile(rows // 2)
+    steps = rows // 2 // tile
+    count = len(lefts)
+
+    def body(*refs):
+        total = product(refs[0][...], refs[count][...])
+        for k in range(1, count):
+            total += product(refs[k][...], refs[count + k][...])
+
+        @pl.when(pl.program_id(0) < steps)
+        def _():
+            refs[-2][...] = total.astype(types[0])
+
+        @pl.when(pl.program_id(0) >= steps)
+        def _():
+            refs[-1][...] = total.astype(types[1])
+
+    shapes = [jax.ShapeDtypeStruct((rows // 2, cols), kind) for kind in types]
+    return call(
+        body,
+        2 * steps,
+        [by_rows(tile, depth)] * count + [held(right) for right in rights],
+        list(zip(shapes, by_stream(tile, cols, steps))),
+        (*lefts, *rights),
+        2 * count * rows * depth * cols,
+    )
+
+
+def row_kernel(left, right, product):
+    rows, depth = left.shape
+    cols = right.shape[1] if product is times else right.shape[0]
+    tile = column_tile(rows)
+
+    def body(left_ref, right_ref, out_ref):
+        out_ref[...] = product(left_ref[...], right_ref[...])
+
+    out = jax.ShapeDtypeStruct((rows, cols), F32)
+    return call(
+        body,
+        rows // tile,
+        [by_rows(tile, depth), held(right)],
+        [(out, by_rows(tile, cols))],
+        (left, right),
+        16 * rows * depth * cols,
+    )[0]
+
+
+def weight_kernel(left, right):
+    depth, rows = left.shape
+    cols = right.shape[1]
+    tile = column_tile(cols)
+
+    def body(left_ref, right_ref, out_ref):
+        out_ref[...] = inner_rows(left_ref[...], right_ref[...]).astype(BF16)
+
+    out = jax.ShapeDtypeStruct((rows, cols), BF16)
+    return call(
+        body,
+        cols // tile,
+        [held(left), by_columns(depth, tile)],
+        [(out, by_columns(rows, tile))],
+        (left, right),
+        2 * rows * depth * cols,
+    )[0]
+
+
+def weight_rows_kernel(left, right):
+    depth, rows = left.shape
+    cols = right.shape[1]
+    tile = column_tile(rows)
+
+    def body(left_ref, right_ref, out_ref):
+        out_ref[...] = inner_rows(left_ref[...], right_ref[...]).astype(BF16)
+
+    out = jax.ShapeDtypeStruct((rows, cols), BF16)
+    return call(
+        body,
+        rows // tile,
+        [by_columns(depth, tile), held(right)],
+        [(out, by_rows(tile, cols))],
+        (left, right),
+        2 * rows * depth * cols,
+    )[0]
 
 
 def local(
@@ -148,24 +410,52 @@
     in_high = jnp.concatenate([in_split[:, :, 1].reshape(part, 3 * half), tiny], axis=1)
     in_pair = jnp.concatenate(trade(in_low, in_high), axis=0)
     out_fold = jnp.concatenate([out_weight[:, :half], out_weight[:, half:]], axis=0)
-    front = gather_chips(jnp.concatenate([in_pair, out_fold], axis=1))
+    front = jnp.concatenate([in_pair, out_fold], axis=1)
 
     wide = jnp.concatenate([gate_weight, up_weight], axis=1)
     wide = wide.reshape(part, 2 * chips, 2, ff_block)
     wide_low = wide[:, :, 0].reshape(part, 2 * ff_half)
     wide_high = wide[:, :, 1].reshape(part, 2 * ff_half)
     wide_pair = jnp.concatenate(trade(wide_low, wide_high), axis=0)
-    weight_gate = gather_chips(wide_pair[:, :ff_half]).reshape(width, ff_half)
-    weight_up = gather_chips(wide_pair[:, ff_half:]).reshape(width, ff_half)
-    weight_down = gather_chips(down_weight).reshape(ff_half, width)
-    cotangent_other = swap_cores(cotangent[0])
-
-    weight_in = front[:, :, : 3 * half].reshape(width, 3 * half)
-    small = front[:, :, 3 * half : 3 * half + LANES].reshape(width, LANES)
+    in_wide = 3 * half
+    picks = (
+        lambda block: block[..., :in_wide],
+        lambda block: block[..., in_wide : in_wide + LANES],
+        lambda block: block[..., in_wide + LANES :],
+    )
+    line_front = line_gather(front)
+    if chips == 16:
+        plane_down = Plane(after(down_weight, front)[None, None])
+        plane_down.corners()
+        line_front, down_low, down_high = lax.optimization_barrier(
+            (line_front, plane_down.low, plane_down.high)
+        )
+        plane_down.low, plane_down.high = down_low, down_high
+    line_gate = line_gather(wide_pair[:, :ff_half])
+    line_up = line_gather(wide_pair[:, ff_half:])
+    if chips == 16:
+        down_plane = plane_down.place().reshape(4 * ff_block, width)
+    else:
+        down_plane = down_weight
+    weight_down = line_gather(after(down_plane, line_gate)).reshape(ff_half, width)
+    plane_front = Plane(line_front)
+    front_x, front_y, line_gate = lax.optimization_barrier(
+        (plane_front.from_x, plane_front.from_y, line_gate)
+    )
+    plane_front.from_x, plane_front.from_y = front_x, front_y
+    plane_front.corners()
+    plane_gate = Plane(line_gate)
+    low, high = lax.optimization_barrier((plane_front.low, plane_front.high))
+    plane_front.low, plane_front.high = low, high
+    fronts = [plane_front.place(pick) for pick in picks]
+    cotangent_other = swap_cores(after(cotangent[0], tokens_other))
+
+    weight_in = fronts[0].reshape(width, in_wide)
+    small = fronts[1].reshape(width, LANES)
     small = small[:, :8].astype(F32).T
     gain_first, gain_second = small[0], small[1]
     taps = lax.dynamic_slice(small[2:5], (0, core * half), (3, half))
-    out_mine = front[:, :, 3 * half + LANES :]
+    out_mine = fronts[2].reshape(chips, pair, half)
     out_even, out_odd = ordered(out_mine, swap_cores(out_mine))
     weight_out = jnp.stack(
         [
@@ -180,7 +470,13 @@
     keep_state = 1.0 - jnp.stack([span_flags[0, 0].astype(F32), flag_other[0, 0]])
     keep_state = keep_state[:, None, None]
     hidden = (inputs * rms_scale(inputs) * gain_first).astype(BF16)
-    projected = times(hidden, weight_in)
+    gate_x, gate_y, line_up, hidden = lax.optimization_barrier(
+        (plane_gate.from_x, plane_gate.from_y, line_up, hidden)
+    )
+    plane_gate.from_x, plane_gate.from_y = gate_x, gate_y
+    plane_gate.corners()
+    plane_up = Plane(line_up)
+    projected = row_kernel(hidden, weight_in, times)
     b_part = projected[:, :half]
     c_part = projected[:, half : 2 * half]
     v_part = projected[:, 2 * half :]
@@ -203,29 +499,31 @@
     hidden2_own = (normed_two * gain_second).astype(BF16)
     hidden2 = jnp.concatenate([hidden2_own, swap_cores(hidden2_own)], axis=0)
 
-    gate_proj = times(hidden2, weight_gate)
-    up_proj = times(hidden2, weight_up)
-    sigmoid_gate = jax.nn.sigmoid(gate_proj)
-    silu_gate = gate_proj * sigmoid_gate
-    active = (silu_gate * up_proj).astype(BF16)
-    result = times(active, weight_down)
-    result = resid + result[:rows] + swap_cores(result[rows:].astype(BF16)).astype(F32)
-    output = result.astype(BF16)[None]
+    weight_gate = plane_gate.place().reshape(width, ff_half)
+    up_x, up_y, hidden2 = lax.optimization_barrier((plane_up.from_x, plane_up.from_y, hidden2))
+    plane_up.from_x, plane_up.from_y = up_x, up_y
+    gate_proj = gate_kernel(hidden2, weight_gate)
+    plane_up.corners()
+    weight_up = plane_up.place().reshape(width, ff_half)
+    active, up_proj = active_kernel(hidden2, weight_up, gate_proj)
 
     d_down = jnp.concatenate([cotangent[0], cotangent_other], axis=0)
-    grad_down = inner_rows(active, d_down).astype(BF16)
-    shard_down = scatter_chips(grad_down.reshape(chips, ff_block, width))
-    d_active = times_transposed(d_down, weight_down)
-    d_gate = (
-        d_active * up_proj * sigmoid_gate * (1.0 + gate_proj * (1.0 - sigmoid_gate))
-    ).astype(BF16)
-    d_upper = (d_active * silu_gate).astype(BF16)
-    d_hidden2 = times_transposed(d_gate, weight_gate) + times_transposed(d_upper, weight_up)
-    d_hidden2 = d_hidden2[:rows] + swap_cores(d_hidden2[rows:])
-    grad_gate = inner_rows(hidden2, d_gate).astype(BF16)
-    shard_gate = scatter_chips(grad_gate.reshape(chips, pair, ff_half))
-    grad_up = inner_rows(hidden2, d_upper).astype(BF16)
-    shard_up = scatter_chips(grad_up.reshape(chips, pair, ff_half))
+    grad_down = weight_rows_kernel(active, d_down)
+    scatter_down = Scatter(grad_down.reshape(chips, ff_block, width))
+    d_down = scatter_down.opened(d_down)
+    d_gate, d_upper = split_kernel(d_down, weight_down, gate_proj, up_proj)
+    d_gate = scatter_down.turned(d_gate)
+    grad_gate = weight_kernel(hidden2, d_gate)
+    scatter_gate = Scatter(grad_gate.reshape(chips, pair, ff_half))
+    d_gate = scatter_gate.opened(d_gate)
+    d_hidden2, d_hidden2_give = rows_kernel(
+        times_transposed, (d_gate, d_upper), (weight_gate, weight_up), (F32, F32)
+    )
+    d_upper, d_hidden2_give = lax.optimization_barrier((d_upper, d_hidden2_give))
+    d_hidden2_got = swap_cores(d_hidden2_give)
+    d_upper = scatter_down.landed(d_upper)
+    grad_up = scatter_gate.turned(weight_kernel(hidden2, d_upper))
+    d_hidden2 = d_hidden2 + after(d_hidden2_got, grad_up)
 
     grad_gain_two = jnp.sum(d_hidden2 * normed_two, axis=0)
     d_normed_two = d_hidden2 * gain_second
@@ -243,6 +541,11 @@
     grad_out = (out_keep + swap_cores(out_give).astype(F32)).astype(BF16)
     grad_out = jnp.concatenate([grad_out[:, :, :half], grad_out[:, :, half:]], axis=1)
 
+    scatter_up = Scatter(
+        jnp.concatenate([grad_up.reshape(chips, pair, ff_half), grad_out], axis=2)
+    )
+    d_mixed = scatter_up.opened(d_mixed)
+
     d_c_part = d_mixed * conv_out
     d_conv = (d_mixed * c_part).reshape(2, rows, half)
     grad_taps = jnp.stack(
@@ -263,6 +566,7 @@
         * keep_state
     )
     from_next = shift(d_state, -1)
+    d_conv = scatter_up.turned(scatter_gate.landed(d_conv))
     following = jnp.pad(d_conv, ((0, 0), (0, 2), (0, 0)))
     d_gated = (
         taps[2] * following[:, :-2] + taps[1] * following[:, 1:-1] + taps[0] * following[:, 2:]
@@ -271,9 +575,12 @@
     d_projected = jnp.concatenate(
         [d_gated * v_part, d_c_part, d_gated * b_part], axis=1
     ).astype(BF16)
-    d_hidden = times_transposed(d_projected, weight_in)
-    d_hidden = d_hidden[:rows] + swap_cores(d_hidden[rows:])
-    grad_in = inner_rows(hidden, d_projected).astype(BF16)
+    d_hidden, d_hidden_give = rows_kernel(
+        times_transposed, (d_projected,), (weight_in,), (F32, F32)
+    )
+    d_projected = after(d_projected, d_hidden_give)
+    grad_in = scatter_up.landed(weight_kernel(hidden, d_projected))
+    d_hidden = d_hidden + after(swap_cores(d_hidden_give), grad_in)
 
     scale_one = rms_scale(own_inputs)
     normed_one = own_inputs * scale_one
@@ -289,16 +596,25 @@
     )
     small_grads = jnp.concatenate([grad_gain_one[None], grad_gain_two[None], taps_wide], axis=0)
     small_grads = jnp.pad(small_grads.T, ((0, 0), (0, LANES - small_grads.shape[0])))
-    shard_front = scatter_chips(
-        jnp.concatenate(
-            [
-                grad_in.reshape(chips, pair, 3 * half),
-                small_grads.astype(BF16).reshape(chips, pair, LANES),
-                grad_out,
-            ],
-            axis=2,
-        )
-    )
+    front_terms = jnp.concatenate(
+        [
+            grad_in.reshape(chips, pair, in_wide),
+            small_grads.astype(BF16).reshape(chips, pair, LANES),
+        ],
+        axis=2,
+    )
+    scatter_front = Scatter(front_terms)
+
+    result, result_give = rows_kernel(
+        times, (scatter_front.opened(active),), (weight_down,), (F32, BF16)
+    )
+    result_give = scatter_front.turned(result_give)
+    result = resid + result + swap_cores(result_give).astype(F32)
+    output = scatter_front.landed(result.astype(BF16)[None])
+    shard_down, shard_gate, shard_up, output = lax.optimization_barrier(
+        (scatter_down.shard, scatter_gate.shard, scatter_up.shard, output)
+    )
+    shard_front = scatter_front.shard
 
     def rejoin(shard):
         keep = jnp.where(first, shard[:part], shard[part:])
@@ -314,7 +630,7 @@
     )
     tail = keep[:, 3 * half :].astype(F32) + got[:, 3 * half :].astype(F32)
     tail = tail[:, :8].T
-    out_pieces = shard_front[:, 3 * half + LANES :]
+    out_pieces = shard_up[:, ff_half:]
     shard_out = jnp.concatenate([out_pieces[:part], out_pieces[part:]], axis=1).astype(F32)
 
     def interleave(shard):
@@ -336,7 +652,7 @@
         shard_out,
         tail[1],
         interleave(shard_gate),
-        interleave(shard_up),
+        interleave(shard_up[:, :ff_half]),
         shard_down.astype(F32),
     )
 

time: 590 us -> 530 us (0.90)
  matrix products: 147 us -> 5.65 us
  Pallas kernels: 0 us -> 136 us
  waiting for transfers between devices: 198 us -> 133 us
  other arithmetic: 79 us -> 93.2 us
    pallas_call x0 -> x11, Pallas kernels: none -> 136 us  [call(): pl.pallas_call(body, grid=(grid,), in_specs=ins, out_specs=[spec for _, s...]
    all_gather x4, waiting for transfers between devices: 92.6 us -> 29.4 us  [line_gather(): lax.all_gather(shard, 'seq', axis_index_groups=columns_of_line(peers), ax...]
    dot_general x5 -> x1, matrix products: 60 us -> 1.96 us  [times(): return jnp.dot(left, right, preferred_element_type=F32)]
    dot_general x5 -> x1, matrix products: 45.6 us -> 1.86 us  [times_transposed(): lax.dot_general(left, right, (((1,), (1,)), ((), ())), preferred_element_...]
    dot_general x5 -> x1, matrix products: 41.1 us -> 1.84 us  [inner_rows(): lax.dot_general(left, right, (((0,), (0,)), ((), ())), preferred_element_...]
    ppermute x32, waiting for transfers between devices: 74.4 us -> 92.1 us  [across(): return lax.ppermute(x, 'seq', [(i, i ^ bit) for i in range(peers)])]
    reduce_scatter x4, waiting for transfers between devices: 26.5 us -> 9.12 us  [landed(): lax.psum_scatter(mine.reshape(self.depth * self.rows, self.cols), 'seq',...]
    slice x14 -> x8, local copies, waits for them, and re-layouts: 20.5 us -> 5.4 us  [the longest x3 2.24 us: corners(): self.low = across(self.from_x[:half], 2)]
  transfers between devices with their start and end apart: 58 -> 58, of which waited for: 18 -> 15; matrix products, arithmetic and copies ran while one was open for 41% -> 28% of each run, Pallas kernels for 0% -> 26%
where the time goes in v2:
time: 530 us; the launch traced here: 520 us
  Pallas kernels  136 us (26%)
  waiting for transfers between devices  133 us (25%)
  other arithmetic  93.2 us (18%)
  local copies, waits for them, and re-layouts  84.2 us (16%)
  starting transfers between devices  51.7 us (10%)
  between operations  16.6 us (3%)
  matrix products  5.65 us (1%)
    pallas_call x11, Pallas kernels, call(): pl.pallas_call(body, grid=(grid,), in_specs=ins, out_specs=[spec for _, s...  136 us
    ppermute x32, waiting for transfers between devices, across(): return lax.ppermute(x, 'seq', [(i, i ^ bit) for i in range(peers)])  92.1 us
    all_gather x4, waiting for transfers between devices, line_gather(): lax.all_gather(shard, 'seq', axis_index_groups=columns_of_line(peers), ax...  29.4 us
    ppermute x32, starting transfers between devices, across(): return lax.ppermute(x, 'seq', [(i, i ^ bit) for i in range(peers)])  28.3 us
    unnamed x124, local copies, waits for them, and re-layouts  20.7 us
    ppermute x16, starting transfers between devices, swap_cores(): return lax.ppermute(x, 'fsdp', [(0, 1), (1, 0)])  19.2 us
  transfers between devices with their start and end apart: 58, of which 15 were waited for; matrix products, arithmetic and copies ran while one was open for 28% of the time, Pallas kernels for 26%

profile of v2, /device:TPU:1, one launch (start us, length us, event | category | flops | bytes accessed | tf_op | source)
XLA Modules:
  0.0 520.3 jit_solution(12332880586456843407)
XLA Ops:
  12.0 1.8 reshape.173
  13.8 2.3 fusion.58
  22.0 2.2 collective-permute-done.16
  24.6 2.3 collective-permute-start.1
  31.9 2.4 collective-permute-done.1
  40.3 1.8 collective-permute-start.24
  42.8 7.2 %all-gather.5.cloned.1.call-done = bf16[256,2176]{1,0:T(8,128)(2,1)} async-done(((bf16[64,2176]{1,0:T(8,128)(2,1)}), bf16[256,2176]{1,0:T(8,128)(2,1)}) %all-gather.5.cloned.1.call-update) | async-done | bytes 1114128 | tf_op jit(solution)/shard_map/all_gather | solution.py:43
  59.6 22.2 %all-gather.7.cloned.1.call-done = bf16[256,2304]{1,0:T(8,128)(2,1)} async-done(((bf16[64,2304]{1,0:T(8,128)(2,1)}), bf16[256,2304]{1,0:T(8,128)(2,1)}) %all-gather.7.cloned.1.call-update) | async-done | bytes 1179664 | tf_op jit(solution)/shard_map/all_gather | solution.py:43
  94.2 3.0 broadcast.83.clone
  99.1 2.2 pad_maximum_fusion.4.right_ref.d_down_ref
  101.4 20.1 %collective-permute-done.11 = bf16[2,1,64,2176]{3,2,0,1:T(8,128)(2,1)S(1)} collective-permute-done((bf16[2,1,64,2176]{3,2,0,1:T(8,128)(2,1)S(1)}, bf16[2,1,64,2176]{3,2,0,1:T(8,128)(2,1)S(1)}, u32[]{:S(2)}, u32[]{:S(2)}) %collective-permute-start.11) | collective-permute-done | bytes 557088 | tf_op jit(solution)/shard_map/ppermute | solution.py:20
  122.8 2.4 collective-permute-start.18
  128.4 3.3 fusion.2.left_ref
  131.7 1.9 copy-done.13
  133.6 1.9 copy-done.15
  135.5 7.4 %shard_map.186 = f32[1536,1536]{1,0:T(8,128)} custom-call(bf16[1536,1024]{1,0:T(8,128)(2,1)S(1)} %copy-done.15, bf16[1024,1536]{1,0:T(8,128)(2,1)S(1)} %bitcast.184), custom_call_target="tpu_custom_call" | custom-call | flops 38654705664 | bytes 77309408 | tf_op jit(solution)/shard_map/pallas_call | solution.py:171
  142.9 3.5 multiply_convert_fusion.1
  146.5 2.2 collective-permute-start.15
  149.2 2.1 collective-permute-start.13
  154.5 3.5 fusion.16
  163.2 2.0 multiply_reduce_fusion.5
  165.7 3.1 constant_dynamic-update-slice_fusion.8
  171.9 2.4 constant_dynamic-update-slice_fusion.7
  174.4 16.6 %collective-permute-done.22 = bf16[2,1,64,2304]{3,2,1,0:T(8,128)(2,1)S(1)} collective-permute-done((bf16[2,1,64,2304]{3,2,1,0:T(8,128)(2,1)S(1)}, bf16[2,1,64,2304]{3,2,1,0:T(8,128)(2,1)S(1)}, u32[]{:S(2)}, u32[]{:S(2)}) %collective-permute-start.22) | collective-permute-done | bytes 589856 | tf_op jit(solution)/shard_map/ppermute | solution.py:20
  194.9 12.6 %shard_map.187.gate_ref = bf16[1536,2304]{1,0:T(8,128)(2,1)} custom-call(bf16[1536,1024]{1,0:T(8,128)(2,1)S(1)} %pad_maximum_fusion.3.hidden_ref.left_ref, bf16[1024,2304]{1,0:T(8,128)(2,1)} %bitcast.43.weight_ref.refs_2_), custom_call_target="tpu_custom_call" | custom-call | flops 7247757312 | bytes 14495514 | tf_op jit(solution)/shard_map/pallas_call | solution.py:171
  207.9 15.2 %shard_map.188 = (bf16[1536,2304]{1,0:T(8,128)(2,1)}, bf16[1536,2304]{1,0:T(8,128)(2,1)}) custom-call(bf16[1536,1024]{1,0:T(8,128)(2,1)S(1)} %pad_maximum_fusion.3.hidden_ref.left_ref, bf16[1024,2304]{1,0:T(8,128)(2,1)S(1)} %bitcast.182, bf16[1536,2304]{1,0:T(8,128)(2,1)} %shard_map.187.gate_ref), custom_call_target="tpu_custom_call" | custom-call | flops 7247757312 | bytes 14495514 | tf_op jit(solution)/shard_map/pallas_call | solution.py:171
  223.1 10.8 %shard_map.189 = bf16[2304,1024]{1,0:T(8,128)(2,1)S(1)} custom-call(bf16[1536,2304]{1,0:T(8,128)(2,1)} %get-tuple-element.178.left_ref.refs_0_, bf16[1536,1024]{1,0:T(8,128)(2,1)S(1)} %pad_maximum_fusion.4.right_ref.d_down_ref), custom_call_target="tpu_custom_call" | custom-call | flops 7247757312 | bytes 14495514 | tf_op jit(solution)/shard_map/pallas_call | solution.py:171
  233.9 2.1 copy-done.4
  237.5 1.9 copy-done.8
  239.4 2.3 copy-done.17
  241.8 17.6 %shard_map.190 = (bf16[1536,2304]{1,0:T(8,128)(2,1)}, bf16[1536,2304]{1,0:T(8,128)(2,1)}) custom-call(bf16[1536,1024]{1,0:T(8,128)(2,1)S(1)} %copy-done.8, bf16[2304,1024]{1,0:T(8,128)(2,1)S(1)} %copy-done.17, bf16[1536,2304]{1,0:T(8,128)(2,1)} %shard_map.187.gate_ref, bf16[1536,2304]{1,0:T(8,128)(2,1)} %get-tuple-element.125.upper_ref), custom_call_target="tpu_custom_call" | custom-call | flops 7247757312 | bytes 14495514 | tf_op jit(solution)/shard_map/pallas_call | solution.py:171
  263.4 11.2 %shard_map.191 = bf16[1024,2304]{1,0:T(8,128)(2,1)S(1)} custom-call(bf16[1536,1024]{1,0:T(8,128)(2,1)S(1)} %copy-done.10, bf16[1536,2304]{1,0:T(8,128)(2,1)} %get-tuple-element.134.right_ref.refs_0_), custom_call_target="tpu_custom_call" | custom-call | flops 7247757312 | bytes 14495514 | tf_op jit(solution)/shard_map/pallas_call | solution.py:171
  275.8 22.5 %shard_map.192 = (f32[768,1024]{1,0:T(8,128)S(1)}, f32[768,1024]{1,0:T(8,128)}) custom-call(bf16[1536,2304]{1,0:T(8,128)(2,1)} %get-tuple-element.134.right_ref.refs_0_, bf16[1536,2304]{1,0:T(8,128)(2,1)} %get-tuple-element.143.refs_1_.right_ref, bf16[1024,2304]{1,0:T(8,128)(2,1)} %bitcast.43.weight_ref.refs_2_, bf16[1024,2304]{1,0:T(8,128)(2,1)} %bitcast.183), custom_call_target="tpu_custom_call" | custom-call | flops 14495514624 | bytes 28991028 | tf_op jit(solution)/shard_map/pallas_call | solution.py:171
  298.2 3.5 collective-permute-start.33
  302.6 3.0 add_convert_fusion.3
  305.7 11.4 %shard_map.193 = bf16[1024,2304]{1,0:T(8,128)(2,1)S(1)} custom-call(bf16[1536,1024]{1,0:T(8,128)(2,1)S(1)} %copy-done.11, bf16[1536,2304]{1,0:T(8,128)(2,1)} %get-tuple-element.143.refs_1_.right_ref), custom_call_target="tpu_custom_call" | custom-call | flops 7247757312 | bytes 14495514 | tf_op jit(solution)/shard_map/pallas_call | solution.py:171
  322.4 2.4 multiply_add_fusion
  324.9 1.8 fusion.24
  329.8 1.9 fusion.27
  331.7 2.1 slice_select_fusion.1
  336.7 3.0 fusion.20
  340.0 2.8 fusion.32
  342.8 3.4 pad_maximum_fusion.5
  346.2 7.2 %multiply_reduce_fusion = (f32[512]{0:T(512)S(1)}, f32[1536,512]{1,0:T(8,128)}, bf16[1536,512]{1,0:T(8,128)(2,1)}) fusion(f32[1536,512]{1,0:T(8,128)} %pad_maximum_fusion.5, f32[1536,1536]{1,0:T(8,128)S(1)} %bitcast.187, f32[2,768,512]{2,1,0:T(8,128)} %copy-done.29), kind=kLoop, calls=%fused_computation.57 | loop fusion | flops 6290944 | bytes 20449280 | tf_op jit(solution)/shard_map/reduce_sum | solution.py:555
  353.5 9.7 %collective-permute-done.31 = bf16[4,1,64,2304]{3,2,1,0:T(8,128)(2,1)} collective-permute-done((bf16[4,1,64,2304]{3,2,1,0:T(8,128)(2,1)}, bf16[4,1,64,2304]{3,2,1,0:T(8,128)(2,1)}, u32[]{:S(2)}, u32[]{:S(2)}) %collective-permute-start.31) | collective-permute-done | bytes 1179680 | tf_op jit(solution)/shard_map/ppermute | solution.py:20
  364.8 3.4 add_convert_fusion.2
  369.9 10.7 %collective-permute-done.36 = bf16[2,1,64,2816]{3,2,1,0:T(8,128)(2,1)S(1)} collective-permute-done((bf16[2,1,64,2816]{3,2,1,0:T(8,128)(2,1)}, bf16[2,1,64,2816]{3,2,1,0:T(8,128)(2,1)S(1)}, u32[]{:S(2)}, u32[]{:S(2)}) %collective-permute-start.36) | collective-permute-done | bytes 720928 | tf_op jit(solution)/shard_map/ppermute | solution.py:20
  385.8 2.6 pad_maximum_fusion.refs_0_.right_ref
  389.4 9.2 %shard_map.194 = (f32[768,1024]{1,0:T(8,128)S(1)}, f32[768,1024]{1,0:T(8,128)}) custom-call(bf16[1536,1536]{1,0:T(8,128)(2,1)} %pad_maximum_fusion.refs_0_.right_ref, bf16[1024,1536]{1,0:T(8,128)(2,1)S(1)} %bitcast.185), custom_call_target="tpu_custom_call" | custom-call | flops 4831838208 | bytes 9663676 | tf_op jit(solution)/shard_map/pallas_call | solution.py:171
  400.4 2.3 collective-permute-start.41
  404.9 4.6 multiply_reduce_fusion.2
  409.8 8.0 %shard_map.195 = bf16[1024,1536]{1,0:T(8,128)(2,1)S(1)} custom-call(bf16[1536,1024]{1,0:T(8,128)(2,1)S(1)} %copy-done.16, bf16[1536,1536]{1,0:T(8,128)(2,1)} %pad_maximum_fusion.refs_0_.right_ref), custom_call_target="tpu_custom_call" | custom-call | flops 4831838208 | bytes 9663676 | tf_op jit(solution)/shard_map/pallas_call | solution.py:171
  417.8 18.4 %collective-permute-done.38 = bf16[4,1,64,2816]{3,2,1,0:T(8,128)(2,1)S(1)} collective-permute-done((bf16[4,1,64,2816]{3,2,1,0:T(8,128)(2,1)}, bf16[4,1,64,2816]{3,2,1,0:T(8,128)(2,1)S(1)}, u32[]{:S(2)}, u32[]{:S(2)}) %collective-permute-start.38) | collective-permute-done | bytes 1441824 | tf_op jit(solution)/shard_map/ppermute | solution.py:20
  438.8 4.4 fusion.8
  444.6 2.3 copy-done.18
  446.9 10.1 %shard_map.196 = (f32[768,1024]{1,0:T(8,128)S(1)}, bf16[768,1024]{1,0:T(8,128)(2,1)S(1)}) custom-call(bf16[1536,2304]{1,0:T(8,128)(2,1)} %get-tuple-element.178.left_ref.refs_0_, bf16[2304,1024]{1,0:T(8,128)(2,1)S(1)} %copy-done.18), custom_call_target="tpu_custom_call" | custom-call | flops 7247757312 | bytes 14495514 | tf_op jit(solution)/shard_map/pallas_call | solution.py:171
  457.5 1.7 collective-permute-start.46
  461.3 4.4 fusion.12
  465.7 2.1 fusion.21
  467.8 11.9 %collective-permute-done.44 = bf16[4,1,64,1664]{3,2,0,1:T(8,128)(2,1)S(1)} collective-permute-done((bf16[4,1,64,1664]{3,2,0,1:T(8,128)(2,1)S(1)}, bf16[4,1,64,1664]{3,2,0,1:T(8,128)(2,1)S(1)}, u32[]{:S(2)}, u32[]{:S(2)}) %collective-permute-start.44) | collective-permute-done | bytes 852000 | tf_op jit(solution)/shard_map/ppermute | solution.py:20
  485.9 1.8 convert_element_type.188
  491.3 2.1 reshape.193
  495.1 9.1 %reduce-scatter.11.cloned.1.call-done = bf16[64,1664]{1,0:T(8,128)(2,1)} async-done(((bf16[256,1664]{1,0:T(8,128)(2,1)}), bf16[64,1664]{1,0:T(8,128)(2,1)}) %reduce-scatter.11.cloned.1.call-update) | async-done | bytes 213008 | tf_op jit(solution)/shard_map/reduce_scatter | solution.py:135
  507.8 2.1 reshape.194
  (363 shorter events, 124.3 us)
Async XLA Ops:
  7.2 42.8 %all-gather.5.cloned.1.call-start = ((), (), s32[]{:S(2)}) async-start(), calls=%async_computation.4 | async-start | bytes 1392640 | tf_op jit(solution)/shard_map/all_gather | solution.py:43
  10.8 7.3 %collective-permute-start = (bf16[32,1664]{1,0:T(8,128)(2,1)}, bf16[32,1664]{1,0:T(8,128)(2,1)S(1)}, u32[]{:S(2)}, u32[]{:S(2)}) collective-permute-start(bf16[32,1664]{1,0:T(8,128)(2,1)} %broadcast_select_fusion.20), channel_id=1, source_target_pairs={{0,1},{1,0},{2,3},{3,2},{4,5},{5,4},{6,7},{7,6},{8,9},{9,8},{10,11... | collective-permute-start | bytes 319496 | tf_op jit(solution)/shard_map/ppermute | solution.py:15
  16.8 2.8 collective-permute-start.7
  19.0 62.8 %all-gather.7.cloned.1.call-start = ((), (), s32[]{:S(2)}) async-start(), calls=%async_computation.5 | async-start | bytes 1474560 | tf_op jit(solution)/shard_map/all_gather | solution.py:43
  20.6 111.1 %all-gather.9.cloned.1.call-start = ((), (), s32[]{:S(2)}) async-start(), calls=%async_computation.6 | async-start | bytes 1474560 | tf_op jit(solution)/shard_map/all_gather | solution.py:43
  20.7 19.7 %collective-permute-start.10 = (bf16[768,1024]{1,0:T(8,128)(2,1)S(1)}, bf16[768,1024]{1,0:T(8,128)(2,1)S(1)}, u32[]{:S(2)}, u32[]{:S(2)}) collective-permute-start(bf16[768,1024]{1,0:T(8,128)(2,1)S(1)} %bitcast.188), channel_id=1, source_target_pairs={{0,1},{1,0},{2,3},{3,2},{4,5},{5,4},{6,7},{7,6},{8,9},{9,8},{10,11... | collective-permute-start | bytes 4718600 | tf_op jit(solution)/shard_map/ppermute | solution.py:15
  21.4 2.7 collective-permute-start.16
  24.6 9.7 %collective-permute-start.1 = (bf16[1,1,144,1024]{3,2,1,0:T(8,128)(2,1)}, bf16[1,1,144,1024]{3,2,1,0:T(8,128)(2,1)}, u32[]{:S(2)}, u32[]{:S(2)}) collective-permute-start(bf16[1,1,144,1024]{3,2,1,0:T(8,128)(2,1)} %bitcast.4), channel_id=1, source_target_pairs={{0,2},{2,0},{4,6},{6,4},{8,10},{10,8},{12,14},{14,12},{16,18},{18,... | collective-permute-start | bytes 884744 | tf_op jit(solution)/shard_map/ppermute | solution.py:20
  27.0 9.6 %collective-permute-start.3 = (bf16[1,1,144,1024]{3,2,1,0:T(8,128)(2,1)}, bf16[1,1,144,1024]{3,2,1,0:T(8,128)(2,1)S(1)}, u32[]{:S(2)}, u32[]{:S(2)}) collective-permute-start(bf16[1,1,144,1024]{3,2,1,0:T(8,128)(2,1)} %bitcast.4), channel_id=1, source_target_pairs={{0,4},{2,6},{4,0},{6,2},{8,12},{10,14},{12,8},{14,10},{16,20},{18,... | collective-permute-start | bytes 884744 | tf_op jit(solution)/shard_map/ppermute | solution.py:20
  31.9 205.6 %all-gather.11.cloned.1.call-start = ((), (), s32[]{:S(2)}) async-start(), calls=%async_computation.7 | async-start | bytes 5898240 | tf_op jit(solution)/shard_map/all_gather | solution.py:43
  35.3 7.5 %collective-permute-start.2 = (bf16[1,1,64,1024]{3,2,1,0:T(8,128)(2,1)S(1)}, bf16[1,1,64,1024]{3,2,1,0:T(8,128)(2,1)}, u32[]{:S(2)}, u32[]{:S(2)}) collective-permute-start(bf16[1,1,64,1024]{3,2,1,0:T(8,128)(2,1)S(1)} %slice.336), channel_id=1, source_target_pairs={{0,4},{2,6},{4,0},{6,2},{8,12},{10,14},{12,8},{14,10},{16,20},{18,... | collective-permute-start | bytes 393224 | tf_op jit(solution)/shard_map/ppermute | solution.py:20
  36.6 6.2 %collective-permute-start.4 = (bf16[1,1,80,1024]{3,2,1,0:T(8,128)(2,1)S(1)}, bf16[1,1,80,1024]{3,2,1,0:T(8,128)(2,1)}, u32[]{:S(2)}, u32[]{:S(2)}) collective-permute-start(bf16[1,1,80,1024]{3,2,1,0:T(8,128)(2,1)S(1)} %slice.337), channel_id=1, source_target_pairs={{0,2},{2,0},{4,6},{6,4},{8,10},{10,8},{12,14},{14,12},{16,18},{18,... | collective-permute-start | bytes 491528 | tf_op jit(solution)/shard_map/ppermute | solution.py:20
  40.3 58.8 %collective-permute-start.24 = (bf16[768,1024]{1,0:T(8,128)(2,1)}, bf16[768,1024]{1,0:T(8,128)(2,1)}, u32[]{:S(2)}, u32[]{:S(2)}) collective-permute-start(bf16[768,1024]{1,0:T(8,128)(2,1)} %bitcast.44), channel_id=1, source_target_pairs={{0,1},{1,0},{2,3},{3,2},{4,5},{5,4},{6,7},{7,6},{8,9},{9,8},{10,11... | collective-permute-start | bytes 4718600 | tf_op jit(solution)/shard_map/ppermute | solution.py:15
  50.0 32.1 %collective-permute-start.5 = (bf16[4,1,64,2176]{3,2,0,1:T(8,128)(2,1)}, bf16[4,1,64,2176]{3,2,0,1:T(8,128)(2,1)}, u32[]{:S(2)}, u32[]{:S(2)}) collective-permute-start(bf16[4,1,64,2176]{3,2,0,1:T(8,128)(2,1)} %bitcast.216), channel_id=1, source_target_pairs={{0,2},{2,0},{4,6},{6,4},{8,10},{10,8},{12,14},{14,12},{16,18},{18,... | collective-permute-start | bytes 3342344 | tf_op jit(solution)/shard_map/ppermute | solution.py:20
  51.2 30.9 %collective-permute-start.6 = (bf16[4,1,64,2176]{3,2,0,1:T(8,128)(2,1)}, bf16[4,1,64,2176]{3,2,0,1:T(8,128)(2,1)}, u32[]{:S(2)}, u32[]{:S(2)}) collective-permute-start(bf16[4,1,64,2176]{3,2,0,1:T(8,128)(2,1)} %bitcast.217), channel_id=1, source_target_pairs={{0,4},{2,6},{4,0},{6,2},{8,12},{10,14},{12,8},{14,10},{16,20},{18,... | collective-permute-start | bytes 3342344 | tf_op jit(solution)/shard_map/ppermute | solution.py:20
  81.8 399.9 %reduce-scatter.5.cloned.1.call-start = ((), (), s32[]{:S(2)}) async-start(), calls=%async_computation.8 | async-start | bytes 1474560 | tf_op jit(solution)/shard_map/reduce_scatter | solution.py:135
  82.1 49.6 %collective-permute-start.8 = (bf16[4,1,64,2304]{3,2,1,0:T(8,128)(2,1)}, bf16[4,1,64,2304]{3,2,1,0:T(8,128)(2,1)}, u32[]{:S(2)}, u32[]{:S(2)}) collective-permute-start(bf16[4,1,64,2304]{3,2,1,0:T(8,128)(2,1)} %bitcast.213), channel_id=1, source_target_pairs={{0,2},{2,0},{4,6},{6,4},{8,10},{10,8},{12,14},{14,12},{16,18},{18,... | collective-permute-start | bytes 3538952 | tf_op jit(solution)/shard_map/ppermute | solution.py:20
  83.4 48.4 %collective-permute-start.9 = (bf16[4,1,64,2304]{3,2,1,0:T(8,128)(2,1)}, bf16[4,1,64,2304]{3,2,1,0:T(8,128)(2,1)}, u32[]{:S(2)}, u32[]{:S(2)}) collective-permute-start(bf16[4,1,64,2304]{3,2,1,0:T(8,128)(2,1)} %bitcast.214), channel_id=1, source_target_pairs={{0,4},{2,6},{4,0},{6,2},{8,12},{10,14},{12,8},{14,10},{16,20},{18,... | collective-permute-start | bytes 3538952 | tf_op jit(solution)/shard_map/ppermute | solution.py:20
  86.5 34.9 %collective-permute-start.11 = (bf16[2,1,64,2176]{3,2,0,1:T(8,128)(2,1)S(1)}, bf16[2,1,64,2176]{3,2,0,1:T(8,128)(2,1)S(1)}, u32[]{:S(2)}, u32[]{:S(2)}) collective-permute-start(bf16[2,1,64,2176]{3,2,0,1:T(8,128)(2,1)S(1)} %slice.270), channel_id=1, source_target_pairs={{0,4},{2,6},{4,0},{6,2},{8,12},{10,14},{12,8},{14,10},{16,20},{18,... | collective-permute-start | bytes 1671176 | tf_op jit(solution)/shard_map/ppermute | solution.py:20
  87.9 33.5 %collective-permute-start.12 = (bf16[2,1,64,2176]{3,2,0,1:T(8,128)(2,1)S(1)}, bf16[2,1,64,2176]{3,2,0,1:T(8,128)(2,1)S(1)}, u32[]{:S(2)}, u32[]{:S(2)}) collective-permute-start(bf16[2,1,64,2176]{3,2,0,1:T(8,128)(2,1)S(1)} %slice.271), channel_id=1, source_target_pairs={{0,2},{2,0},{4,6},{6,4},{8,10},{10,8},{12,14},{14,12},{16,18},{18,... | collective-permute-start | bytes 1671176 | tf_op jit(solution)/shard_map/ppermute | solution.py:20
  101.3 121.8 %copy-start.7 = (bf16[1536,1024]{1,0:T(8,128)(2,1)}, bf16[1536,1024]{1,0:T(8,128)(2,1)S(1)}, u32[]{:S(2)}) copy-start(bf16[1536,1024]{1,0:T(8,128)(2,1)S(1)} %pad_maximum_fusion.4.right_ref.d_down_ref) | copy-start | bytes 9437188
  122.8 36.2 %collective-permute-start.18 = (bf16[16,64,512]{2,1,0:T(8,128)(2,1)}, bf16[16,64,512]{2,1,0:T(8,128)(2,1)}, u32[]{:S(2)}, u32[]{:S(2)}) collective-permute-start(bf16[16,64,512]{2,1,0:T(8,128)(2,1)} %bitcast.35), channel_id=1, source_target_pairs={{0,1},{1,0},{2,3},{3,2},{4,5},{5,4},{6,7},{7,6},{8,9},{9,8},{10,11... | collective-permute-start | bytes 3145736 | tf_op jit(solution)/shard_map/ppermute | solution.py:15
  146.5 6.4 %collective-permute-start.15 = (bf16[2,2,512]{2,1,0:T(2,128)(2,1)S(1)}, bf16[2,2,512]{2,1,0:T(2,128)(2,1)S(1)}, u32[]{:S(2)}, u32[]{:S(2)}) collective-permute-start(bf16[2,2,512]{2,1,0:T(2,128)(2,1)S(1)} %slice.348), channel_id=1, source_target_pairs={{0,2},{2,4},{4,6},{6,8},{8,10},{10,12},{12,14},{14,16},{16,18},{18... | collective-permute-start | bytes 12296 | tf_op jit(solution)/shard_map/ppermute | solution.py:26
  149.2 43.9 %collective-permute-start.13 = (bf16[4,1,64,2304]{3,2,1,0:T(8,128)(2,1)S(1)}, bf16[4,1,64,2304]{3,2,1,0:T(8,128)(2,1)S(1)}, u32[]{:S(2)}, u32[]{:S(2)}) collective-permute-start(bf16[4,1,64,2304]{3,2,1,0:T(8,128)(2,1)S(1)} %bitcast.210), channel_id=1, source_target_pairs={{0,2},{2,0},{4,6},{6,4},{8,10},{10,8},{12,14},{14,12},{16,18},{18,... | collective-permute-start | bytes 3538952 | tf_op jit(solution)/shard_map/ppermute | solution.py:20
  151.3 41.8 %collective-permute-start.14 = (bf16[4,1,64,2304]{3,2,1,0:T(8,128)(2,1)S(1)}, bf16[4,1,64,2304]{3,2,1,0:T(8,128)(2,1)S(1)}, u32[]{:S(2)}, u32[]{:S(2)}) collective-permute-start(bf16[4,1,64,2304]{3,2,1,0:T(8,128)(2,1)S(1)} %bitcast.211), channel_id=1, source_target_pairs={{0,4},{2,6},{4,0},{6,2},{8,12},{10,14},{12,8},{14,10},{16,20},{18,... | collective-permute-start | bytes 3538952 | tf_op jit(solution)/shard_map/ppermute | solution.py:20
  158.1 3.2 collective-permute-start.17
  165.6 27.2 %collective-permute-start.19 = (bf16[768,1024]{1,0:T(8,128)(2,1)S(1)}, bf16[768,1024]{1,0:T(8,128)(2,1)S(1)}, u32[]{:S(2)}, u32[]{:S(2)}) collective-permute-start(bf16[768,1024]{1,0:T(8,128)(2,1)S(1)} %multiply_convert_fusion), channel_id=1, source_target_pairs={{0,1},{1,0},{2,3},{3,2},{4,5},{5,4},{6,7},{7,6},{8,9},{9,8},{10,11... | collective-permute-start | bytes 4718600 | tf_op jit(solution)/shard_map/ppermute | solution.py:15
  169.8 21.1 %collective-permute-start.22 = (bf16[2,1,64,2304]{3,2,1,0:T(8,128)(2,1)S(1)}, bf16[2,1,64,2304]{3,2,1,0:T(8,128)(2,1)S(1)}, u32[]{:S(2)}, u32[]{:S(2)}) collective-permute-start(bf16[2,1,64,2304]{3,2,1,0:T(8,128)(2,1)S(1)} %slice.306), channel_id=1, source_target_pairs={{0,4},{2,6},{4,0},{6,2},{8,12},{10,14},{12,8},{14,10},{16,20},{18,... | collective-permute-start | bytes 1769480 | tf_op jit(solution)/shard_map/ppermute | solution.py:20
  171.4 20.5 %collective-permute-start.23 = (bf16[2,1,64,2304]{3,2,1,0:T(8,128)(2,1)S(1)}, bf16[2,1,64,2304]{3,2,1,0:T(8,128)(2,1)S(1)}, u32[]{:S(2)}, u32[]{:S(2)}) collective-permute-start(bf16[2,1,64,2304]{3,2,1,0:T(8,128)(2,1)S(1)} %slice.307), channel_id=1, source_target_pairs={{0,2},{2,0},{4,6},{6,4},{8,10},{10,8},{12,14},{14,12},{16,18},{18,... | collective-permute-start | bytes 1769480 | tf_op jit(solution)/shard_map/ppermute | solution.py:20
  193.1 14.6 %collective-permute-start.20 = (bf16[2,1,64,2304]{3,2,1,0:T(8,128)(2,1)S(1)}, bf16[2,1,64,2304]{3,2,1,0:T(8,128)(2,1)S(1)}, u32[]{:S(2)}, u32[]{:S(2)}) collective-permute-start(bf16[2,1,64,2304]{3,2,1,0:T(8,128)(2,1)S(1)} %slice.304), channel_id=1, source_target_pairs={{0,4},{2,6},{4,0},{6,2},{8,12},{10,14},{12,8},{14,10},{16,20},{18,... | collective-permute-start | bytes 1769480 | tf_op jit(solution)/shard_map/ppermute | solution.py:20
  194.4 13.4 %collective-permute-start.21 = (bf16[2,1,64,2304]{3,2,1,0:T(8,128)(2,1)S(1)}, bf16[2,1,64,2304]{3,2,1,0:T(8,128)(2,1)S(1)}, u32[]{:S(2)}, u32[]{:S(2)}) collective-permute-start(bf16[2,1,64,2304]{3,2,1,0:T(8,128)(2,1)S(1)} %slice.305), channel_id=1, source_target_pairs={{0,2},{2,0},{4,6},{6,4},{8,10},{10,8},{12,14},{14,12},{16,18},{18,... | collective-permute-start | bytes 1769480 | tf_op jit(solution)/shard_map/ppermute | solution.py:20
  236.1 23.2 %collective-permute-start.25 = (bf16[2,1,144,1024]{3,2,1,0:T(8,128)(2,1)S(1)}, bf16[2,1,144,1024]{3,2,1,0:T(8,128)(2,1)S(1)}, u32[]{:S(2)}, u32[]{:S(2)}) collective-permute-start(bf16[2,1,144,1024]{3,2,1,0:T(8,128)(2,1)S(1)} %get-tuple-element.119), channel_id=1, source_target_pairs={{0,2},{2,0},{4,6},{6,4},{8,10},{10,8},{12,14},{14,12},{16,18},{18,... | collective-permute-start | bytes 1769480 | tf_op jit(solution)/shard_map/ppermute | solution.py:20
  237.2 22.1 %collective-permute-start.26 = (bf16[2,1,144,1024]{3,2,1,0:T(8,128)(2,1)S(1)}, bf16[2,1,144,1024]{3,2,1,0:T(8,128)(2,1)S(1)}, u32[]{:S(2)}, u32[]{:S(2)}) collective-permute-start(bf16[2,1,144,1024]{3,2,1,0:T(8,128)(2,1)S(1)} %get-tuple-element.120), channel_id=1, source_target_pairs={{0,4},{2,6},{4,0},{6,2},{8,12},{10,14},{12,8},{14,10},{16,20},{18,... | collective-permute-start | bytes 1769480 | tf_op jit(solution)/shard_map/ppermute | solution.py:20
  261.8 40.8 %collective-permute-start.27 = (bf16[4,1,144,1024]{3,2,1,0:T(8,128)(2,1)}, bf16[4,1,144,1024]{3,2,1,0:T(8,128)(2,1)S(1)}, u32[]{:S(2)}, u32[]{:S(2)}) collective-permute-start(bf16[4,1,144,1024]{3,2,1,0:T(8,128)(2,1)} %pad_maximum_fusion.10), channel_id=1, source_target_pairs={{0,2},{2,0},{4,6},{6,4},{8,10},{10,8},{12,14},{14,12},{16,18},{18,... | collective-permute-start | bytes 3538952 | tf_op jit(solution)/shard_map/ppermute | solution.py:20
  262.2 40.4 %collective-permute-start.28 = (bf16[4,1,144,1024]{3,2,1,0:T(8,128)(2,1)}, bf16[4,1,144,1024]{3,2,1,0:T(8,128)(2,1)}, u32[]{:S(2)}, u32[]{:S(2)}) collective-permute-start(bf16[4,1,144,1024]{3,2,1,0:T(8,128)(2,1)} %pad_maximum_fusion.11), channel_id=1, source_target_pairs={{0,4},{2,6},{4,0},{6,2},{8,12},{10,14},{12,8},{14,10},{16,20},{18,... | collective-permute-start | bytes 3538952 | tf_op jit(solution)/shard_map/ppermute | solution.py:20
  274.6 42.5 %copy-start.3 = (bf16[1024,2304]{1,0:T(8,128)(2,1)}, bf16[1024,2304]{1,0:T(8,128)(2,1)S(1)}, u32[]{:S(2)}) copy-start(bf16[1024,2304]{1,0:T(8,128)(2,1)S(1)} %shard_map.191) | copy-start | bytes 14155780
  298.2 22.9 %collective-permute-start.33 = (f32[768,1024]{1,0:T(8,128)}, f32[768,1024]{1,0:T(8,128)S(1)}, u32[]{:S(2)}, u32[]{:S(2)}) collective-permute-start(f32[768,1024]{1,0:T(8,128)} %get-tuple-element.151), channel_id=1, source_target_pairs={{0,1},{1,0},{2,3},{3,2},{4,5},{5,4},{6,7},{7,6},{8,9},{9,8},{10,11... | collective-permute-start | bytes 9437192 | tf_op jit(solution)/shard_map/ppermute | solution.py:15
  301.7 15.3 %collective-permute-start.29 = (bf16[2,1,64,2304]{3,2,1,0:T(8,128)(2,1)}, bf16[2,1,64,2304]{3,2,1,0:T(8,128)(2,1)S(1)}, u32[]{:S(2)}, u32[]{:S(2)}) collective-permute-start(bf16[2,1,64,2304]{3,2,1,0:T(8,128)(2,1)} %get-tuple-element.141), channel_id=1, source_target_pairs={{0,2},{2,0},{4,6},{6,4},{8,10},{10,8},{12,14},{14,12},{16,18},{18,... | collective-permute-start | bytes 1769480 | tf_op jit(solution)/shard_map/ppermute | solution.py:20
  302.3 14.9 %collective-permute-start.30 = (bf16[2,1,64,2304]{3,2,1,0:T(8,128)(2,1)}, bf16[2,1,64,2304]{3,2,1,0:T(8,128)(2,1)}, u32[]{:S(2)}, u32[]{:S(2)}) collective-permute-start(bf16[2,1,64,2304]{3,2,1,0:T(8,128)(2,1)} %get-tuple-element.142), channel_id=1, source_target_pairs={{0,4},{2,6},{4,0},{6,2},{8,12},{10,14},{12,8},{14,10},{16,20},{18,... | collective-permute-start | bytes 1769480 | tf_op jit(solution)/shard_map/ppermute | solution.py:20
  326.9 9.8 %collective-permute-start.34 = (bf16[16,32,1024]{2,1,0:T(8,128)(2,1)S(1)}, bf16[16,32,1024]{2,1,0:T(8,128)(2,1)S(1)}, u32[]{:S(2)}, u32[]{:S(2)}) collective-permute-start(bf16[16,32,1024]{2,1,0:T(8,128)(2,1)S(1)} %fusion.23), channel_id=1, source_target_pairs={{0,1},{1,0},{2,3},{3,2},{4,5},{5,4},{6,7},{7,6},{8,9},{9,8},{10,11... | collective-permute-start | bytes 3145736 | tf_op jit(solution)/shard_map/ppermute | solution.py:15
  333.8 9.0 %collective-permute-start.35 = (f32[768,512]{1,0:T(8,128)}, f32[768,512]{1,0:T(8,128)}, u32[]{:S(2)}, u32[]{:S(2)}) collective-permute-start(f32[768,512]{1,0:T(8,128)} %get-tuple-element.293), channel_id=1, source_target_pairs={{0,1},{1,0},{2,3},{3,2},{4,5},{5,4},{6,7},{7,6},{8,9},{9,8},{10,11... | collective-permute-start | bytes 4718600 | tf_op jit(solution)/shard_map/ppermute | solution.py:15
  335.1 146.6 %reduce-scatter.7.cloned.1.call-start = ((), (), s32[]{:S(2)}) async-start(), calls=%async_computation.9 | async-start | bytes 1474560 | tf_op jit(solution)/shard_map/reduce_scatter | solution.py:135
  335.2 28.0 %collective-permute-start.31 = (bf16[4,1,64,2304]{3,2,1,0:T(8,128)(2,1)}, bf16[4,1,64,2304]{3,2,1,0:T(8,128)(2,1)}, u32[]{:S(2)}, u32[]{:S(2)}) collective-permute-start(bf16[4,1,64,2304]{3,2,1,0:T(8,128)(2,1)} %pad_maximum_fusion.12), channel_id=1, source_target_pairs={{0,2},{2,0},{4,6},{6,4},{8,10},{10,8},{12,14},{14,12},{16,18},{18,... | collective-permute-start | bytes 3538952 | tf_op jit(solution)/shard_map/ppermute | solution.py:20
  336.2 27.6 %collective-permute-start.32 = (bf16[4,1,64,2304]{3,2,1,0:T(8,128)(2,1)}, bf16[4,1,64,2304]{3,2,1,0:T(8,128)(2,1)}, u32[]{:S(2)}, u32[]{:S(2)}) collective-permute-start(bf16[4,1,64,2304]{3,2,1,0:T(8,128)(2,1)} %pad_maximum_fusion.13), channel_id=1, source_target_pairs={{0,4},{2,6},{4,0},{6,2},{8,12},{10,14},{12,8},{14,10},{16,20},{18,... | collective-permute-start | bytes 3538952 | tf_op jit(solution)/shard_map/ppermute | solution.py:20
  340.0 40.6 %copy-start.30 = (bf16[16,64,512]{2,1,0:T(8,128)(2,1)}, bf16[16,64,512]{2,1,0:T(8,128)(2,1)S(1)}, u32[]{:S(2)}) copy-start(bf16[16,64,512]{2,1,0:T(8,128)(2,1)S(1)} %pad_maximum_fusion.14) | copy-start | bytes 3145732
  346.2 34.3 %slice-start = ((s8[4718592]{0:T(1024)(128)(4,1)}), s8[4194304]{0:T(1024)(128)(4,1)S(1)}, s32[]{:S(2)}) async-start(s8[4718592]{0:T(1024)(128)(4,1)} %bitcast.167), calls=%async_computation.12 | async-start | bytes 8388608
  346.2 34.3 %slice-start.1 = ((s8[4718592]{0:T(1024)(128)(4,1)}), s8[524288]{0:T(1024)(128)(4,1)S(1)}, s32[]{:S(2)}) async-start(s8[4718592]{0:T(1024)(128)(4,1)} %bitcast.167), calls=%async_computation.13 | async-start | bytes 1048576
  363.8 16.7 %collective-permute-start.36 = (bf16[2,1,64,2816]{3,2,1,0:T(8,128)(2,1)}, bf16[2,1,64,2816]{3,2,1,0:T(8,128)(2,1)S(1)}, u32[]{:S(2)}, u32[]{:S(2)}) collective-permute-start(bf16[2,1,64,2816]{3,2,1,0:T(8,128)(2,1)} %get-tuple-element.158), channel_id=1, source_target_pairs={{0,2},{2,0},{4,6},{6,4},{8,10},{10,8},{12,14},{14,12},{16,18},{18,... | collective-permute-start | bytes 2162696 | tf_op jit(solution)/shard_map/ppermute | solution.py:20
  364.3 16.2 %collective-permute-start.37 = (bf16[2,1,64,2816]{3,2,1,0:T(8,128)(2,1)S(1)}, bf16[2,1,64,2816]{3,2,1,0:T(8,128)(2,1)S(1)}, u32[]{:S(2)}, u32[]{:S(2)}) collective-permute-start(bf16[2,1,64,2816]{3,2,1,0:T(8,128)(2,1)S(1)} %get-tuple-element.159), channel_id=1, source_target_pairs={{0,4},{2,6},{4,0},{6,2},{8,12},{10,14},{12,8},{14,10},{16,20},{18,... | collective-permute-start | bytes 2162696 | tf_op jit(solution)/shard_map/ppermute | solution.py:20
  368.4 15.2 %collective-permute-start.40 = (f32[2,2,512]{2,1,0:T(2,128)S(1)}, f32[2,2,512]{2,1,0:T(2,128)S(1)}, u32[]{:S(2)}, u32[]{:S(2)}) collective-permute-start(f32[2,2,512]{2,1,0:T(2,128)S(1)} %maximum_multiply_fusion), channel_id=1, source_target_pairs={{2,0},{4,2},{6,4},{8,6},{10,8},{12,10},{14,12},{16,14},{18,16},{20... | collective-permute-start | bytes 24584 | tf_op jit(solution)/shard_map/ppermute | solution.py:26
  400.4 38.4 %collective-permute-start.41 = (f32[768,1024]{1,0:T(8,128)}, f32[768,1024]{1,0:T(8,128)}, u32[]{:S(2)}, u32[]{:S(2)}) collective-permute-start(f32[768,1024]{1,0:T(8,128)} %get-tuple-element.167), channel_id=1, source_target_pairs={{0,1},{1,0},{2,3},{3,2},{4,5},{5,4},{6,7},{7,6},{8,9},{9,8},{10,11... | collective-permute-start | bytes 9437192 | tf_op jit(solution)/shard_map/ppermute | solution.py:15
  402.7 79.1 %reduce-scatter.9.cloned.1.call-start = ((), (), s32[]{:S(2)}) async-start(), calls=%async_computation.10 | async-start | bytes 1802240 | tf_op jit(solution)/shard_map/reduce_scatter | solution.py:135
  402.7 33.5 %collective-permute-start.38 = (bf16[4,1,64,2816]{3,2,1,0:T(8,128)(2,1)}, bf16[4,1,64,2816]{3,2,1,0:T(8,128)(2,1)S(1)}, u32[]{:S(2)}, u32[]{:S(2)}) collective-permute-start(bf16[4,1,64,2816]{3,2,1,0:T(8,128)(2,1)} %pad_maximum_fusion.8), channel_id=1, source_target_pairs={{0,2},{2,0},{4,6},{6,4},{8,10},{10,8},{12,14},{14,12},{16,18},{18,... | collective-permute-start | bytes 4325384 | tf_op jit(solution)/shard_map/ppermute | solution.py:20
  403.9 33.1 %collective-permute-start.39 = (bf16[4,1,64,2816]{3,2,1,0:T(8,128)(2,1)}, bf16[4,1,64,2816]{3,2,1,0:T(8,128)(2,1)S(1)}, u32[]{:S(2)}, u32[]{:S(2)}) collective-permute-start(bf16[4,1,64,2816]{3,2,1,0:T(8,128)(2,1)} %pad_maximum_fusion.9), channel_id=1, source_target_pairs={{0,4},{2,6},{4,0},{6,2},{8,12},{10,14},{12,8},{14,10},{16,20},{18,... | collective-permute-start | bytes 4325384 | tf_op jit(solution)/shard_map/ppermute | solution.py:20
  409.5 27.6 %slice-start.2 = ((s8[4718592]{0:T(1024)(128)(4,1)}), s8[4194304]{0:T(1024)(128)(4,1)S(1)}, s32[]{:S(2)}) async-start(s8[4718592]{0:T(1024)(128)(4,1)} %bitcast.170), calls=%async_computation.14 | async-start | bytes 8388608
  438.7 65.5 %reduce-scatter.11.cloned.1.call-start = ((), (), s32[]{:S(2)}) async-start(), calls=%async_computation.11 | async-start | bytes 1064960 | tf_op jit(solution)/shard_map/reduce_scatter | solution.py:135
  443.6 13.4 %collective-permute-start.42 = (bf16[2,1,64,1664]{3,2,0,1:T(8,128)(2,1)S(1)}, bf16[2,1,64,1664]{3,2,0,1:T(8,128)(2,1)S(1)}, u32[]{:S(2)}, u32[]{:S(2)}) collective-permute-start(bf16[2,1,64,1664]{3,2,0,1:T(8,128)(2,1)S(1)} %get-tuple-element.176), channel_id=1, source_target_pairs={{0,2},{2,0},{4,6},{6,4},{8,10},{10,8},{12,14},{14,12},{16,18},{18,... | collective-permute-start | bytes 1277960 | tf_op jit(solution)/shard_map/ppermute | solution.py:20
  444.0 13.0 %collective-permute-start.43 = (bf16[2,1,64,1664]{3,2,0,1:T(8,128)(2,1)S(1)}, bf16[2,1,64,1664]{3,2,0,1:T(8,128)(2,1)S(1)}, u32[]{:S(2)}, u32[]{:S(2)}) collective-permute-start(bf16[2,1,64,1664]{3,2,0,1:T(8,128)(2,1)S(1)} %get-tuple-element.177), channel_id=1, source_target_pairs={{0,4},{2,6},{4,0},{6,2},{8,12},{10,14},{12,8},{14,10},{16,20},{18,... | collective-permute-start | bytes 1277960 | tf_op jit(solution)/shard_map/ppermute | solution.py:20
  457.5 8.2 %collective-permute-start.46 = (bf16[768,1024]{1,0:T(8,128)(2,1)S(1)}, bf16[768,1024]{1,0:T(8,128)(2,1)S(1)}, u32[]{:S(2)}, u32[]{:S(2)}) collective-permute-start(bf16[768,1024]{1,0:T(8,128)(2,1)S(1)} %get-tuple-element.186), channel_id=1, source_target_pairs={{0,1},{1,0},{2,3},{3,2},{4,5},{5,4},{6,7},{7,6},{8,9},{9,8},{10,11... | collective-permute-start | bytes 4718600 | tf_op jit(solution)/shard_map/ppermute | solution.py:15
  459.2 20.5 %collective-permute-start.44 = (bf16[4,1,64,1664]{3,2,0,1:T(8,128)(2,1)S(1)}, bf16[4,1,64,1664]{3,2,0,1:T(8,128)(2,1)S(1)}, u32[]{:S(2)}, u32[]{:S(2)}) collective-permute-start(bf16[4,1,64,1664]{3,2,0,1:T(8,128)(2,1)S(1)} %pad_maximum_fusion.17), channel_id=1, source_target_pairs={{0,2},{2,0},{4,6},{6,4},{8,10},{10,8},{12,14},{14,12},{16,18},{18,... | collective-permute-start | bytes 2555912 | tf_op jit(solution)/shard_map/ppermute | solution.py:20
  460.4 20.2 %collective-permute-start.45 = (bf16[4,1,64,1664]{3,2,0,1:T(8,128)(2,1)S(1)}, bf16[4,1,64,1664]{3,2,0,1:T(8,128)(2,1)S(1)}, u32[]{:S(2)}, u32[]{:S(2)}) collective-permute-start(bf16[4,1,64,1664]{3,2,0,1:T(8,128)(2,1)S(1)} %pad_maximum_fusion.18), channel_id=1, source_target_pairs={{0,4},{2,6},{4,0},{6,2},{8,12},{10,14},{12,8},{14,10},{16,20},{18,... | collective-permute-start | bytes 2555912 | tf_op jit(solution)/shard_map/ppermute | solution.py:20
  482.8 5.6 %collective-permute-start.48 = (bf16[32,2304]{1,0:T(8,128)(2,1)S(1)}, bf16[32,2304]{1,0:T(8,128)(2,1)S(1)}, u32[]{:S(2)}, u32[]{:S(2)}) collective-permute-start(bf16[32,2304]{1,0:T(8,128)(2,1)S(1)} %broadcast_select_fusion.14), channel_id=1, source_target_pairs={{0,1},{1,0},{2,3},{3,2},{4,5},{5,4},{6,7},{7,6},{8,9},{9,8},{10,11... | collective-permute-start | bytes 442376 | tf_op jit(solution)/shard_map/ppermute | solution.py:15
  485.9 7.6 %collective-permute-start.49 = (bf16[32,2304]{1,0:T(8,128)(2,1)S(1)}, bf16[32,2304]{1,0:T(8,128)(2,1)S(1)}, u32[]{:S(2)}, u32[]{:S(2)}) collective-permute-start(bf16[32,2304]{1,0:T(8,128)(2,1)S(1)} %broadcast_select_fusion.10), channel_id=1, source_target_pairs={{0,1},{1,0},{2,3},{3,2},{4,5},{5,4},{6,7},{7,6},{8,9},{9,8},{10,11... | collective-permute-start | bytes 442376 | tf_op jit(solution)/shard_map/ppermute | solution.py:15
  505.2 4.8 collective-permute-start.47
  (54 other events, 398.7 us)
Sparse Core Ops, SparseCore 0:
  19.1 30.8 all-gather.4
  52.2 29.5 all-gather.6
  83.9 29.5 all-gather.8
  115.0 89.1 all-gather.10
  335.2 27.2 reduce-scatter.4
  402.8 27.2 reduce-scatter.6
  438.8 31.6 reduce-scatter.8
  481.9 22.2 reduce-scatter.10

commit v3 on v2

--- a/solution.py
+++ b/solution.py
@@ -412,6 +412,7 @@
     out_fold = jnp.concatenate([out_weight[:, :half], out_weight[:, half:]], axis=0)
     front = jnp.concatenate([in_pair, out_fold], axis=1)
 
+    gate_weight, up_weight, front = lax.optimization_barrier((gate_weight, up_weight, front))
     wide = jnp.concatenate([gate_weight, up_weight], axis=1)
     wide = wide.reshape(part, 2 * chips, 2, ff_block)
     wide_low = wide[:, :, 0].reshape(part, 2 * ff_half)
@@ -492,6 +493,9 @@
     mixed = jnp.concatenate(
         ordered(mixed_half[:rows], swap_cores(mixed_half[rows:])), axis=1
     )
+    up_x, up_y, mixed = lax.optimization_barrier((plane_up.from_x, plane_up.from_y, mixed))
+    plane_up.from_x, plane_up.from_y = up_x, up_y
+    plane_up.corners()
 
     resid = own_inputs + times(mixed, weight_out)
     scale_two = rms_scale(resid)
@@ -500,10 +504,7 @@
     hidden2 = jnp.concatenate([hidden2_own, swap_cores(hidden2_own)], axis=0)
 
     weight_gate = plane_gate.place().reshape(width, ff_half)
-    up_x, up_y, hidden2 = lax.optimization_barrier((plane_up.from_x, plane_up.from_y, hidden2))
-    plane_up.from_x, plane_up.from_y = up_x, up_y
     gate_proj = gate_kernel(hidden2, weight_gate)
-    plane_up.corners()
     weight_up = plane_up.place().reshape(width, ff_half)
     active, up_proj = active_kernel(hidden2, weight_up, gate_proj)
 
@@ -566,7 +567,7 @@
         * keep_state
     )
     from_next = shift(d_state, -1)
-    d_conv = scatter_up.turned(scatter_gate.landed(d_conv))
+    d_conv = scatter_gate.landed(d_conv)
     following = jnp.pad(d_conv, ((0, 0), (0, 2), (0, 0)))
     d_gated = (
         taps[2] * following[:, :-2] + taps[1] * following[:, 1:-1] + taps[0] * following[:, 2:]
@@ -575,11 +576,12 @@
     d_projected = jnp.concatenate(
         [d_gated * v_part, d_c_part, d_gated * b_part], axis=1
     ).astype(BF16)
+    d_projected = scatter_up.turned(d_projected)
     d_hidden, d_hidden_give = rows_kernel(
         times_transposed, (d_projected,), (weight_in,), (F32, F32)
     )
     d_projected = after(d_projected, d_hidden_give)
-    grad_in = scatter_up.landed(weight_kernel(hidden, d_projected))
+    grad_in = weight_kernel(hidden, d_projected)
     d_hidden = d_hidden + after(swap_cores(d_hidden_give), grad_in)
 
     scale_one = rms_scale(own_inputs)
@@ -608,7 +610,7 @@
     result, result_give = rows_kernel(
         times, (scatter_front.opened(active),), (weight_down,), (F32, BF16)
     )
-    result_give = scatter_front.turned(result_give)
+    result_give = scatter_front.turned(scatter_up.landed(result_give))
     result = resid + result + swap_cores(result_give).astype(F32)
     output = scatter_front.landed(result.astype(BF16)[None])
     shard_down, shard_gate, shard_up, output = lax.optimization_barrier(

time: 530 us -> 527 us (level)
  waiting for transfers between devices: 133 us -> 124 us
  starting transfers between devices: 51.7 us -> 57.5 us
    ppermute x32, waiting for transfers between devices: 92.1 us -> 80.2 us  [across(): return lax.ppermute(x, 'seq', [(i, i ^ bit) for i in range(peers)])]
    unnamed x124 -> x138, local copies, waits for them, and re-layouts: 20.7 us -> 19.9 us
  transfers between devices with their start and end apart: 58 -> 58, of which waited for: 15 -> 23; matrix products, arithmetic and copies ran while one was open for 28% -> 28% of each run, Pallas kernels for 26% -> 26%
where the time goes in v3:
time: 527 us; the launch traced here: 517 us
  Pallas kernels  136 us (26%)
  waiting for transfers between devices  124 us (24%)
  other arithmetic  93.5 us (18%)
  local copies, waits for them, and re-layouts  84.1 us (16%)
  starting transfers between devices  57.5 us (11%)
  between operations  16.6 us (3%)
  matrix products  5.61 us (1%)
    pallas_call x11, Pallas kernels, call(): pl.pallas_call(body, grid=(grid,), in_specs=ins, out_specs=[spec for _, s...  136 us
    ppermute x32, waiting for transfers between devices, across(): return lax.ppermute(x, 'seq', [(i, i ^ bit) for i in range(peers)])  80.2 us
    ppermute x32, starting transfers between devices, across(): return lax.ppermute(x, 'seq', [(i, i ^ bit) for i in range(peers)])  32.5 us
    all_gather x4, waiting for transfers between devices, line_gather(): lax.all_gather(shard, 'seq', axis_index_groups=columns_of_line(peers), ax...  28.3 us
    unnamed x138, local copies, waits for them, and re-layouts  19.9 us
    ppermute x16, starting transfers between devices, swap_cores(): return lax.ppermute(x, 'fsdp', [(0, 1), (1, 0)])  19.4 us
    reduce_scatter x4, waiting for transfers between devices, landed(): lax.psum_scatter(mine.reshape(self.depth * self.rows, self.cols), 'seq',...  12.2 us
    convert_element_type x4, other arithmetic, landed(): mine = (self.piece(0, 0, self.depth).astype(F32) + from_x.astype(F32) + f...  11.2 us
  transfers between devices with their start and end apart: 58, of which 23 were waited for; matrix products, arithmetic and copies ran while one was open for 28% of the time, Pallas kernels for 26%

profile of v3, /device:TPU:1, one launch (start us, length us, event | category | flops | bytes accessed | tf_op | source)
XLA Modules:
  0.0 517.3 jit_solution(5117286872627400896)
XLA Ops:
  14.3 2.3 fusion.56
  21.3 2.2 collective-permute-done.16
  24.0 2.4 collective-permute-start.1
  31.2 2.5 collective-permute-done.1
  42.4 6.3 %all-gather.5.cloned.1.call-done = bf16[256,2176]{1,0:T(8,128)(2,1)} async-done(((bf16[64,2176]{1,0:T(8,128)(2,1)}), bf16[256,2176]{1,0:T(8,128)(2,1)}) %all-gather.5.cloned.1.call-update) | async-done | bytes 1114128 | tf_op jit(solution)/shard_map/all_gather | solution.py:43
  58.3 22.1 %all-gather.7.cloned.1.call-done = bf16[256,2304]{1,0:T(8,128)(2,1)} async-done(((bf16[64,2304]{1,0:T(8,128)(2,1)}), bf16[256,2304]{1,0:T(8,128)(2,1)}) %all-gather.7.cloned.1.call-update) | async-done | bytes 1179664 | tf_op jit(solution)/shard_map/all_gather | solution.py:43
  92.7 3.0 broadcast.83.clone
  97.8 2.2 pad_maximum_fusion.4.right_ref.d_down_ref
  100.0 20.0 %collective-permute-done.11 = bf16[2,1,64,2176]{3,2,0,1:T(8,128)(2,1)S(1)} collective-permute-done((bf16[2,1,64,2176]{3,2,0,1:T(8,128)(2,1)S(1)}, bf16[2,1,64,2176]{3,2,0,1:T(8,128)(2,1)S(1)}, u32[]{:S(2)}, u32[]{:S(2)}) %collective-permute-start.11) | collective-permute-done | bytes 557088 | tf_op jit(solution)/shard_map/ppermute | solution.py:20
  122.4 2.5 collective-permute-start.18
  126.7 3.3 fusion.2.left_ref
  131.6 1.9 copy-done.14
  133.5 1.9 copy-done.16
  135.4 7.4 %shard_map.186 = f32[1536,1536]{1,0:T(8,128)} custom-call(bf16[1536,1024]{1,0:T(8,128)(2,1)S(1)} %copy-done.16, bf16[1024,1536]{1,0:T(8,128)(2,1)S(1)} %bitcast.186), custom_call_target="tpu_custom_call" | custom-call | flops 38654705664 | bytes 77309408 | tf_op jit(solution)/shard_map/pallas_call | solution.py:171
  142.8 3.4 multiply_convert_fusion.1
  146.2 3.4 collective-permute-start.15
  150.7 2.5 constant_dynamic-update-slice_fusion.8
  153.9 2.5 constant_dynamic-update-slice_fusion.7
  158.3 2.1 collective-permute-start.23
  161.4 3.5 fusion.16
  173.2 1.9 multiply_reduce_fusion.5
  180.3 11.8 %collective-permute-done.20 = bf16[2,1,64,2304]{3,2,1,0:T(8,128)(2,1)S(1)} collective-permute-done((bf16[2,1,64,2304]{3,2,1,0:T(8,128)(2,1)S(1)}, bf16[2,1,64,2304]{3,2,1,0:T(8,128)(2,1)S(1)}, u32[]{:S(2)}, u32[]{:S(2)}) %collective-permute-start.20) | collective-permute-done | bytes 589856 | tf_op jit(solution)/shard_map/ppermute | solution.py:20
  193.6 13.2 %shard_map.187.gate_ref = bf16[1536,2304]{1,0:T(8,128)(2,1)} custom-call(bf16[1536,1024]{1,0:T(8,128)(2,1)S(1)} %pad_maximum_fusion.3.hidden_ref.left_ref, bf16[1024,2304]{1,0:T(8,128)(2,1)} %bitcast.43.weight_ref.refs_2_), custom_call_target="tpu_custom_call" | custom-call | flops 7247757312 | bytes 14495514 | tf_op jit(solution)/shard_map/pallas_call | solution.py:171
  206.8 14.5 %shard_map.188 = (bf16[1536,2304]{1,0:T(8,128)(2,1)}, bf16[1536,2304]{1,0:T(8,128)(2,1)}) custom-call(bf16[1536,1024]{1,0:T(8,128)(2,1)S(1)} %pad_maximum_fusion.3.hidden_ref.left_ref, bf16[1024,2304]{1,0:T(8,128)(2,1)S(1)} %bitcast.184, bf16[1536,2304]{1,0:T(8,128)(2,1)} %shard_map.187.gate_ref), custom_call_target="tpu_custom_call" | custom-call | flops 7247757312 | bytes 14495514 | tf_op jit(solution)/shard_map/pallas_call | solution.py:171
  221.3 10.7 %shard_map.189 = bf16[2304,1024]{1,0:T(8,128)(2,1)S(1)} custom-call(bf16[1536,2304]{1,0:T(8,128)(2,1)} %get-tuple-element.177.left_ref.refs_0_, bf16[1536,1024]{1,0:T(8,128)(2,1)S(1)} %pad_maximum_fusion.4.right_ref.d_down_ref), custom_call_target="tpu_custom_call" | custom-call | flops 7247757312 | bytes 14495514 | tf_op jit(solution)/shard_map/pallas_call | solution.py:171
  232.1 2.1 copy-done.5
  235.7 1.9 copy-done.9
  237.6 2.3 copy-done.20
  239.9 17.6 %shard_map.190 = (bf16[1536,2304]{1,0:T(8,128)(2,1)}, bf16[1536,2304]{1,0:T(8,128)(2,1)}) custom-call(bf16[1536,1024]{1,0:T(8,128)(2,1)S(1)} %copy-done.9, bf16[2304,1024]{1,0:T(8,128)(2,1)S(1)} %copy-done.20, bf16[1536,2304]{1,0:T(8,128)(2,1)} %shard_map.187.gate_ref, bf16[1536,2304]{1,0:T(8,128)(2,1)} %get-tuple-element.131.upper_ref), custom_call_target="tpu_custom_call" | custom-call | flops 7247757312 | bytes 14495514 | tf_op jit(solution)/shard_map/pallas_call | solution.py:171
  261.6 11.2 %shard_map.191 = bf16[1024,2304]{1,0:T(8,128)(2,1)S(1)} custom-call(bf16[1536,1024]{1,0:T(8,128)(2,1)S(1)} %copy-done.11, bf16[1536,2304]{1,0:T(8,128)(2,1)} %get-tuple-element.140.right_ref.refs_0_), custom_call_target="tpu_custom_call" | custom-call | flops 7247757312 | bytes 14495514 | tf_op jit(solution)/shard_map/pallas_call | solution.py:171
  274.0 22.4 %shard_map.192 = (f32[768,1024]{1,0:T(8,128)S(1)}, f32[768,1024]{1,0:T(8,128)}) custom-call(bf16[1536,2304]{1,0:T(8,128)(2,1)} %get-tuple-element.140.right_ref.refs_0_, bf16[1536,2304]{1,0:T(8,128)(2,1)} %get-tuple-element.149.refs_1_.right_ref, bf16[1024,2304]{1,0:T(8,128)(2,1)} %bitcast.43.weight_ref.refs_2_, bf16[1024,2304]{1,0:T(8,128)(2,1)} %bitcast.185), custom_call_target="tpu_custom_call" | custom-call | flops 14495514624 | bytes 28991028 | tf_op jit(solution)/shard_map/pallas_call | solution.py:171
  296.5 2.6 collective-permute-start.33
  300.4 3.0 add_convert_fusion.3
  303.5 11.4 %shard_map.193 = bf16[1024,2304]{1,0:T(8,128)(2,1)S(1)} custom-call(bf16[1536,1024]{1,0:T(8,128)(2,1)S(1)} %copy-done.12, bf16[1536,2304]{1,0:T(8,128)(2,1)} %get-tuple-element.149.refs_1_.right_ref), custom_call_target="tpu_custom_call" | custom-call | flops 7247757312 | bytes 14495514 | tf_op jit(solution)/shard_map/pallas_call | solution.py:171
  320.3 2.4 multiply_add_fusion
  322.7 1.8 fusion.28
  324.6 2.1 copy-done.40
  329.2 1.9 fusion.26
  332.6 3.3 fusion.20
  336.2 3.0 fusion.32
  339.2 3.6 pad_maximum_fusion.5
  342.8 4.7 multiply_reduce_fusion
  347.5 11.5 %collective-permute-done.31 = bf16[4,1,64,2304]{3,2,1,0:T(8,128)(2,1)} collective-permute-done((bf16[4,1,64,2304]{3,2,1,0:T(8,128)(2,1)}, bf16[4,1,64,2304]{3,2,1,0:T(8,128)(2,1)}, u32[]{:S(2)}, u32[]{:S(2)}) %collective-permute-start.31) | collective-permute-done | bytes 1179680 | tf_op jit(solution)/shard_map/ppermute | solution.py:20
  360.7 3.4 add_convert_fusion.2
  364.1 2.1 collective-permute-start.36
  369.4 2.6 pad_maximum_fusion.refs_0_.right_ref
  372.0 8.7 %collective-permute-done.36 = bf16[2,1,64,2816]{3,2,1,0:T(8,128)(2,1)S(1)} collective-permute-done((bf16[2,1,64,2816]{3,2,1,0:T(8,128)(2,1)S(1)}, bf16[2,1,64,2816]{3,2,1,0:T(8,128)(2,1)S(1)}, u32[]{:S(2)}, u32[]{:S(2)}) %collective-permute-start.36) | collective-permute-done | bytes 720928 | tf_op jit(solution)/shard_map/ppermute | solution.py:20
  384.5 9.2 %shard_map.194 = (f32[768,1024]{1,0:T(8,128)S(1)}, f32[768,1024]{1,0:T(8,128)}) custom-call(bf16[1536,1536]{1,0:T(8,128)(2,1)} %pad_maximum_fusion.refs_0_.right_ref, bf16[1024,1536]{1,0:T(8,128)(2,1)S(1)} %bitcast.187), custom_call_target="tpu_custom_call" | custom-call | flops 4831838208 | bytes 9663676 | tf_op jit(solution)/shard_map/pallas_call | solution.py:171
  395.5 3.1 collective-permute-start.41
  399.2 3.6 multiply_reduce_fusion.2
  405.2 7.9 %shard_map.195 = bf16[1024,1536]{1,0:T(8,128)(2,1)S(1)} custom-call(bf16[1536,1024]{1,0:T(8,128)(2,1)S(1)} %copy-done.17, bf16[1536,1536]{1,0:T(8,128)(2,1)} %pad_maximum_fusion.refs_0_.right_ref), custom_call_target="tpu_custom_call" | custom-call | flops 4831838208 | bytes 9663676 | tf_op jit(solution)/shard_map/pallas_call | solution.py:171
  413.1 2.9 fusion.8
  419.1 2.5 copy-done.21
  421.6 10.1 %shard_map.196 = (f32[768,1024]{1,0:T(8,128)S(1)}, bf16[768,1024]{1,0:T(8,128)(2,1)S(1)}) custom-call(bf16[1536,2304]{1,0:T(8,128)(2,1)} %get-tuple-element.177.left_ref.refs_0_, bf16[2304,1024]{1,0:T(8,128)(2,1)S(1)} %copy-done.21), custom_call_target="tpu_custom_call" | custom-call | flops 7247757312 | bytes 14495514 | tf_op jit(solution)/shard_map/pallas_call | solution.py:171
  431.7 4.7 collective-permute-done.39
  438.7 3.5 add_convert_fusion.1
  442.5 4.9 collective-permute-done.42
  450.4 2.3 collective-permute-start.46
  455.1 5.4 %fusion.12 = f32[1,768,1024]{2,1,0:T(8,128)} fusion(f32[768,1024]{1,0:T(8,128)} %copy-done.39, f32[768]{0:T(1024)S(1)} %broadcast_multiply_fusion, f32[1024]{0:T(1024)S(1)} %copy-done.59, f32[768]{0:T(1024)S(1)} %add_rsqrt_fusion.1, bf16[1,768,1024]{2,1,0:T(8,128)(2,1)S(1)} %copy-done.32, f32[768,1024]{1,0:T(8,128)S(1)} %copy-done.3, ...), kind=kLoop, calls=%fused_computation.41 | loop fusion | flops 6291456 | bytes 14166016 | tf_op jit(solution)/shard_map/broadcast_in_dim | solution.py:650
  460.5 2.1 fusion.21
  462.6 10.8 %collective-permute-done.44 = bf16[4,1,64,1664]{3,2,0,1:T(8,128)(2,1)S(1)} collective-permute-done((bf16[4,1,64,1664]{3,2,0,1:T(8,128)(2,1)S(1)}, bf16[4,1,64,1664]{3,2,0,1:T(8,128)(2,1)S(1)}, u32[]{:S(2)}, u32[]{:S(2)}) %collective-permute-start.44) | collective-permute-done | bytes 852000 | tf_op jit(solution)/shard_map/ppermute | solution.py:20
  486.4 2.1 reshape.193
  490.1 11.1 %reduce-scatter.11.cloned.1.call-done = bf16[64,1664]{1,0:T(8,128)(2,1)} async-done(((bf16[256,1664]{1,0:T(8,128)(2,1)}), bf16[64,1664]{1,0:T(8,128)(2,1)}) %reduce-scatter.11.cloned.1.call-update) | async-done | bytes 213008 | tf_op jit(solution)/shard_map/reduce_scatter | solution.py:135
  504.8 2.1 reshape.194
  (378 shorter events, 137.4 us)
Async XLA Ops:
  7.2 41.5 %all-gather.5.cloned.1.call-start = ((), (), s32[]{:S(2)}) async-start(), calls=%async_computation.4 | async-start | bytes 1392640 | tf_op jit(solution)/shard_map/all_gather | solution.py:43
  10.2 1.4 collective-permute-start
  17.3 1.6 collective-permute-start.7
  17.6 62.8 %all-gather.7.cloned.1.call-start = ((), (), s32[]{:S(2)}) async-start(), calls=%async_computation.5 | async-start | bytes 1474560 | tf_op jit(solution)/shard_map/all_gather | solution.py:43
  19.9 110.1 %all-gather.9.cloned.1.call-start = ((), (), s32[]{:S(2)}) async-start(), calls=%async_computation.6 | async-start | bytes 1474560 | tf_op jit(solution)/shard_map/all_gather | solution.py:43
  20.0 20.1 %collective-permute-start.10 = (bf16[768,1024]{1,0:T(8,128)(2,1)S(1)}, bf16[768,1024]{1,0:T(8,128)(2,1)S(1)}, u32[]{:S(2)}, u32[]{:S(2)}) collective-permute-start(bf16[768,1024]{1,0:T(8,128)(2,1)S(1)} %bitcast.190), channel_id=1, source_target_pairs={{0,1},{1,0},{2,3},{3,2},{4,5},{5,4},{6,7},{7,6},{8,9},{9,8},{10,11... | collective-permute-start | bytes 4718600 | tf_op jit(solution)/shard_map/ppermute | solution.py:15
  20.9 2.6 collective-permute-start.16
  24.0 9.8 %collective-permute-start.1 = (bf16[1,1,144,1024]{3,2,1,0:T(8,128)(2,1)}, bf16[1,1,144,1024]{3,2,1,0:T(8,128)(2,1)S(1)}, u32[]{:S(2)}, u32[]{:S(2)}) collective-permute-start(bf16[1,1,144,1024]{3,2,1,0:T(8,128)(2,1)} %bitcast.5), channel_id=1, source_target_pairs={{0,2},{2,0},{4,6},{6,4},{8,10},{10,8},{12,14},{14,12},{16,18},{18,... | collective-permute-start | bytes 884744 | tf_op jit(solution)/shard_map/ppermute | solution.py:20
  26.3 9.3 %collective-permute-start.3 = (bf16[1,1,144,1024]{3,2,1,0:T(8,128)(2,1)}, bf16[1,1,144,1024]{3,2,1,0:T(8,128)(2,1)S(1)}, u32[]{:S(2)}, u32[]{:S(2)}) collective-permute-start(bf16[1,1,144,1024]{3,2,1,0:T(8,128)(2,1)} %bitcast.5), channel_id=1, source_target_pairs={{0,4},{2,6},{4,0},{6,2},{8,12},{10,14},{12,8},{14,10},{16,20},{18,... | collective-permute-start | bytes 884744 | tf_op jit(solution)/shard_map/ppermute | solution.py:20
  34.4 7.9 %collective-permute-start.2 = (bf16[1,1,64,1024]{3,2,1,0:T(8,128)(2,1)}, bf16[1,1,64,1024]{3,2,1,0:T(8,128)(2,1)}, u32[]{:S(2)}, u32[]{:S(2)}) collective-permute-start(bf16[1,1,64,1024]{3,2,1,0:T(8,128)(2,1)} %slice.336), channel_id=1, source_target_pairs={{0,4},{2,6},{4,0},{6,2},{8,12},{10,14},{12,8},{14,10},{16,20},{18,... | collective-permute-start | bytes 393224 | tf_op jit(solution)/shard_map/ppermute | solution.py:20
  36.3 6.1 %collective-permute-start.4 = (bf16[1,1,80,1024]{3,2,1,0:T(8,128)(2,1)}, bf16[1,1,80,1024]{3,2,1,0:T(8,128)(2,1)}, u32[]{:S(2)}, u32[]{:S(2)}) collective-permute-start(bf16[1,1,80,1024]{3,2,1,0:T(8,128)(2,1)} %slice.337), channel_id=1, source_target_pairs={{0,2},{2,0},{4,6},{6,4},{8,10},{10,8},{12,14},{14,12},{16,18},{18,... | collective-permute-start | bytes 491528 | tf_op jit(solution)/shard_map/ppermute | solution.py:20
  37.5 198.1 %all-gather.11.cloned.1.call-start = ((), (), s32[]{:S(2)}) async-start(), calls=%async_computation.7 | async-start | bytes 5898240 | tf_op jit(solution)/shard_map/all_gather | solution.py:43
  40.0 57.7 %collective-permute-start.24 = (bf16[768,1024]{1,0:T(8,128)(2,1)}, bf16[768,1024]{1,0:T(8,128)(2,1)}, u32[]{:S(2)}, u32[]{:S(2)}) collective-permute-start(bf16[768,1024]{1,0:T(8,128)(2,1)} %bitcast.44), channel_id=1, source_target_pairs={{0,1},{1,0},{2,3},{3,2},{4,5},{5,4},{6,7},{7,6},{8,9},{9,8},{10,11... | collective-permute-start | bytes 4718600 | tf_op jit(solution)/shard_map/ppermute | solution.py:15
  48.7 32.0 %collective-permute-start.5 = (bf16[4,1,64,2176]{3,2,0,1:T(8,128)(2,1)}, bf16[4,1,64,2176]{3,2,0,1:T(8,128)(2,1)}, u32[]{:S(2)}, u32[]{:S(2)}) collective-permute-start(bf16[4,1,64,2176]{3,2,0,1:T(8,128)(2,1)} %bitcast.218), channel_id=1, source_target_pairs={{0,2},{2,0},{4,6},{6,4},{8,10},{10,8},{12,14},{14,12},{16,18},{18,... | collective-permute-start | bytes 3342344 | tf_op jit(solution)/shard_map/ppermute | solution.py:20
  49.9 30.8 %collective-permute-start.6 = (bf16[4,1,64,2176]{3,2,0,1:T(8,128)(2,1)}, bf16[4,1,64,2176]{3,2,0,1:T(8,128)(2,1)}, u32[]{:S(2)}, u32[]{:S(2)}) collective-permute-start(bf16[4,1,64,2176]{3,2,0,1:T(8,128)(2,1)} %bitcast.219), channel_id=1, source_target_pairs={{0,4},{2,6},{4,0},{6,2},{8,12},{10,14},{12,8},{14,10},{16,20},{18,... | collective-permute-start | bytes 3342344 | tf_op jit(solution)/shard_map/ppermute | solution.py:20
  80.4 394.7 %reduce-scatter.5.cloned.1.call-start = ((), (), s32[]{:S(2)}) async-start(), calls=%async_computation.8 | async-start | bytes 1474560 | tf_op jit(solution)/shard_map/reduce_scatter | solution.py:135
  80.7 49.3 %collective-permute-start.8 = (bf16[4,1,64,2304]{3,2,1,0:T(8,128)(2,1)}, bf16[4,1,64,2304]{3,2,1,0:T(8,128)(2,1)}, u32[]{:S(2)}, u32[]{:S(2)}) collective-permute-start(bf16[4,1,64,2304]{3,2,1,0:T(8,128)(2,1)} %bitcast.215), channel_id=1, source_target_pairs={{0,2},{2,0},{4,6},{6,4},{8,10},{10,8},{12,14},{14,12},{16,18},{18,... | collective-permute-start | bytes 3538952 | tf_op jit(solution)/shard_map/ppermute | solution.py:20
  82.0 48.1 %collective-permute-start.9 = (bf16[4,1,64,2304]{3,2,1,0:T(8,128)(2,1)}, bf16[4,1,64,2304]{3,2,1,0:T(8,128)(2,1)}, u32[]{:S(2)}, u32[]{:S(2)}) collective-permute-start(bf16[4,1,64,2304]{3,2,1,0:T(8,128)(2,1)} %bitcast.216), channel_id=1, source_target_pairs={{0,4},{2,6},{4,0},{6,2},{8,12},{10,14},{12,8},{14,10},{16,20},{18,... | collective-permute-start | bytes 3538952 | tf_op jit(solution)/shard_map/ppermute | solution.py:20
  85.1 34.9 %collective-permute-start.11 = (bf16[2,1,64,2176]{3,2,0,1:T(8,128)(2,1)S(1)}, bf16[2,1,64,2176]{3,2,0,1:T(8,128)(2,1)S(1)}, u32[]{:S(2)}, u32[]{:S(2)}) collective-permute-start(bf16[2,1,64,2176]{3,2,0,1:T(8,128)(2,1)S(1)} %slice.270), channel_id=1, source_target_pairs={{0,4},{2,6},{4,0},{6,2},{8,12},{10,14},{12,8},{14,10},{16,20},{18,... | collective-permute-start | bytes 1671176 | tf_op jit(solution)/shard_map/ppermute | solution.py:20
  86.5 33.5 %collective-permute-start.12 = (bf16[2,1,64,2176]{3,2,0,1:T(8,128)(2,1)S(1)}, bf16[2,1,64,2176]{3,2,0,1:T(8,128)(2,1)S(1)}, u32[]{:S(2)}, u32[]{:S(2)}) collective-permute-start(bf16[2,1,64,2176]{3,2,0,1:T(8,128)(2,1)S(1)} %slice.271), channel_id=1, source_target_pairs={{0,2},{2,0},{4,6},{6,4},{8,10},{10,8},{12,14},{14,12},{16,18},{18,... | collective-permute-start | bytes 1671176 | tf_op jit(solution)/shard_map/ppermute | solution.py:20
  100.0 121.3 %copy-start.8 = (bf16[1536,1024]{1,0:T(8,128)(2,1)}, bf16[1536,1024]{1,0:T(8,128)(2,1)S(1)}, u32[]{:S(2)}) copy-start(bf16[1536,1024]{1,0:T(8,128)(2,1)S(1)} %pad_maximum_fusion.4.right_ref.d_down_ref) | copy-start | bytes 9437188
  100.0 26.7 %copy-start.28 = (bf16[1,768,1024]{2,1,0:T(8,128)(2,1)S(1)}, bf16[1,768,1024]{2,1,0:T(8,128)(2,1)}, u32[]{:S(2)}) copy-start(bf16[1,768,1024]{2,1,0:T(8,128)(2,1)} %param.11) | copy-start | bytes 4718596
  100.0 26.7 %copy-start.42 = (bf16[768,1024]{1,0:T(8,128)(2,1)S(1)}, bf16[768,1024]{1,0:T(8,128)(2,1)}, u32[]{:S(2)}) copy-start(bf16[768,1024]{1,0:T(8,128)(2,1)} %copy-done.41) | copy-start | bytes 4718596
  122.4 42.5 %collective-permute-start.18 = (bf16[16,64,512]{2,1,0:T(8,128)(2,1)}, bf16[16,64,512]{2,1,0:T(8,128)(2,1)}, u32[]{:S(2)}, u32[]{:S(2)}) collective-permute-start(bf16[16,64,512]{2,1,0:T(8,128)(2,1)} %bitcast.35), channel_id=1, source_target_pairs={{0,1},{1,0},{2,3},{3,2},{4,5},{5,4},{6,7},{7,6},{8,9},{9,8},{10,11... | collective-permute-start | bytes 3145736 | tf_op jit(solution)/shard_map/ppermute | solution.py:15
  130.0 41.8 %collective-permute-start.13 = (bf16[4,1,64,2304]{3,2,1,0:T(8,128)(2,1)}, bf16[4,1,64,2304]{3,2,1,0:T(8,128)(2,1)S(1)}, u32[]{:S(2)}, u32[]{:S(2)}) collective-permute-start(bf16[4,1,64,2304]{3,2,1,0:T(8,128)(2,1)} %bitcast.212), channel_id=1, source_target_pairs={{0,2},{2,0},{4,6},{6,4},{8,10},{10,8},{12,14},{14,12},{16,18},{18,... | collective-permute-start | bytes 3538952 | tf_op jit(solution)/shard_map/ppermute | solution.py:20
  130.4 41.5 %collective-permute-start.14 = (bf16[4,1,64,2304]{3,2,1,0:T(8,128)(2,1)}, bf16[4,1,64,2304]{3,2,1,0:T(8,128)(2,1)S(1)}, u32[]{:S(2)}, u32[]{:S(2)}) collective-permute-start(bf16[4,1,64,2304]{3,2,1,0:T(8,128)(2,1)} %bitcast.213), channel_id=1, source_target_pairs={{0,4},{2,6},{4,0},{6,2},{8,12},{10,14},{12,8},{14,10},{16,20},{18,... | collective-permute-start | bytes 3538952 | tf_op jit(solution)/shard_map/ppermute | solution.py:20
  146.2 12.1 %collective-permute-start.15 = (bf16[2,2,512]{2,1,0:T(2,128)(2,1)S(1)}, bf16[2,2,512]{2,1,0:T(2,128)(2,1)S(1)}, u32[]{:S(2)}, u32[]{:S(2)}) collective-permute-start(bf16[2,2,512]{2,1,0:T(2,128)(2,1)S(1)} %slice.348), channel_id=1, source_target_pairs={{0,2},{2,4},{4,6},{6,8},{8,10},{10,12},{12,14},{14,16},{16,18},{18... | collective-permute-start | bytes 12296 | tf_op jit(solution)/shard_map/ppermute | solution.py:26
  153.2 17.4 %collective-permute-start.22 = (bf16[2,1,64,2304]{3,2,1,0:T(8,128)(2,1)S(1)}, bf16[2,1,64,2304]{3,2,1,0:T(8,128)(2,1)S(1)}, u32[]{:S(2)}, u32[]{:S(2)}) collective-permute-start(bf16[2,1,64,2304]{3,2,1,0:T(8,128)(2,1)S(1)} %slice.306), channel_id=1, source_target_pairs={{0,4},{2,6},{4,0},{6,2},{8,12},{10,14},{12,8},{14,10},{16,20},{18,... | collective-permute-start | bytes 1769480 | tf_op jit(solution)/shard_map/ppermute | solution.py:20
  158.3 18.2 %collective-permute-start.23 = (bf16[2,1,64,2304]{3,2,1,0:T(8,128)(2,1)S(1)}, bf16[2,1,64,2304]{3,2,1,0:T(8,128)(2,1)S(1)}, u32[]{:S(2)}, u32[]{:S(2)}) collective-permute-start(bf16[2,1,64,2304]{3,2,1,0:T(8,128)(2,1)S(1)} %slice.307), channel_id=1, source_target_pairs={{0,2},{2,0},{4,6},{6,4},{8,10},{10,8},{12,14},{14,12},{16,18},{18,... | collective-permute-start | bytes 1769480 | tf_op jit(solution)/shard_map/ppermute | solution.py:20
  164.9 6.5 %collective-permute-start.17 = (bf16[768,512]{1,0:T(8,128)(2,1)S(1)}, bf16[768,512]{1,0:T(8,128)(2,1)S(1)}, u32[]{:S(2)}, u32[]{:S(2)}) collective-permute-start(bf16[768,512]{1,0:T(8,128)(2,1)S(1)} %slice.352), channel_id=1, source_target_pairs={{0,1},{1,0},{2,3},{3,2},{4,5},{5,4},{6,7},{7,6},{8,9},{9,8},{10,11... | collective-permute-start | bytes 2359304 | tf_op jit(solution)/shard_map/ppermute | solution.py:15
  175.5 17.8 %collective-permute-start.19 = (bf16[768,1024]{1,0:T(8,128)(2,1)S(1)}, bf16[768,1024]{1,0:T(8,128)(2,1)S(1)}, u32[]{:S(2)}, u32[]{:S(2)}) collective-permute-start(bf16[768,1024]{1,0:T(8,128)(2,1)S(1)} %multiply_convert_fusion), channel_id=1, source_target_pairs={{0,1},{1,0},{2,3},{3,2},{4,5},{5,4},{6,7},{7,6},{8,9},{9,8},{10,11... | collective-permute-start | bytes 4718600 | tf_op jit(solution)/shard_map/ppermute | solution.py:15
  177.5 14.6 %collective-permute-start.20 = (bf16[2,1,64,2304]{3,2,1,0:T(8,128)(2,1)S(1)}, bf16[2,1,64,2304]{3,2,1,0:T(8,128)(2,1)S(1)}, u32[]{:S(2)}, u32[]{:S(2)}) collective-permute-start(bf16[2,1,64,2304]{3,2,1,0:T(8,128)(2,1)S(1)} %slice.304), channel_id=1, source_target_pairs={{0,4},{2,6},{4,0},{6,2},{8,12},{10,14},{12,8},{14,10},{16,20},{18,... | collective-permute-start | bytes 1769480 | tf_op jit(solution)/shard_map/ppermute | solution.py:20
  178.9 14.4 %collective-permute-start.21 = (bf16[2,1,64,2304]{3,2,1,0:T(8,128)(2,1)S(1)}, bf16[2,1,64,2304]{3,2,1,0:T(8,128)(2,1)S(1)}, u32[]{:S(2)}, u32[]{:S(2)}) collective-permute-start(bf16[2,1,64,2304]{3,2,1,0:T(8,128)(2,1)S(1)} %slice.305), channel_id=1, source_target_pairs={{0,2},{2,0},{4,6},{6,4},{8,10},{10,8},{12,14},{14,12},{16,18},{18,... | collective-permute-start | bytes 1769480 | tf_op jit(solution)/shard_map/ppermute | solution.py:20
  234.3 23.3 %collective-permute-start.25 = (bf16[2,1,144,1024]{3,2,1,0:T(8,128)(2,1)S(1)}, bf16[2,1,144,1024]{3,2,1,0:T(8,128)(2,1)S(1)}, u32[]{:S(2)}, u32[]{:S(2)}) collective-permute-start(bf16[2,1,144,1024]{3,2,1,0:T(8,128)(2,1)S(1)} %get-tuple-element.125), channel_id=1, source_target_pairs={{0,2},{2,0},{4,6},{6,4},{8,10},{10,8},{12,14},{14,12},{16,18},{18,... | collective-permute-start | bytes 1769480 | tf_op jit(solution)/shard_map/ppermute | solution.py:20
  235.4 22.2 %collective-permute-start.26 = (bf16[2,1,144,1024]{3,2,1,0:T(8,128)(2,1)S(1)}, bf16[2,1,144,1024]{3,2,1,0:T(8,128)(2,1)S(1)}, u32[]{:S(2)}, u32[]{:S(2)}) collective-permute-start(bf16[2,1,144,1024]{3,2,1,0:T(8,128)(2,1)S(1)} %get-tuple-element.126), channel_id=1, source_target_pairs={{0,4},{2,6},{4,0},{6,2},{8,12},{10,14},{12,8},{14,10},{16,20},{18,... | collective-permute-start | bytes 1769480 | tf_op jit(solution)/shard_map/ppermute | solution.py:20
  260.0 40.4 %collective-permute-start.27 = (bf16[4,1,144,1024]{3,2,1,0:T(8,128)(2,1)}, bf16[4,1,144,1024]{3,2,1,0:T(8,128)(2,1)S(1)}, u32[]{:S(2)}, u32[]{:S(2)}) collective-permute-start(bf16[4,1,144,1024]{3,2,1,0:T(8,128)(2,1)} %pad_maximum_fusion.10), channel_id=1, source_target_pairs={{0,2},{2,0},{4,6},{6,4},{8,10},{10,8},{12,14},{14,12},{16,18},{18,... | collective-permute-start | bytes 3538952 | tf_op jit(solution)/shard_map/ppermute | solution.py:20
  260.4 40.0 %collective-permute-start.28 = (bf16[4,1,144,1024]{3,2,1,0:T(8,128)(2,1)}, bf16[4,1,144,1024]{3,2,1,0:T(8,128)(2,1)}, u32[]{:S(2)}, u32[]{:S(2)}) collective-permute-start(bf16[4,1,144,1024]{3,2,1,0:T(8,128)(2,1)} %pad_maximum_fusion.11), channel_id=1, source_target_pairs={{0,4},{2,6},{4,0},{6,2},{8,12},{10,14},{12,8},{14,10},{16,20},{18,... | collective-permute-start | bytes 3538952 | tf_op jit(solution)/shard_map/ppermute | solution.py:20
  272.8 42.2 %copy-start.4 = (bf16[1024,2304]{1,0:T(8,128)(2,1)}, bf16[1024,2304]{1,0:T(8,128)(2,1)S(1)}, u32[]{:S(2)}) copy-start(bf16[1024,2304]{1,0:T(8,128)(2,1)S(1)} %shard_map.191) | copy-start | bytes 14155780
  296.5 22.5 %collective-permute-start.33 = (f32[768,1024]{1,0:T(8,128)}, f32[768,1024]{1,0:T(8,128)S(1)}, u32[]{:S(2)}, u32[]{:S(2)}) collective-permute-start(f32[768,1024]{1,0:T(8,128)} %get-tuple-element.157), channel_id=1, source_target_pairs={{0,1},{1,0},{2,3},{3,2},{4,5},{5,4},{6,7},{7,6},{8,9},{9,8},{10,11... | collective-permute-start | bytes 9437192 | tf_op jit(solution)/shard_map/ppermute | solution.py:15
  299.0 15.8 %collective-permute-start.29 = (bf16[2,1,64,2304]{3,2,1,0:T(8,128)(2,1)}, bf16[2,1,64,2304]{3,2,1,0:T(8,128)(2,1)S(1)}, u32[]{:S(2)}, u32[]{:S(2)}) collective-permute-start(bf16[2,1,64,2304]{3,2,1,0:T(8,128)(2,1)} %get-tuple-element.147), channel_id=1, source_target_pairs={{0,2},{2,0},{4,6},{6,4},{8,10},{10,8},{12,14},{14,12},{16,18},{18,... | collective-permute-start | bytes 1769480 | tf_op jit(solution)/shard_map/ppermute | solution.py:20
  300.1 14.9 %collective-permute-start.30 = (bf16[2,1,64,2304]{3,2,1,0:T(8,128)(2,1)}, bf16[2,1,64,2304]{3,2,1,0:T(8,128)(2,1)}, u32[]{:S(2)}, u32[]{:S(2)}) collective-permute-start(bf16[2,1,64,2304]{3,2,1,0:T(8,128)(2,1)} %get-tuple-element.148), channel_id=1, source_target_pairs={{0,4},{2,6},{4,0},{6,2},{8,12},{10,14},{12,8},{14,10},{16,20},{18,... | collective-permute-start | bytes 1769480 | tf_op jit(solution)/shard_map/ppermute | solution.py:20
  327.9 4.8 collective-permute-start.34
  331.5 7.7 %collective-permute-start.35 = (f32[768,512]{1,0:T(8,128)S(1)}, f32[768,512]{1,0:T(8,128)}, u32[]{:S(2)}, u32[]{:S(2)}) collective-permute-start(f32[768,512]{1,0:T(8,128)S(1)} %get-tuple-element.299), channel_id=1, source_target_pairs={{0,1},{1,0},{2,3},{3,2},{4,5},{5,4},{6,7},{7,6},{8,9},{9,8},{10,11... | collective-permute-start | bytes 4718600 | tf_op jit(solution)/shard_map/ppermute | solution.py:15
  331.6 143.6 %reduce-scatter.7.cloned.1.call-start = ((), (), s32[]{:S(2)}) async-start(), calls=%async_computation.9 | async-start | bytes 1474560 | tf_op jit(solution)/shard_map/reduce_scatter | solution.py:135
  331.6 27.4 %collective-permute-start.31 = (bf16[4,1,64,2304]{3,2,1,0:T(8,128)(2,1)}, bf16[4,1,64,2304]{3,2,1,0:T(8,128)(2,1)}, u32[]{:S(2)}, u32[]{:S(2)}) collective-permute-start(bf16[4,1,64,2304]{3,2,1,0:T(8,128)(2,1)} %pad_maximum_fusion.12), channel_id=1, source_target_pairs={{0,2},{2,0},{4,6},{6,4},{8,10},{10,8},{12,14},{14,12},{16,18},{18,... | collective-permute-start | bytes 3538952 | tf_op jit(solution)/shard_map/ppermute | solution.py:20
  332.1 27.0 %collective-permute-start.32 = (bf16[4,1,64,2304]{3,2,1,0:T(8,128)(2,1)}, bf16[4,1,64,2304]{3,2,1,0:T(8,128)(2,1)}, u32[]{:S(2)}, u32[]{:S(2)}) collective-permute-start(bf16[4,1,64,2304]{3,2,1,0:T(8,128)(2,1)} %pad_maximum_fusion.13), channel_id=1, source_target_pairs={{0,4},{2,6},{4,0},{6,2},{8,12},{10,14},{12,8},{14,10},{16,20},{18,... | collective-permute-start | bytes 3538952 | tf_op jit(solution)/shard_map/ppermute | solution.py:20
  347.5 18.7 %copy-start.53 = (bf16[2,1,64,2816]{3,2,1,0:T(8,128)(2,1)S(1)}, bf16[2,1,64,2816]{3,2,1,0:T(8,128)(2,1)}, u32[]{:S(2)}) copy-start(bf16[2,1,64,2816]{3,2,1,0:T(8,128)(2,1)} %get-tuple-element.165) | copy-start | bytes 2162692
  359.2 7.9 %collective-permute-start.38 = (f32[2,2,512]{2,1,0:T(2,128)S(1)}, f32[2,2,512]{2,1,0:T(2,128)S(1)}, u32[]{:S(2)}, u32[]{:S(2)}) collective-permute-start(f32[2,2,512]{2,1,0:T(2,128)S(1)} %maximum_multiply_fusion), channel_id=1, source_target_pairs={{2,0},{4,2},{6,4},{8,6},{10,8},{12,10},{14,12},{16,14},{18,16},{20... | collective-permute-start | bytes 24584 | tf_op jit(solution)/shard_map/ppermute | solution.py:26
  364.1 16.6 %collective-permute-start.36 = (bf16[2,1,64,2816]{3,2,1,0:T(8,128)(2,1)S(1)}, bf16[2,1,64,2816]{3,2,1,0:T(8,128)(2,1)S(1)}, u32[]{:S(2)}, u32[]{:S(2)}) collective-permute-start(bf16[2,1,64,2816]{3,2,1,0:T(8,128)(2,1)S(1)} %copy-done.54), channel_id=1, source_target_pairs={{0,2},{2,0},{4,6},{6,4},{8,10},{10,8},{12,14},{14,12},{16,18},{18,... | collective-permute-start | bytes 2162696 | tf_op jit(solution)/shard_map/ppermute | solution.py:20
  366.2 15.4 %collective-permute-start.37 = (bf16[2,1,64,2816]{3,2,1,0:T(8,128)(2,1)S(1)}, bf16[2,1,64,2816]{3,2,1,0:T(8,128)(2,1)S(1)}, u32[]{:S(2)}, u32[]{:S(2)}) collective-permute-start(bf16[2,1,64,2816]{3,2,1,0:T(8,128)(2,1)S(1)} %copy-done.53), channel_id=1, source_target_pairs={{0,4},{2,6},{4,0},{6,2},{8,12},{10,14},{12,8},{14,10},{16,20},{18,... | collective-permute-start | bytes 2162696 | tf_op jit(solution)/shard_map/ppermute | solution.py:20
  395.5 17.5 %collective-permute-start.41 = (f32[768,1024]{1,0:T(8,128)}, f32[768,1024]{1,0:T(8,128)}, u32[]{:S(2)}, u32[]{:S(2)}) collective-permute-start(f32[768,1024]{1,0:T(8,128)} %get-tuple-element.173), channel_id=1, source_target_pairs={{0,1},{1,0},{2,3},{3,2},{4,5},{5,4},{6,7},{7,6},{8,9},{9,8},{10,11... | collective-permute-start | bytes 9437192 | tf_op jit(solution)/shard_map/ppermute | solution.py:15
  399.1 77.1 %reduce-scatter.9.cloned.1.call-start = ((), (), s32[]{:S(2)}) async-start(), calls=%async_computation.10 | async-start | bytes 1802240 | tf_op jit(solution)/shard_map/reduce_scatter | solution.py:135
  402.8 33.6 %collective-permute-start.39 = (bf16[4,1,64,2816]{3,2,1,0:T(8,128)(2,1)}, bf16[4,1,64,2816]{3,2,1,0:T(8,128)(2,1)}, u32[]{:S(2)}, u32[]{:S(2)}) collective-permute-start(bf16[4,1,64,2816]{3,2,1,0:T(8,128)(2,1)} %pad_maximum_fusion.8), channel_id=1, source_target_pairs={{0,2},{2,0},{4,6},{6,4},{8,10},{10,8},{12,14},{14,12},{16,18},{18,... | collective-permute-start | bytes 4325384 | tf_op jit(solution)/shard_map/ppermute | solution.py:20
  403.7 33.2 %collective-permute-start.40 = (bf16[4,1,64,2816]{3,2,1,0:T(8,128)(2,1)}, bf16[4,1,64,2816]{3,2,1,0:T(8,128)(2,1)}, u32[]{:S(2)}, u32[]{:S(2)}) collective-permute-start(bf16[4,1,64,2816]{3,2,1,0:T(8,128)(2,1)} %pad_maximum_fusion.9), channel_id=1, source_target_pairs={{0,4},{2,6},{4,0},{6,2},{8,12},{10,14},{12,8},{14,10},{16,20},{18,... | collective-permute-start | bytes 4325384 | tf_op jit(solution)/shard_map/ppermute | solution.py:20
  419.1 19.6 %slice-start.2 = ((s8[4718592]{0:T(1024)(128)(4,1)}), s8[4194304]{0:T(1024)(128)(4,1)S(1)}, s32[]{:S(2)}) async-start(s8[4718592]{0:T(1024)(128)(4,1)} %bitcast.172), calls=%async_computation.14 | async-start | bytes 8388608
  436.9 10.5 %collective-permute-start.42 = (bf16[2,1,64,1664]{3,2,0,1:T(8,128)(2,1)}, bf16[2,1,64,1664]{3,2,0,1:T(8,128)(2,1)}, u32[]{:S(2)}, u32[]{:S(2)}) collective-permute-start(bf16[2,1,64,1664]{3,2,0,1:T(8,128)(2,1)} %get-tuple-element.183), channel_id=1, source_target_pairs={{0,2},{2,0},{4,6},{6,4},{8,10},{10,8},{12,14},{14,12},{16,18},{18,... | collective-permute-start | bytes 1277960 | tf_op jit(solution)/shard_map/ppermute | solution.py:20
  437.6 10.2 %collective-permute-start.43 = (bf16[2,1,64,1664]{3,2,0,1:T(8,128)(2,1)}, bf16[2,1,64,1664]{3,2,0,1:T(8,128)(2,1)}, u32[]{:S(2)}, u32[]{:S(2)}) collective-permute-start(bf16[2,1,64,1664]{3,2,0,1:T(8,128)(2,1)} %get-tuple-element.184), channel_id=1, source_target_pairs={{0,4},{2,6},{4,0},{6,2},{8,12},{10,14},{12,8},{14,10},{16,20},{18,... | collective-permute-start | bytes 1277960 | tf_op jit(solution)/shard_map/ppermute | solution.py:20
  442.2 59.0 %reduce-scatter.11.cloned.1.call-start = ((), (), s32[]{:S(2)}) async-start(), calls=%async_computation.11 | async-start | bytes 1064960 | tf_op jit(solution)/shard_map/reduce_scatter | solution.py:135
  450.4 10.1 %collective-permute-start.46 = (bf16[768,1024]{1,0:T(8,128)(2,1)S(1)}, bf16[768,1024]{1,0:T(8,128)(2,1)S(1)}, u32[]{:S(2)}, u32[]{:S(2)}) collective-permute-start(bf16[768,1024]{1,0:T(8,128)(2,1)S(1)} %copy-done.23), channel_id=1, source_target_pairs={{0,1},{1,0},{2,3},{3,2},{4,5},{5,4},{6,7},{7,6},{8,9},{9,8},{10,11... | collective-permute-start | bytes 4718600 | tf_op jit(solution)/shard_map/ppermute | solution.py:15
  452.7 20.6 %collective-permute-start.44 = (bf16[4,1,64,1664]{3,2,0,1:T(8,128)(2,1)S(1)}, bf16[4,1,64,1664]{3,2,0,1:T(8,128)(2,1)S(1)}, u32[]{:S(2)}, u32[]{:S(2)}) collective-permute-start(bf16[4,1,64,1664]{3,2,0,1:T(8,128)(2,1)S(1)} %pad_maximum_fusion.15), channel_id=1, source_target_pairs={{0,2},{2,0},{4,6},{6,4},{8,10},{10,8},{12,14},{14,12},{16,18},{18,... | collective-permute-start | bytes 2555912 | tf_op jit(solution)/shard_map/ppermute | solution.py:20
  453.6 20.2 %collective-permute-start.45 = (bf16[4,1,64,1664]{3,2,0,1:T(8,128)(2,1)S(1)}, bf16[4,1,64,1664]{3,2,0,1:T(8,128)(2,1)S(1)}, u32[]{:S(2)}, u32[]{:S(2)}) collective-permute-start(bf16[4,1,64,1664]{3,2,0,1:T(8,128)(2,1)S(1)} %pad_maximum_fusion.16), channel_id=1, source_target_pairs={{0,4},{2,6},{4,0},{6,2},{8,12},{10,14},{12,8},{14,10},{16,20},{18,... | collective-permute-start | bytes 2555912 | tf_op jit(solution)/shard_map/ppermute | solution.py:20
  477.2 5.2 %collective-permute-start.48 = (bf16[32,2304]{1,0:T(8,128)(2,1)S(1)}, bf16[32,2304]{1,0:T(8,128)(2,1)S(1)}, u32[]{:S(2)}, u32[]{:S(2)}) collective-permute-start(bf16[32,2304]{1,0:T(8,128)(2,1)S(1)} %broadcast_select_fusion.14), channel_id=1, source_target_pairs={{0,1},{1,0},{2,3},{3,2},{4,5},{5,4},{6,7},{7,6},{8,9},{9,8},{10,11... | collective-permute-start | bytes 442376 | tf_op jit(solution)/shard_map/ppermute | solution.py:15
  479.9 8.5 %collective-permute-start.49 = (bf16[32,2304]{1,0:T(8,128)(2,1)S(1)}, bf16[32,2304]{1,0:T(8,128)(2,1)S(1)}, u32[]{:S(2)}, u32[]{:S(2)}) collective-permute-start(bf16[32,2304]{1,0:T(8,128)(2,1)S(1)} %broadcast_select_fusion.10), channel_id=1, source_target_pairs={{0,1},{1,0},{2,3},{3,2},{4,5},{5,4},{6,7},{7,6},{8,9},{9,8},{10,11... | collective-permute-start | bytes 442376 | tf_op jit(solution)/shard_map/ppermute | solution.py:15
  502.1 4.7 collective-permute-start.47
  (61 other events, 422.7 us)
Sparse Core Ops, SparseCore 0:
  17.7 30.9 all-gather.4
  50.8 29.5 all-gather.6
  82.5 29.5 all-gather.8
  113.6 89.1 all-gather.10
  331.7 27.1 reduce-scatter.4
  399.2 28.2 reduce-scatter.6
  442.3 33.8 reduce-scatter.8
  478.5 22.5 reduce-scatter.10

commit v4 on v3

--- a/solution.py
+++ b/solution.py
@@ -174,7 +174,7 @@
         in_specs=ins,
         out_specs=[spec for _, spec in outs],
         out_shape=[shape for shape, _ in outs],
-        compiler_params=pltpu.CompilerParams(vmem_limit_bytes=44 * 1024 * 1024),
+        compiler_params=pltpu.CompilerParams(vmem_limit_bytes=32 * 1024 * 1024),
         cost_estimate=pl.CostEstimate(
             flops=flops, bytes_accessed=flops // 500, transcendentals=0
         ),

time: 527 us -> 531 us (level)
  local copies, waits for them, and re-layouts: 84.1 us -> 111 us
  Pallas kernels: 136 us -> 116 us
  other arithmetic: 93.5 us -> 87 us
    unnamed x138 -> x160, local copies, waits for them, and re-layouts: 19.9 us -> 44.1 us
    pallas_call x11, Pallas kernels: 136 us -> 116 us  [call(): pl.pallas_call(body, grid=(grid,), in_specs=ins, out_specs=[spec for _, s...]
  transfers between devices with their start and end apart: 58 -> 58, of which waited for: 23 -> 22; matrix products, arithmetic and copies ran while one was open for 28% -> 26% of each run, Pallas kernels for 26% -> 22%
where the time goes in v4:
time: 531 us; the launch traced here: 523 us
  waiting for transfers between devices  129 us (24%)
  Pallas kernels  116 us (22%)
  local copies, waits for them, and re-layouts  111 us (21%)
  other arithmetic  87 us (16%)
  starting transfers between devices  58 us (11%)
  between operations  16.7 us (3%)
  matrix products  5.63 us (1%)
    pallas_call x11, Pallas kernels, call(): pl.pallas_call(body, grid=(grid,), in_specs=ins, out_specs=[spec for _, s...  116 us
    ppermute x32, waiting for transfers between devices, across(): return lax.ppermute(x, 'seq', [(i, i ^ bit) for i in range(peers)])  83 us
    unnamed x160, local copies, waits for them, and re-layouts  44.1 us
    ppermute x32, starting transfers between devices, across(): return lax.ppermute(x, 'seq', [(i, i ^ bit) for i in range(peers)])  33.9 us
    all_gather x4, waiting for transfers between devices, line_gather(): lax.all_gather(shard, 'seq', axis_index_groups=columns_of_line(peers), ax...  28.4 us
    ppermute x16, starting transfers between devices, swap_cores(): return lax.ppermute(x, 'fsdp', [(0, 1), (1, 0)])  18.4 us
    reduce_scatter x4, waiting for transfers between devices, landed(): lax.psum_scatter(mine.reshape(self.depth * self.rows, self.cols), 'seq',...  12.6 us
    convert_element_type x4, other arithmetic, landed(): mine = (self.piece(0, 0, self.depth).astype(F32) + from_x.astype(F32) + f...  11.2 us
  transfers between devices with their start and end apart: 58, of which 22 were waited for; matrix products, arithmetic and copies ran while one was open for 26% of the time, Pallas kernels for 22%

profile of v4, /device:TPU:1, one launch (start us, length us, event | category | flops | bytes accessed | tf_op | source)
XLA Modules:
  0.0 522.9 jit_solution(13898688416125978595)
XLA Ops:
  14.3 2.3 fusion.56
  21.3 2.2 collective-permute-done.16
  24.0 2.4 collective-permute-start.1
  31.2 2.6 collective-permute-done.1
  42.4 6.3 %all-gather.5.cloned.1.call-done = bf16[256,2176]{1,0:T(8,128)(2,1)} async-done(((bf16[64,2176]{1,0:T(8,128)(2,1)}), bf16[256,2176]{1,0:T(8,128)(2,1)}) %all-gather.5.cloned.1.call-update) | async-done | bytes 1114128 | tf_op jit(solution)/shard_map/all_gather | solution.py:43
  58.3 22.1 %all-gather.7.cloned.1.call-done = bf16[256,2304]{1,0:T(8,128)(2,1)} async-done(((bf16[64,2304]{1,0:T(8,128)(2,1)}), bf16[256,2304]{1,0:T(8,128)(2,1)}) %all-gather.7.cloned.1.call-update) | async-done | bytes 1179664 | tf_op jit(solution)/shard_map/all_gather | solution.py:43
  92.8 2.9 broadcast.83.clone
  97.6 2.2 pad_maximum_fusion.4.right_ref.d_down_ref
  99.9 20.2 %collective-permute-done.11 = bf16[2,1,64,2176]{3,2,0,1:T(8,128)(2,1)S(1)} collective-permute-done((bf16[2,1,64,2176]{3,2,0,1:T(8,128)(2,1)S(1)}, bf16[2,1,64,2176]{3,2,0,1:T(8,128)(2,1)S(1)}, u32[]{:S(2)}, u32[]{:S(2)}) %collective-permute-start.11) | collective-permute-done | bytes 557088 | tf_op jit(solution)/shard_map/ppermute | solution.py:20
  122.5 2.5 collective-permute-start.18
  126.7 3.3 fusion.2.left_ref
  135.4 5.9 %shard_map.186 = f32[1536,1536]{1,0:T(8,128)S(1)} custom-call(bf16[1536,1024]{1,0:T(8,128)(2,1)S(1)} %copy-done.20, bf16[1024,1536]{1,0:T(8,128)(2,1)S(1)} %bitcast.188), custom_call_target="tpu_custom_call" | custom-call | flops 38654705664 | bytes 77309408 | tf_op jit(solution)/shard_map/pallas_call | solution.py:171
  141.9 3.4 collective-permute-start.15
  147.2 2.5 constant_dynamic-update-slice_fusion.8
  150.4 2.5 constant_dynamic-update-slice_fusion.7
  156.1 2.3 collective-permute-start.23
  164.7 6.0 %collective-permute-done.22 = bf16[2,1,64,2304]{3,2,1,0:T(8,128)(2,1)} collective-permute-done((bf16[2,1,64,2304]{3,2,1,0:T(8,128)(2,1)}, bf16[2,1,64,2304]{3,2,1,0:T(8,128)(2,1)}, u32[]{:S(2)}, u32[]{:S(2)}) %collective-permute-start.22) | collective-permute-done | bytes 589856 | tf_op jit(solution)/shard_map/ppermute | solution.py:20
  170.6 2.0 constant_dynamic-update-slice_fusion.6
  181.5 11.8 %collective-permute-done.20 = bf16[2,1,64,2304]{3,2,1,0:T(8,128)(2,1)S(1)} collective-permute-done((bf16[2,1,64,2304]{3,2,1,0:T(8,128)(2,1)S(1)}, bf16[2,1,64,2304]{3,2,1,0:T(8,128)(2,1)S(1)}, u32[]{:S(2)}, u32[]{:S(2)}) %collective-permute-start.20) | collective-permute-done | bytes 589856 | tf_op jit(solution)/shard_map/ppermute | solution.py:20
  194.8 11.2 %shard_map.187.gate_ref = bf16[1536,2304]{1,0:T(8,128)(2,1)S(1)} custom-call(bf16[1536,1024]{1,0:T(8,128)(2,1)S(1)} %pad_maximum_fusion.3.hidden_ref.left_ref, bf16[1024,2304]{1,0:T(8,128)(2,1)} %bitcast.43.weight_ref.refs_2_), custom_call_target="tpu_custom_call" | custom-call | flops 7247757312 | bytes 14495514 | tf_op jit(solution)/shard_map/pallas_call | solution.py:171
  206.0 2.9 copy-done.31
  208.9 11.8 %shard_map.188 = (bf16[1536,2304]{1,0:T(8,128)(2,1)S(1)}, bf16[1536,2304]{1,0:T(8,128)(2,1)S(1)}) custom-call(bf16[1536,1024]{1,0:T(8,128)(2,1)S(1)} %pad_maximum_fusion.3.hidden_ref.left_ref, bf16[1024,2304]{1,0:T(8,128)(2,1)S(1)} %bitcast.186, bf16[1536,2304]{1,0:T(8,128)(2,1)} %copy-done.31), custom_call_target="tpu_custom_call" | custom-call | flops 7247757312 | bytes 14495514 | tf_op jit(solution)/shard_map/pallas_call | solution.py:171
  220.7 2.9 copy-done.32
  223.6 9.6 %shard_map.189 = bf16[2304,1024]{1,0:T(8,128)(2,1)S(1)} custom-call(bf16[1536,2304]{1,0:T(8,128)(2,1)S(1)} %get-tuple-element.177.left_ref.refs_0_, bf16[1536,1024]{1,0:T(8,128)(2,1)S(1)} %pad_maximum_fusion.4.right_ref.d_down_ref), custom_call_target="tpu_custom_call" | custom-call | flops 7247757312 | bytes 14495514 | tf_op jit(solution)/shard_map/pallas_call | solution.py:171
  233.3 2.1 copy-done.6
  239.7 2.3 copy-done.24
  242.1 14.8 %shard_map.190 = (bf16[1536,2304]{1,0:T(8,128)(2,1)S(1)}, bf16[1536,2304]{1,0:T(8,128)(2,1)S(1)}) custom-call(bf16[1536,1024]{1,0:T(8,128)(2,1)S(1)} %copy-done.13, bf16[2304,1024]{1,0:T(8,128)(2,1)S(1)} %copy-done.24, bf16[1536,2304]{1,0:T(8,128)(2,1)} %copy-done.31, bf16[1536,2304]{1,0:T(8,128)(2,1)} %copy-done.32), custom_call_target="tpu_custom_call" | custom-call | flops 7247757312 | bytes 14495514 | tf_op jit(solution)/shard_map/pallas_call | solution.py:171
  256.9 2.9 copy-done.29
  263.8 10.4 %shard_map.191 = bf16[1024,2304]{1,0:T(8,128)(2,1)S(1)} custom-call(bf16[1536,1024]{1,0:T(8,128)(2,1)S(1)} %copy-done.15, bf16[1536,2304]{1,0:T(8,128)(2,1)S(1)} %get-tuple-element.140.right_ref.refs_0_), custom_call_target="tpu_custom_call" | custom-call | flops 7247757312 | bytes 14495514 | tf_op jit(solution)/shard_map/pallas_call | solution.py:171
  275.4 3.2 copy-done.11
  278.5 18.8 %shard_map.192 = (f32[768,1024]{1,0:T(8,128)S(1)}, f32[768,1024]{1,0:T(8,128)S(1)}) custom-call(bf16[1536,2304]{1,0:T(8,128)(2,1)S(1)} %get-tuple-element.140.right_ref.refs_0_, bf16[1536,2304]{1,0:T(8,128)(2,1)} %copy-done.29, bf16[1024,2304]{1,0:T(8,128)(2,1)} %bitcast.43.weight_ref.refs_2_, bf16[1024,2304]{1,0:T(8,128)(2,1)S(1)} %bitcast.187), custom_call_target="tpu_custom_call" | custom-call | flops 14495514624 | bytes 28991028 | tf_op jit(solution)/shard_map/pallas_call | solution.py:171
  299.1 2.6 collective-permute-start.33
  303.2 3.0 add_convert_fusion.3
  306.2 3.0 copy-done.30
  309.2 10.5 %shard_map.193 = bf16[1024,2304]{1,0:T(8,128)(2,1)S(1)} custom-call(bf16[1536,1024]{1,0:T(8,128)(2,1)S(1)} %copy-done.16, bf16[1536,2304]{1,0:T(8,128)(2,1)S(1)} %copy-done.30), custom_call_target="tpu_custom_call" | custom-call | flops 7247757312 | bytes 14495514 | tf_op jit(solution)/shard_map/pallas_call | solution.py:171
  323.9 2.8 multiply_reduce_fusion.3
  326.8 3.4 multiply_add_fusion
  332.1 2.1 copy-done.51
  339.9 3.3 fusion.20
  343.5 3.1 fusion.32
  346.5 3.5 pad_maximum_fusion.5
  350.1 4.7 multiply_reduce_fusion
  354.9 10.8 %collective-permute-done.31 = bf16[4,1,64,2304]{3,2,1,0:T(8,128)(2,1)} collective-permute-done((bf16[4,1,64,2304]{3,2,1,0:T(8,128)(2,1)}, bf16[4,1,64,2304]{3,2,1,0:T(8,128)(2,1)}, u32[]{:S(2)}, u32[]{:S(2)}) %collective-permute-start.31) | collective-permute-done | bytes 1179680 | tf_op jit(solution)/shard_map/ppermute | solution.py:20
  367.3 3.4 add_convert_fusion.2
  370.7 2.1 collective-permute-start.36
  376.8 10.6 %collective-permute-done.36 = bf16[2,1,64,2816]{3,2,1,0:T(8,128)(2,1)S(1)} collective-permute-done((bf16[2,1,64,2816]{3,2,1,0:T(8,128)(2,1)S(1)}, bf16[2,1,64,2816]{3,2,1,0:T(8,128)(2,1)S(1)}, u32[]{:S(2)}, u32[]{:S(2)}) %collective-permute-start.36) | collective-permute-done | bytes 720928 | tf_op jit(solution)/shard_map/ppermute | solution.py:20
  391.3 7.4 %shard_map.194 = (f32[768,1024]{1,0:T(8,128)S(1)}, f32[768,1024]{1,0:T(8,128)}) custom-call(bf16[1536,1536]{1,0:T(8,128)(2,1)S(1)} %pad_maximum_fusion.refs_0_.right_ref, bf16[1024,1536]{1,0:T(8,128)(2,1)S(1)} %bitcast.189), custom_call_target="tpu_custom_call" | custom-call | flops 4831838208 | bytes 9663676 | tf_op jit(solution)/shard_map/pallas_call | solution.py:171
  400.5 3.1 collective-permute-start.41
  404.1 3.6 multiply_reduce_fusion.2
  410.1 2.0 copy-done.21
  412.1 6.9 %shard_map.195 = bf16[1024,1536]{1,0:T(8,128)(2,1)S(1)} custom-call(bf16[1536,1024]{1,0:T(8,128)(2,1)S(1)} %copy-done.21, bf16[1536,1536]{1,0:T(8,128)(2,1)S(1)} %copy-done.9), custom_call_target="tpu_custom_call" | custom-call | flops 4831838208 | bytes 9663676 | tf_op jit(solution)/shard_map/pallas_call | solution.py:171
  419.0 2.9 fusion.8
  425.1 2.5 copy-done.25
  427.6 3.3 copy-done.34
  430.9 8.6 %shard_map.196 = (f32[768,1024]{1,0:T(8,128)S(1)}, bf16[768,1024]{1,0:T(8,128)(2,1)S(1)}) custom-call(bf16[1536,2304]{1,0:T(8,128)(2,1)S(1)} %copy-done.34, bf16[2304,1024]{1,0:T(8,128)(2,1)S(1)} %copy-done.25), custom_call_target="tpu_custom_call" | custom-call | flops 7247757312 | bytes 14495514 | tf_op jit(solution)/shard_map/pallas_call | solution.py:171
  443.7 3.5 add_convert_fusion.1
  447.5 4.9 collective-permute-done.42
  455.3 2.4 collective-permute-start.46
  460.1 5.4 %fusion.12 = f32[1,768,1024]{2,1,0:T(8,128)} fusion(f32[768,1024]{1,0:T(8,128)} %copy-done.50, f32[768]{0:T(1024)S(1)} %broadcast_multiply_fusion, f32[1024]{0:T(1024)S(1)} %copy-done.70, f32[768]{0:T(1024)S(1)} %add_rsqrt_fusion.1, bf16[1,768,1024]{2,1,0:T(8,128)(2,1)S(1)} %copy-done.43, f32[768,1024]{1,0:T(8,128)S(1)} %copy-done.4, ...), kind=kLoop, calls=%fused_computation.41 | loop fusion | flops 6291456 | bytes 14166016 | tf_op jit(solution)/shard_map/broadcast_in_dim | solution.py:650
  465.5 2.1 fusion.21
  467.6 10.7 %collective-permute-done.44 = bf16[4,1,64,1664]{3,2,0,1:T(8,128)(2,1)S(1)} collective-permute-done((bf16[4,1,64,1664]{3,2,0,1:T(8,128)(2,1)S(1)}, bf16[4,1,64,1664]{3,2,0,1:T(8,128)(2,1)S(1)}, u32[]{:S(2)}, u32[]{:S(2)}) %collective-permute-start.44) | collective-permute-done | bytes 852000 | tf_op jit(solution)/shard_map/ppermute | solution.py:20
  492.0 2.1 reshape.193
  495.8 11.0 %reduce-scatter.11.cloned.1.call-done = bf16[64,1664]{1,0:T(8,128)(2,1)} async-done(((bf16[256,1664]{1,0:T(8,128)(2,1)}), bf16[64,1664]{1,0:T(8,128)(2,1)}) %reduce-scatter.11.cloned.1.call-update) | async-done | bytes 213008 | tf_op jit(solution)/shard_map/reduce_scatter | solution.py:135
  510.4 2.1 reshape.194
  (400 shorter events, 154.7 us)
Async XLA Ops:
  7.2 41.5 %all-gather.5.cloned.1.call-start = ((), (), s32[]{:S(2)}) async-start(), calls=%async_computation.4 | async-start | bytes 1392640 | tf_op jit(solution)/shard_map/all_gather | solution.py:43
  10.2 1.4 collective-permute-start
  17.3 1.6 collective-permute-start.7
  17.6 62.8 %all-gather.7.cloned.1.call-start = ((), (), s32[]{:S(2)}) async-start(), calls=%async_computation.5 | async-start | bytes 1474560 | tf_op jit(solution)/shard_map/all_gather | solution.py:43
  19.9 110.2 %all-gather.9.cloned.1.call-start = ((), (), s32[]{:S(2)}) async-start(), calls=%async_computation.6 | async-start | bytes 1474560 | tf_op jit(solution)/shard_map/all_gather | solution.py:43
  20.0 20.1 %collective-permute-start.10 = (bf16[768,1024]{1,0:T(8,128)(2,1)S(1)}, bf16[768,1024]{1,0:T(8,128)(2,1)S(1)}, u32[]{:S(2)}, u32[]{:S(2)}) collective-permute-start(bf16[768,1024]{1,0:T(8,128)(2,1)S(1)} %bitcast.190), channel_id=1, source_target_pairs={{0,1},{1,0},{2,3},{3,2},{4,5},{5,4},{6,7},{7,6},{8,9},{9,8},{10,11... | collective-permute-start | bytes 4718600 | tf_op jit(solution)/shard_map/ppermute | solution.py:15
  20.9 2.6 collective-permute-start.16
  24.0 9.8 %collective-permute-start.1 = (bf16[1,1,144,1024]{3,2,1,0:T(8,128)(2,1)}, bf16[1,1,144,1024]{3,2,1,0:T(8,128)(2,1)S(1)}, u32[]{:S(2)}, u32[]{:S(2)}) collective-permute-start(bf16[1,1,144,1024]{3,2,1,0:T(8,128)(2,1)} %bitcast.5), channel_id=1, source_target_pairs={{0,2},{2,0},{4,6},{6,4},{8,10},{10,8},{12,14},{14,12},{16,18},{18,... | collective-permute-start | bytes 884744 | tf_op jit(solution)/shard_map/ppermute | solution.py:20
  26.3 9.3 %collective-permute-start.3 = (bf16[1,1,144,1024]{3,2,1,0:T(8,128)(2,1)}, bf16[1,1,144,1024]{3,2,1,0:T(8,128)(2,1)S(1)}, u32[]{:S(2)}, u32[]{:S(2)}) collective-permute-start(bf16[1,1,144,1024]{3,2,1,0:T(8,128)(2,1)} %bitcast.5), channel_id=1, source_target_pairs={{0,4},{2,6},{4,0},{6,2},{8,12},{10,14},{12,8},{14,10},{16,20},{18,... | collective-permute-start | bytes 884744 | tf_op jit(solution)/shard_map/ppermute | solution.py:20
  34.4 7.9 %collective-permute-start.2 = (bf16[1,1,64,1024]{3,2,1,0:T(8,128)(2,1)}, bf16[1,1,64,1024]{3,2,1,0:T(8,128)(2,1)}, u32[]{:S(2)}, u32[]{:S(2)}) collective-permute-start(bf16[1,1,64,1024]{3,2,1,0:T(8,128)(2,1)} %slice.336), channel_id=1, source_target_pairs={{0,4},{2,6},{4,0},{6,2},{8,12},{10,14},{12,8},{14,10},{16,20},{18,... | collective-permute-start | bytes 393224 | tf_op jit(solution)/shard_map/ppermute | solution.py:20
  36.3 6.1 %collective-permute-start.4 = (bf16[1,1,80,1024]{3,2,1,0:T(8,128)(2,1)}, bf16[1,1,80,1024]{3,2,1,0:T(8,128)(2,1)}, u32[]{:S(2)}, u32[]{:S(2)}) collective-permute-start(bf16[1,1,80,1024]{3,2,1,0:T(8,128)(2,1)} %slice.337), channel_id=1, source_target_pairs={{0,2},{2,0},{4,6},{6,4},{8,10},{10,8},{12,14},{14,12},{16,18},{18,... | collective-permute-start | bytes 491528 | tf_op jit(solution)/shard_map/ppermute | solution.py:20
  37.5 200.3 %all-gather.11.cloned.1.call-start = ((), (), s32[]{:S(2)}) async-start(), calls=%async_computation.7 | async-start | bytes 5898240 | tf_op jit(solution)/shard_map/all_gather | solution.py:43
  40.0 57.6 %collective-permute-start.24 = (bf16[768,1024]{1,0:T(8,128)(2,1)}, bf16[768,1024]{1,0:T(8,128)(2,1)}, u32[]{:S(2)}, u32[]{:S(2)}) collective-permute-start(bf16[768,1024]{1,0:T(8,128)(2,1)} %bitcast.44), channel_id=1, source_target_pairs={{0,1},{1,0},{2,3},{3,2},{4,5},{5,4},{6,7},{7,6},{8,9},{9,8},{10,11... | collective-permute-start | bytes 4718600 | tf_op jit(solution)/shard_map/ppermute | solution.py:15
  48.7 32.0 %collective-permute-start.5 = (bf16[4,1,64,2176]{3,2,0,1:T(8,128)(2,1)}, bf16[4,1,64,2176]{3,2,0,1:T(8,128)(2,1)}, u32[]{:S(2)}, u32[]{:S(2)}) collective-permute-start(bf16[4,1,64,2176]{3,2,0,1:T(8,128)(2,1)} %bitcast.218), channel_id=1, source_target_pairs={{0,2},{2,0},{4,6},{6,4},{8,10},{10,8},{12,14},{14,12},{16,18},{18,... | collective-permute-start | bytes 3342344 | tf_op jit(solution)/shard_map/ppermute | solution.py:20
  49.9 30.8 %collective-permute-start.6 = (bf16[4,1,64,2176]{3,2,0,1:T(8,128)(2,1)}, bf16[4,1,64,2176]{3,2,0,1:T(8,128)(2,1)}, u32[]{:S(2)}, u32[]{:S(2)}) collective-permute-start(bf16[4,1,64,2176]{3,2,0,1:T(8,128)(2,1)} %bitcast.219), channel_id=1, source_target_pairs={{0,4},{2,6},{4,0},{6,2},{8,12},{10,14},{12,8},{14,10},{16,20},{18,... | collective-permute-start | bytes 3342344 | tf_op jit(solution)/shard_map/ppermute | solution.py:20
  80.4 399.9 %reduce-scatter.5.cloned.1.call-start = ((), (), s32[]{:S(2)}) async-start(), calls=%async_computation.8 | async-start | bytes 1474560 | tf_op jit(solution)/shard_map/reduce_scatter | solution.py:135
  80.7 49.4 %collective-permute-start.8 = (bf16[4,1,64,2304]{3,2,1,0:T(8,128)(2,1)}, bf16[4,1,64,2304]{3,2,1,0:T(8,128)(2,1)}, u32[]{:S(2)}, u32[]{:S(2)}) collective-permute-start(bf16[4,1,64,2304]{3,2,1,0:T(8,128)(2,1)} %bitcast.215), channel_id=1, source_target_pairs={{0,2},{2,0},{4,6},{6,4},{8,10},{10,8},{12,14},{14,12},{16,18},{18,... | collective-permute-start | bytes 3538952 | tf_op jit(solution)/shard_map/ppermute | solution.py:20
  82.0 48.1 %collective-permute-start.9 = (bf16[4,1,64,2304]{3,2,1,0:T(8,128)(2,1)}, bf16[4,1,64,2304]{3,2,1,0:T(8,128)(2,1)}, u32[]{:S(2)}, u32[]{:S(2)}) collective-permute-start(bf16[4,1,64,2304]{3,2,1,0:T(8,128)(2,1)} %bitcast.216), channel_id=1, source_target_pairs={{0,4},{2,6},{4,0},{6,2},{8,12},{10,14},{12,8},{14,10},{16,20},{18,... | collective-permute-start | bytes 3538952 | tf_op jit(solution)/shard_map/ppermute | solution.py:20
  85.1 34.9 %collective-permute-start.11 = (bf16[2,1,64,2176]{3,2,0,1:T(8,128)(2,1)S(1)}, bf16[2,1,64,2176]{3,2,0,1:T(8,128)(2,1)S(1)}, u32[]{:S(2)}, u32[]{:S(2)}) collective-permute-start(bf16[2,1,64,2176]{3,2,0,1:T(8,128)(2,1)S(1)} %slice.270), channel_id=1, source_target_pairs={{0,4},{2,6},{4,0},{6,2},{8,12},{10,14},{12,8},{14,10},{16,20},{18,... | collective-permute-start | bytes 1671176 | tf_op jit(solution)/shard_map/ppermute | solution.py:20
  86.5 33.5 %collective-permute-start.12 = (bf16[2,1,64,2176]{3,2,0,1:T(8,128)(2,1)S(1)}, bf16[2,1,64,2176]{3,2,0,1:T(8,128)(2,1)S(1)}, u32[]{:S(2)}, u32[]{:S(2)}) collective-permute-start(bf16[2,1,64,2176]{3,2,0,1:T(8,128)(2,1)S(1)} %slice.271), channel_id=1, source_target_pairs={{0,2},{2,0},{4,6},{6,4},{8,10},{10,8},{12,14},{14,12},{16,18},{18,... | collective-permute-start | bytes 1671176 | tf_op jit(solution)/shard_map/ppermute | solution.py:20
  99.8 123.8 %copy-start.12 = (bf16[1536,1024]{1,0:T(8,128)(2,1)}, bf16[1536,1024]{1,0:T(8,128)(2,1)S(1)}, u32[]{:S(2)}) copy-start(bf16[1536,1024]{1,0:T(8,128)(2,1)S(1)} %pad_maximum_fusion.4.right_ref.d_down_ref) | copy-start | bytes 9437188
  99.9 26.9 %copy-start.39 = (bf16[1,768,1024]{2,1,0:T(8,128)(2,1)S(1)}, bf16[1,768,1024]{2,1,0:T(8,128)(2,1)}, u32[]{:S(2)}) copy-start(bf16[1,768,1024]{2,1,0:T(8,128)(2,1)} %param.11) | copy-start | bytes 4718596
  99.9 26.9 %copy-start.53 = (bf16[768,1024]{1,0:T(8,128)(2,1)S(1)}, bf16[768,1024]{1,0:T(8,128)(2,1)}, u32[]{:S(2)}) copy-start(bf16[768,1024]{1,0:T(8,128)(2,1)} %copy-done.52) | copy-start | bytes 4718596
  122.5 38.7 %collective-permute-start.18 = (bf16[16,64,512]{2,1,0:T(8,128)(2,1)}, bf16[16,64,512]{2,1,0:T(8,128)(2,1)}, u32[]{:S(2)}, u32[]{:S(2)}) collective-permute-start(bf16[16,64,512]{2,1,0:T(8,128)(2,1)} %bitcast.35), channel_id=1, source_target_pairs={{0,1},{1,0},{2,3},{3,2},{4,5},{5,4},{6,7},{7,6},{8,9},{9,8},{10,11... | collective-permute-start | bytes 3145736 | tf_op jit(solution)/shard_map/ppermute | solution.py:15
  130.1 42.9 %collective-permute-start.13 = (bf16[4,1,64,2304]{3,2,1,0:T(8,128)(2,1)}, bf16[4,1,64,2304]{3,2,1,0:T(8,128)(2,1)S(1)}, u32[]{:S(2)}, u32[]{:S(2)}) collective-permute-start(bf16[4,1,64,2304]{3,2,1,0:T(8,128)(2,1)} %bitcast.212), channel_id=1, source_target_pairs={{0,2},{2,0},{4,6},{6,4},{8,10},{10,8},{12,14},{14,12},{16,18},{18,... | collective-permute-start | bytes 3538952 | tf_op jit(solution)/shard_map/ppermute | solution.py:20
  130.4 42.6 %collective-permute-start.14 = (bf16[4,1,64,2304]{3,2,1,0:T(8,128)(2,1)}, bf16[4,1,64,2304]{3,2,1,0:T(8,128)(2,1)S(1)}, u32[]{:S(2)}, u32[]{:S(2)}) collective-permute-start(bf16[4,1,64,2304]{3,2,1,0:T(8,128)(2,1)} %bitcast.213), channel_id=1, source_target_pairs={{0,4},{2,6},{4,0},{6,2},{8,12},{10,14},{12,8},{14,10},{16,20},{18,... | collective-permute-start | bytes 3538952 | tf_op jit(solution)/shard_map/ppermute | solution.py:20
  141.3 18.1 %copy-start = (f32[1536,1536]{1,0:T(8,128)}, f32[1536,1536]{1,0:T(8,128)S(1)}, u32[]{:S(2)}) copy-start(f32[1536,1536]{1,0:T(8,128)S(1)} %shard_map.186) | copy-start | bytes 28311556
  141.9 14.2 %collective-permute-start.15 = (bf16[2,2,512]{2,1,0:T(2,128)(2,1)S(1)}, bf16[2,2,512]{2,1,0:T(2,128)(2,1)S(1)}, u32[]{:S(2)}, u32[]{:S(2)}) collective-permute-start(bf16[2,2,512]{2,1,0:T(2,128)(2,1)S(1)} %slice.348), channel_id=1, source_target_pairs={{0,2},{2,4},{4,6},{6,8},{8,10},{10,12},{12,14},{14,16},{16,18},{18... | collective-permute-start | bytes 12296 | tf_op jit(solution)/shard_map/ppermute | solution.py:26
  149.7 20.9 %collective-permute-start.22 = (bf16[2,1,64,2304]{3,2,1,0:T(8,128)(2,1)}, bf16[2,1,64,2304]{3,2,1,0:T(8,128)(2,1)}, u32[]{:S(2)}, u32[]{:S(2)}) collective-permute-start(bf16[2,1,64,2304]{3,2,1,0:T(8,128)(2,1)} %slice.306), channel_id=1, source_target_pairs={{0,4},{2,6},{4,0},{6,2},{8,12},{10,14},{12,8},{14,10},{16,20},{18,... | collective-permute-start | bytes 1769480 | tf_op jit(solution)/shard_map/ppermute | solution.py:20
  156.1 21.7 %collective-permute-start.23 = (bf16[2,1,64,2304]{3,2,1,0:T(8,128)(2,1)S(1)}, bf16[2,1,64,2304]{3,2,1,0:T(8,128)(2,1)S(1)}, u32[]{:S(2)}, u32[]{:S(2)}) collective-permute-start(bf16[2,1,64,2304]{3,2,1,0:T(8,128)(2,1)S(1)} %slice.307), channel_id=1, source_target_pairs={{0,2},{2,0},{4,6},{6,4},{8,10},{10,8},{12,14},{14,12},{16,18},{18,... | collective-permute-start | bytes 1769480 | tf_op jit(solution)/shard_map/ppermute | solution.py:20
  161.2 11.4 %collective-permute-start.17 = (bf16[768,512]{1,0:T(8,128)(2,1)S(1)}, bf16[768,512]{1,0:T(8,128)(2,1)S(1)}, u32[]{:S(2)}, u32[]{:S(2)}) collective-permute-start(bf16[768,512]{1,0:T(8,128)(2,1)S(1)} %slice.352), channel_id=1, source_target_pairs={{0,1},{1,0},{2,3},{3,2},{4,5},{5,4},{6,7},{7,6},{8,9},{9,8},{10,11... | collective-permute-start | bytes 2359304 | tf_op jit(solution)/shard_map/ppermute | solution.py:15
  176.6 17.9 %collective-permute-start.19 = (bf16[768,1024]{1,0:T(8,128)(2,1)S(1)}, bf16[768,1024]{1,0:T(8,128)(2,1)S(1)}, u32[]{:S(2)}, u32[]{:S(2)}) collective-permute-start(bf16[768,1024]{1,0:T(8,128)(2,1)S(1)} %multiply_convert_fusion), channel_id=1, source_target_pairs={{0,1},{1,0},{2,3},{3,2},{4,5},{5,4},{6,7},{7,6},{8,9},{9,8},{10,11... | collective-permute-start | bytes 4718600 | tf_op jit(solution)/shard_map/ppermute | solution.py:15
  178.7 14.6 %collective-permute-start.20 = (bf16[2,1,64,2304]{3,2,1,0:T(8,128)(2,1)S(1)}, bf16[2,1,64,2304]{3,2,1,0:T(8,128)(2,1)S(1)}, u32[]{:S(2)}, u32[]{:S(2)}) collective-permute-start(bf16[2,1,64,2304]{3,2,1,0:T(8,128)(2,1)S(1)} %slice.304), channel_id=1, source_target_pairs={{0,4},{2,6},{4,0},{6,2},{8,12},{10,14},{12,8},{14,10},{16,20},{18,... | collective-permute-start | bytes 1769480 | tf_op jit(solution)/shard_map/ppermute | solution.py:20
  180.1 14.3 %collective-permute-start.21 = (bf16[2,1,64,2304]{3,2,1,0:T(8,128)(2,1)S(1)}, bf16[2,1,64,2304]{3,2,1,0:T(8,128)(2,1)S(1)}, u32[]{:S(2)}, u32[]{:S(2)}) collective-permute-start(bf16[2,1,64,2304]{3,2,1,0:T(8,128)(2,1)S(1)} %slice.305), channel_id=1, source_target_pairs={{0,2},{2,0},{4,6},{6,4},{8,10},{10,8},{12,14},{14,12},{16,18},{18,... | collective-permute-start | bytes 1769480 | tf_op jit(solution)/shard_map/ppermute | solution.py:20
  236.5 23.3 %collective-permute-start.25 = (bf16[2,1,144,1024]{3,2,1,0:T(8,128)(2,1)}, bf16[2,1,144,1024]{3,2,1,0:T(8,128)(2,1)S(1)}, u32[]{:S(2)}, u32[]{:S(2)}) collective-permute-start(bf16[2,1,144,1024]{3,2,1,0:T(8,128)(2,1)} %get-tuple-element.125), channel_id=1, source_target_pairs={{0,2},{2,0},{4,6},{6,4},{8,10},{10,8},{12,14},{14,12},{16,18},{18,... | collective-permute-start | bytes 1769480 | tf_op jit(solution)/shard_map/ppermute | solution.py:20
  237.5 22.3 %collective-permute-start.26 = (bf16[2,1,144,1024]{3,2,1,0:T(8,128)(2,1)}, bf16[2,1,144,1024]{3,2,1,0:T(8,128)(2,1)S(1)}, u32[]{:S(2)}, u32[]{:S(2)}) collective-permute-start(bf16[2,1,144,1024]{3,2,1,0:T(8,128)(2,1)} %get-tuple-element.126), channel_id=1, source_target_pairs={{0,4},{2,6},{4,0},{6,2},{8,12},{10,14},{12,8},{14,10},{16,20},{18,... | collective-permute-start | bytes 1769480 | tf_op jit(solution)/shard_map/ppermute | solution.py:20
  262.2 40.9 %collective-permute-start.27 = (bf16[4,1,144,1024]{3,2,1,0:T(8,128)(2,1)}, bf16[4,1,144,1024]{3,2,1,0:T(8,128)(2,1)S(1)}, u32[]{:S(2)}, u32[]{:S(2)}) collective-permute-start(bf16[4,1,144,1024]{3,2,1,0:T(8,128)(2,1)} %pad_maximum_fusion.10), channel_id=1, source_target_pairs={{0,2},{2,0},{4,6},{6,4},{8,10},{10,8},{12,14},{14,12},{16,18},{18,... | collective-permute-start | bytes 3538952 | tf_op jit(solution)/shard_map/ppermute | solution.py:20
  262.6 40.5 %collective-permute-start.28 = (bf16[4,1,144,1024]{3,2,1,0:T(8,128)(2,1)}, bf16[4,1,144,1024]{3,2,1,0:T(8,128)(2,1)}, u32[]{:S(2)}, u32[]{:S(2)}) collective-permute-start(bf16[4,1,144,1024]{3,2,1,0:T(8,128)(2,1)} %pad_maximum_fusion.11), channel_id=1, source_target_pairs={{0,4},{2,6},{4,0},{6,2},{8,12},{10,14},{12,8},{14,10},{16,20},{18,... | collective-permute-start | bytes 3538952 | tf_op jit(solution)/shard_map/ppermute | solution.py:20
  274.2 45.6 %copy-start.5 = (bf16[1024,2304]{1,0:T(8,128)(2,1)}, bf16[1024,2304]{1,0:T(8,128)(2,1)S(1)}, u32[]{:S(2)}) copy-start(bf16[1024,2304]{1,0:T(8,128)(2,1)S(1)} %shard_map.191) | copy-start | bytes 14155780
  299.1 24.6 %collective-permute-start.33 = (f32[768,1024]{1,0:T(8,128)}, f32[768,1024]{1,0:T(8,128)}, u32[]{:S(2)}, u32[]{:S(2)}) collective-permute-start(f32[768,1024]{1,0:T(8,128)} %copy-done.26), channel_id=1, source_target_pairs={{0,1},{1,0},{2,3},{3,2},{4,5},{5,4},{6,7},{7,6},{8,9},{9,8},{10,11... | collective-permute-start | bytes 9437192 | tf_op jit(solution)/shard_map/ppermute | solution.py:15
  301.8 18.0 %collective-permute-start.29 = (bf16[2,1,64,2304]{3,2,1,0:T(8,128)(2,1)}, bf16[2,1,64,2304]{3,2,1,0:T(8,128)(2,1)S(1)}, u32[]{:S(2)}, u32[]{:S(2)}) collective-permute-start(bf16[2,1,64,2304]{3,2,1,0:T(8,128)(2,1)} %get-tuple-element.147), channel_id=1, source_target_pairs={{0,2},{2,0},{4,6},{6,4},{8,10},{10,8},{12,14},{14,12},{16,18},{18,... | collective-permute-start | bytes 1769480 | tf_op jit(solution)/shard_map/ppermute | solution.py:20
  302.8 16.9 %collective-permute-start.30 = (bf16[2,1,64,2304]{3,2,1,0:T(8,128)(2,1)}, bf16[2,1,64,2304]{3,2,1,0:T(8,128)(2,1)S(1)}, u32[]{:S(2)}, u32[]{:S(2)}) collective-permute-start(bf16[2,1,64,2304]{3,2,1,0:T(8,128)(2,1)} %get-tuple-element.148), channel_id=1, source_target_pairs={{0,4},{2,6},{4,0},{6,2},{8,12},{10,14},{12,8},{14,10},{16,20},{18,... | collective-permute-start | bytes 1769480 | tf_op jit(solution)/shard_map/ppermute | solution.py:20
  335.3 4.6 collective-permute-start.34
  338.1 8.4 %collective-permute-start.35 = (f32[768,512]{1,0:T(8,128)S(1)}, f32[768,512]{1,0:T(8,128)}, u32[]{:S(2)}, u32[]{:S(2)}) collective-permute-start(f32[768,512]{1,0:T(8,128)S(1)} %get-tuple-element.299), channel_id=1, source_target_pairs={{0,1},{1,0},{2,3},{3,2},{4,5},{5,4},{6,7},{7,6},{8,9},{9,8},{10,11... | collective-permute-start | bytes 4718600 | tf_op jit(solution)/shard_map/ppermute | solution.py:15
  338.2 142.1 %reduce-scatter.7.cloned.1.call-start = ((), (), s32[]{:S(2)}) async-start(), calls=%async_computation.9 | async-start | bytes 1474560 | tf_op jit(solution)/shard_map/reduce_scatter | solution.py:135
  338.3 27.4 %collective-permute-start.31 = (bf16[4,1,64,2304]{3,2,1,0:T(8,128)(2,1)}, bf16[4,1,64,2304]{3,2,1,0:T(8,128)(2,1)}, u32[]{:S(2)}, u32[]{:S(2)}) collective-permute-start(bf16[4,1,64,2304]{3,2,1,0:T(8,128)(2,1)} %pad_maximum_fusion.12), channel_id=1, source_target_pairs={{0,2},{2,0},{4,6},{6,4},{8,10},{10,8},{12,14},{14,12},{16,18},{18,... | collective-permute-start | bytes 3538952 | tf_op jit(solution)/shard_map/ppermute | solution.py:20
  338.6 27.1 %collective-permute-start.32 = (bf16[4,1,64,2304]{3,2,1,0:T(8,128)(2,1)}, bf16[4,1,64,2304]{3,2,1,0:T(8,128)(2,1)}, u32[]{:S(2)}, u32[]{:S(2)}) collective-permute-start(bf16[4,1,64,2304]{3,2,1,0:T(8,128)(2,1)} %pad_maximum_fusion.13), channel_id=1, source_target_pairs={{0,4},{2,6},{4,0},{6,2},{8,12},{10,14},{12,8},{14,10},{16,20},{18,... | collective-permute-start | bytes 3538952 | tf_op jit(solution)/shard_map/ppermute | solution.py:20
  365.8 8.3 %collective-permute-start.38 = (f32[2,2,512]{2,1,0:T(2,128)S(1)}, f32[2,2,512]{2,1,0:T(2,128)S(1)}, u32[]{:S(2)}, u32[]{:S(2)}) collective-permute-start(f32[2,2,512]{2,1,0:T(2,128)S(1)} %maximum_multiply_fusion), channel_id=1, source_target_pairs={{2,0},{4,2},{6,4},{8,6},{10,8},{12,10},{14,12},{16,14},{18,16},{20... | collective-permute-start | bytes 24584 | tf_op jit(solution)/shard_map/ppermute | solution.py:26
  370.7 16.6 %collective-permute-start.36 = (bf16[2,1,64,2816]{3,2,1,0:T(8,128)(2,1)S(1)}, bf16[2,1,64,2816]{3,2,1,0:T(8,128)(2,1)S(1)}, u32[]{:S(2)}, u32[]{:S(2)}) collective-permute-start(bf16[2,1,64,2816]{3,2,1,0:T(8,128)(2,1)S(1)} %copy-done.65), channel_id=1, source_target_pairs={{0,2},{2,0},{4,6},{6,4},{8,10},{10,8},{12,14},{14,12},{16,18},{18,... | collective-permute-start | bytes 2162696 | tf_op jit(solution)/shard_map/ppermute | solution.py:20
  372.8 15.5 %collective-permute-start.37 = (bf16[2,1,64,2816]{3,2,1,0:T(8,128)(2,1)S(1)}, bf16[2,1,64,2816]{3,2,1,0:T(8,128)(2,1)S(1)}, u32[]{:S(2)}, u32[]{:S(2)}) collective-permute-start(bf16[2,1,64,2816]{3,2,1,0:T(8,128)(2,1)S(1)} %copy-done.64), channel_id=1, source_target_pairs={{0,4},{2,6},{4,0},{6,2},{8,12},{10,14},{12,8},{14,10},{16,20},{18,... | collective-permute-start | bytes 2162696 | tf_op jit(solution)/shard_map/ppermute | solution.py:20
  400.5 18.5 %collective-permute-start.41 = (f32[768,1024]{1,0:T(8,128)}, f32[768,1024]{1,0:T(8,128)}, u32[]{:S(2)}, u32[]{:S(2)}) collective-permute-start(f32[768,1024]{1,0:T(8,128)} %get-tuple-element.173), channel_id=1, source_target_pairs={{0,1},{1,0},{2,3},{3,2},{4,5},{5,4},{6,7},{7,6},{8,9},{9,8},{10,11... | collective-permute-start | bytes 9437192 | tf_op jit(solution)/shard_map/ppermute | solution.py:15
  404.0 77.8 %reduce-scatter.9.cloned.1.call-start = ((), (), s32[]{:S(2)}) async-start(), calls=%async_computation.10 | async-start | bytes 1802240 | tf_op jit(solution)/shard_map/reduce_scatter | solution.py:135
  407.7 33.6 %collective-permute-start.39 = (bf16[4,1,64,2816]{3,2,1,0:T(8,128)(2,1)}, bf16[4,1,64,2816]{3,2,1,0:T(8,128)(2,1)}, u32[]{:S(2)}, u32[]{:S(2)}) collective-permute-start(bf16[4,1,64,2816]{3,2,1,0:T(8,128)(2,1)} %pad_maximum_fusion.8), channel_id=1, source_target_pairs={{0,2},{2,0},{4,6},{6,4},{8,10},{10,8},{12,14},{14,12},{16,18},{18,... | collective-permute-start | bytes 4325384 | tf_op jit(solution)/shard_map/ppermute | solution.py:20
  408.6 33.2 %collective-permute-start.40 = (bf16[4,1,64,2816]{3,2,1,0:T(8,128)(2,1)}, bf16[4,1,64,2816]{3,2,1,0:T(8,128)(2,1)}, u32[]{:S(2)}, u32[]{:S(2)}) collective-permute-start(bf16[4,1,64,2816]{3,2,1,0:T(8,128)(2,1)} %pad_maximum_fusion.9), channel_id=1, source_target_pairs={{0,4},{2,6},{4,0},{6,2},{8,12},{10,14},{12,8},{14,10},{16,20},{18,... | collective-permute-start | bytes 4325384 | tf_op jit(solution)/shard_map/ppermute | solution.py:20
  425.1 18.6 %slice-start.5 = ((s8[4718592]{0:T(1024)(128)(4,1)}), s8[4194304]{0:T(1024)(128)(4,1)S(1)}, s32[]{:S(2)}) async-start(s8[4718592]{0:T(1024)(128)(4,1)} %bitcast.174), calls=%async_computation.17 | async-start | bytes 8388608
  441.8 10.5 %collective-permute-start.42 = (bf16[2,1,64,1664]{3,2,0,1:T(8,128)(2,1)}, bf16[2,1,64,1664]{3,2,0,1:T(8,128)(2,1)}, u32[]{:S(2)}, u32[]{:S(2)}) collective-permute-start(bf16[2,1,64,1664]{3,2,0,1:T(8,128)(2,1)} %get-tuple-element.183), channel_id=1, source_target_pairs={{0,2},{2,0},{4,6},{6,4},{8,10},{10,8},{12,14},{14,12},{16,18},{18,... | collective-permute-start | bytes 1277960 | tf_op jit(solution)/shard_map/ppermute | solution.py:20
  442.4 10.2 %collective-permute-start.43 = (bf16[2,1,64,1664]{3,2,0,1:T(8,128)(2,1)}, bf16[2,1,64,1664]{3,2,0,1:T(8,128)(2,1)}, u32[]{:S(2)}, u32[]{:S(2)}) collective-permute-start(bf16[2,1,64,1664]{3,2,0,1:T(8,128)(2,1)} %get-tuple-element.184), channel_id=1, source_target_pairs={{0,4},{2,6},{4,0},{6,2},{8,12},{10,14},{12,8},{14,10},{16,20},{18,... | collective-permute-start | bytes 1277960 | tf_op jit(solution)/shard_map/ppermute | solution.py:20
  447.2 59.6 %reduce-scatter.11.cloned.1.call-start = ((), (), s32[]{:S(2)}) async-start(), calls=%async_computation.11 | async-start | bytes 1064960 | tf_op jit(solution)/shard_map/reduce_scatter | solution.py:135
  455.3 10.3 %collective-permute-start.46 = (bf16[768,1024]{1,0:T(8,128)(2,1)S(1)}, bf16[768,1024]{1,0:T(8,128)(2,1)S(1)}, u32[]{:S(2)}, u32[]{:S(2)}) collective-permute-start(bf16[768,1024]{1,0:T(8,128)(2,1)S(1)} %copy-done.28), channel_id=1, source_target_pairs={{0,1},{1,0},{2,3},{3,2},{4,5},{5,4},{6,7},{7,6},{8,9},{9,8},{10,11... | collective-permute-start | bytes 4718600 | tf_op jit(solution)/shard_map/ppermute | solution.py:15
  457.7 20.6 %collective-permute-start.44 = (bf16[4,1,64,1664]{3,2,0,1:T(8,128)(2,1)S(1)}, bf16[4,1,64,1664]{3,2,0,1:T(8,128)(2,1)S(1)}, u32[]{:S(2)}, u32[]{:S(2)}) collective-permute-start(bf16[4,1,64,1664]{3,2,0,1:T(8,128)(2,1)S(1)} %pad_maximum_fusion.15), channel_id=1, source_target_pairs={{0,2},{2,0},{4,6},{6,4},{8,10},{10,8},{12,14},{14,12},{16,18},{18,... | collective-permute-start | bytes 2555912 | tf_op jit(solution)/shard_map/ppermute | solution.py:20
  458.6 20.5 %collective-permute-start.45 = (bf16[4,1,64,1664]{3,2,0,1:T(8,128)(2,1)S(1)}, bf16[4,1,64,1664]{3,2,0,1:T(8,128)(2,1)S(1)}, u32[]{:S(2)}, u32[]{:S(2)}) collective-permute-start(bf16[4,1,64,1664]{3,2,0,1:T(8,128)(2,1)S(1)} %pad_maximum_fusion.16), channel_id=1, source_target_pairs={{0,4},{2,6},{4,0},{6,2},{8,12},{10,14},{12,8},{14,10},{16,20},{18,... | collective-permute-start | bytes 2555912 | tf_op jit(solution)/shard_map/ppermute | solution.py:20
  482.9 5.2 collective-permute-start.48
  485.6 8.5 %collective-permute-start.49 = (bf16[32,2304]{1,0:T(8,128)(2,1)S(1)}, bf16[32,2304]{1,0:T(8,128)(2,1)S(1)}, u32[]{:S(2)}, u32[]{:S(2)}) collective-permute-start(bf16[32,2304]{1,0:T(8,128)(2,1)S(1)} %broadcast_select_fusion.10), channel_id=1, source_target_pairs={{0,1},{1,0},{2,3},{3,2},{4,5},{5,4},{6,7},{7,6},{8,9},{9,8},{10,11... | collective-permute-start | bytes 442376 | tf_op jit(solution)/shard_map/ppermute | solution.py:15
  507.7 4.8 collective-permute-start.47
  (72 other events, 482.3 us)
Sparse Core Ops, SparseCore 0:
  17.7 30.9 all-gather.4
  50.8 29.5 all-gather.6
  82.5 29.5 all-gather.8
  113.6 89.1 all-gather.10
  338.4 27.7 reduce-scatter.4
  404.1 28.9 reduce-scatter.6
  447.3 34.5 reduce-scatter.8
  484.2 22.5 reduce-scatter.10
